TPU v7x, 32 devices: a whole 2x2x4 slice. The times are simulated.
32 devices in a mesh: shard: 4 (over y, x), context: 4 (over z), tensor: 2 (over core).
Axes of the slice: x: 2, y: 2, z: 4, core: 2. Of those that a mesh axis runs over, the one named last changes fastest.
Arguments:
- tokens: bfloat16 [4096, 960], P(('shard', 'context', 'tensor')), may hold values from -6 to 6
- cotangent: bfloat16 [4096, 960], P(('shard', 'context', 'tensor')), may hold values from -6 to 6
- lengths: int32 [4, 2], P('shard'), may hold values from 341 to 683, as said below
- qkv_weight: float32 [960, 1600], P('shard'), may hold values from -0.1875 to 0.1875
- qkv_first: float32 [960, 1600], P('shard'), may hold values from -36.48 to 36.48
- qkv_second: float32 [960, 1600], P('shard'), may hold values from 212.992 to 2498.56
- out_weight: float32 [960, 960], P('shard'), may hold values from -3 to 3
- out_first: float32 [960, 960], P('shard'), may hold values from -1.56 to 1.56
- out_second: float32 [960, 960], P('shard'), may hold values from 1.12 to 4.56
- gate_up_weight: float32 [960, 2, 2560], P('shard', None, 'tensor'), may hold values from -0.1875 to 0.1875
- gate_up_first: float32 [960, 2, 2560], P('shard', None, 'tensor'), may hold values from -7.936 to 7.936
- gate_up_second: float32 [960, 2, 2560], P('shard', None, 'tensor'), may hold values from 29.4912 to 118.784
- down_weight: float32 [2560, 960], P('tensor', 'shard'), may hold values from -0.125 to 0.125
- down_first: float32 [2560, 960], P('tensor', 'shard'), may hold values from -12.864 to 12.864
- down_second: float32 [2560, 960], P('tensor', 'shard'), may hold values from 77.4144 to 310.4768
- norm_gains: float32 [2, 960], P(None, 'shard'), may hold values from 0.5 to 1.5
- gains_first: float32 [2, 960], P(None, 'shard'), may hold values from -36.48 to 36.48
- gains_second: float32 [2, 960], P(None, 'shard'), may hold values from 155.648 to 2498.56
Outputs:
- block_out: bfloat16 [4096, 960], P(('shard', 'context', 'tensor'))
- tokens_grad: float32 [4096, 960], P(('shard', 'context', 'tensor'))
- qkv_new: float32 [960, 1600], P('shard')
- qkv_first_new: float32 [960, 1600], P('shard')
- qkv_second_new: float32 [960, 1600], P('shard')
- out_new: float32 [960, 960], P('shard')
- out_first_new: float32 [960, 960], P('shard')
- out_second_new: float32 [960, 960], P('shard')
- gate_up_new: float32 [960, 2, 2560], P('shard', None, 'tensor')
- gate_up_first_new: float32 [960, 2, 2560], P('shard', None, 'tensor')
- gate_up_second_new: float32 [960, 2, 2560], P('shard', None, 'tensor')
- down_new: float32 [2560, 960], P('tensor', 'shard')
- down_first_new: float32 [2560, 960], P('tensor', 'shard')
- down_second_new: float32 [2560, 960], P('tensor', 'shard')
- gains_new: float32 [2, 960], P(None, 'shard')
- gains_first_new: float32 [2, 960], P(None, 'shard')
- gains_second_new: float32 [2, 960], P(None, 'shard')
Inputs may be any that keep to these rules, and one draw needn't show every extreme that they name: Each row lists the lengths of the 2 documents of one pack in order; they sum to 1024, each is 341 or more, and the largest over all packs is 683.
All inputs are finite; a program needn't handle non-finite values.
Results may differ from a plain program's by a relative error of at most 0.028.
Values may be sent and summed in bfloat16 or wider, within the bound.
A program may use at most 128 MiB of HBM per device.

v0:
```python
import math

import jax
import jax.numpy as jnp
from jax import lax
from jax.sharding import PartitionSpec as P

MODEL_WIDTH = 960
QUERY_HEADS = 15
KEY_VALUE_HEADS = 5
HEAD_SIZE = 64
STEP = 10
KEY_COLUMNS = 320


NEGATIVE_HUGE = -1e30
NORM_EPS = 1e-05
ROPE_BASE = 100000.0
BETA_ONE = 0.9
BETA_TWO = 0.95
ADAM_EPS = 1e-08
RATES = (0.06, 1.0, 0.06, 0.04, 0.4)
DECAYS = (0.1, 0.1, 0.1, 0.1, 0.0)


def rope_angles(position):
    halfway = HEAD_SIZE // 2
    frequency = jnp.exp(
        jnp.arange(halfway, dtype=jnp.float32) * (-2.0 * math.log(ROPE_BASE) / HEAD_SIZE)
    )
    angles = position.astype(jnp.float32)[:, None] * frequency[None, :]
    return (jnp.cos(angles)[:, None, :], jnp.sin(angles)[:, None, :])


def apply_rotary(vectors, cosine_table, sine_table):
    halfway = HEAD_SIZE // 2
    leading = vectors[..., :halfway]
    trailing = vectors[..., halfway:]
    return jnp.concatenate(
        [
            leading * cosine_table - trailing * sine_table,
            trailing * cosine_table + leading * sine_table,
        ],
        axis=-1,
    )


def unrotate(gradient, cosine_table, sine_table):
    halfway = HEAD_SIZE // 2
    leading = gradient[..., :halfway]
    trailing = gradient[..., halfway:]
    return jnp.concatenate(
        [
            leading * cosine_table + trailing * sine_table,
            trailing * cosine_table - leading * sine_table,
        ],
        axis=-1,
    )


def doc_starts(length_row, row_index):
    doc_ends = jnp.cumsum(length_row)
    before = jnp.where(doc_ends[None, :] <= row_index[:, None], length_row[None, :], 0)
    return jnp.sum(before, axis=1)


def rms_norm(values, gain_row):
    inverse = lax.rsqrt(jnp.mean(values * values, axis=-1, keepdims=True) + NORM_EPS)
    return (values * inverse * gain_row, inverse)


def norm_back(values, inverse, gain_row, gradient):
    unit_values = values * inverse
    scaled = gradient * gain_row
    gain_grad = jnp.sum(gradient * unit_values, axis=0)
    values_grad = inverse * (
        scaled - unit_values * jnp.mean(scaled * unit_values, axis=-1, keepdims=True)
    )
    return (gain_grad, values_grad)


def adam_step(weight, moment_one, moment_two, gradient, learning, decay_rate):
    first_new = BETA_ONE * moment_one + (1.0 - BETA_ONE) * gradient
    second_new = BETA_TWO * moment_two + (1.0 - BETA_TWO) * gradient * gradient
    first_hat = first_new / (1.0 - BETA_ONE**STEP)
    second_hat = second_new / (1.0 - BETA_TWO**STEP)
    weight_new = weight - learning * (
        first_hat / (jnp.sqrt(second_hat) + ADAM_EPS) + decay_rate * weight
    )
    return (weight_new, first_new, second_new)


def block_scores(query_low, key_block, row_index, row_start, block_id):
    rows_per_block = key_block.shape[0]
    scores = jnp.einsum(
        "qhgd,khd->qhgk", query_low, key_block, preferred_element_type=jnp.float32
    ) * (1.0 / math.sqrt(HEAD_SIZE))
    column_index = block_id * rows_per_block + jnp.arange(rows_per_block, dtype=jnp.int32)
    visible = (column_index[None, :] >= row_start[:, None]) & (
        column_index[None, :] <= row_index[:, None]
    )
    return (scores, visible[:, None, None, :])


def shards(
    tokens,
    cotangent,
    lengths,
    qkv_weight,
    qkv_first,
    qkv_second,
    out_weight,
    out_first,
    out_second,
    gate_up_weight,
    gate_up_first,
    gate_up_second,
    down_weight,
    down_first,
    down_second,
    norm_gains,
    gains_first,
    gains_second,
):
    shard_rows = tokens.shape[0]
    pack_groups = QUERY_HEADS // KEY_VALUE_HEADS
    qkv_low = qkv_weight.astype(jnp.bfloat16)
    out_low = out_weight.astype(jnp.bfloat16)
    gate_up_low = gate_up_weight.astype(jnp.bfloat16)
    down_low = down_weight.astype(jnp.bfloat16)
    gains_low = norm_gains.astype(jnp.bfloat16)
    qkv_mat, out_mat, gate_up_mat, down_mat, gains_all = (
        lax.all_gather(qkv_low, "shard", axis=0, tiled=True),
        lax.all_gather(out_low, "shard", axis=0, tiled=True),
        lax.all_gather(gate_up_low, "shard", axis=0, tiled=True),
        lax.all_gather(down_low, "shard", axis=1, tiled=True),
        lax.all_gather(gains_low, "shard", axis=1, tiled=True),
    )
    gains_full = gains_all.astype(jnp.float32)
    tensor_size = lax.axis_size("tensor")
    offset = (lax.axis_index("context") * tensor_size + lax.axis_index("tensor")) * shard_rows
    row_index = offset + jnp.arange(shard_rows, dtype=jnp.int32)
    row_start = doc_starts(lengths[0], row_index)
    cosine_table, sine_table = rope_angles(row_index - row_start)
    inputs = tokens.astype(jnp.float32)
    normed_one, inverse_one = rms_norm(inputs, gains_full[0])
    first_low = normed_one.astype(jnp.bfloat16)
    projected_output = jnp.dot(first_low, qkv_mat, preferred_element_type=jnp.float32)
    query_low = (
        apply_rotary(
            projected_output[:, :MODEL_WIDTH].reshape(shard_rows, QUERY_HEADS, HEAD_SIZE),
            cosine_table,
            sine_table,
        )
        .astype(jnp.bfloat16)
        .reshape(shard_rows, KEY_VALUE_HEADS, pack_groups, HEAD_SIZE)
    )
    keys_low = (
        apply_rotary(
            projected_output[:, MODEL_WIDTH : MODEL_WIDTH + KEY_COLUMNS].reshape(
                shard_rows, KEY_VALUE_HEADS, HEAD_SIZE
            ),
            cosine_table,
            sine_table,
        )
        .astype(jnp.bfloat16)
        .reshape(shard_rows, KEY_COLUMNS)
    )
    kv_local = jnp.concatenate(
        [keys_low, projected_output[:, MODEL_WIDTH + KEY_COLUMNS :].astype(jnp.bfloat16)], axis=1
    )
    key_value_whole = lax.all_gather(kv_local, ("context", "tensor"), axis=0, tiled=True)
    total_keys = key_value_whole.shape[0]
    rows_per_block = min(512, total_keys)
    count_of_blocks = total_keys // rows_per_block
    key_value_blocks = key_value_whole.reshape(
        count_of_blocks, rows_per_block, 2, KEY_VALUE_HEADS, HEAD_SIZE
    )
    block_numbers = jnp.arange(count_of_blocks, dtype=jnp.int32)

    def scan_total(scan_carry, scan_item):
        running, running_sum = scan_carry
        block_id, kv_block = scan_item
        scores, visible = block_scores(query_low, kv_block[:, 0], row_index, row_start, block_id)
        masked = jnp.where(visible, scores, NEGATIVE_HUGE)
        highest = jnp.maximum(running, jnp.max(masked, axis=-1))
        exponent = jnp.where(visible, jnp.exp(masked - highest[..., None]), 0.0)
        running_sum = running_sum * jnp.exp(running - highest) + jnp.sum(exponent, axis=-1)
        return ((highest, running_sum), None)

    latest_start = jnp.full((shard_rows, KEY_VALUE_HEADS, pack_groups), NEGATIVE_HUGE, jnp.float32)
    (running, running_sum), unused = lax.scan(
        scan_total, (latest_start, jnp.zeros_like(latest_start)), (block_numbers, key_value_blocks)
    )
    log_total = running + jnp.log(running_sum)

    def sweep_output(accumulated, scan_item):
        block_id, kv_block = scan_item
        scores, visible = block_scores(query_low, kv_block[:, 0], row_index, row_start, block_id)
        softmax_rows = jnp.where(visible, jnp.exp(scores - log_total[..., None]), 0.0)
        accumulated = accumulated + jnp.einsum(
            "qhgk,khd->qhgd",
            softmax_rows.astype(jnp.bfloat16),
            kv_block[:, 1],
            preferred_element_type=jnp.float32,
        )
        return (accumulated, None)

    attended_heads, unused = lax.scan(
        sweep_output,
        jnp.zeros((shard_rows, KEY_VALUE_HEADS, pack_groups, HEAD_SIZE), jnp.float32),
        (block_numbers, key_value_blocks),
    )
    attended_low = attended_heads.reshape(shard_rows, MODEL_WIDTH).astype(jnp.bfloat16)
    branch = jnp.dot(attended_low, out_mat, preferred_element_type=jnp.float32)
    hidden_state = inputs + branch
    normed_two, inverse_two = rms_norm(hidden_state, gains_full[1])
    second_low = normed_two.astype(jnp.bfloat16)
    ffn_rows = lax.all_gather(second_low, "tensor", axis=0, tiled=True)
    gate_up = jnp.einsum("td,dcf->tcf", ffn_rows, gate_up_mat, preferred_element_type=jnp.float32)
    gate_vals = gate_up[:, 0]
    upward = gate_up[:, 1]
    gate_sigmoid = jax.nn.sigmoid(gate_vals)
    activated = gate_vals * gate_sigmoid
    hidden_low = (activated * upward).astype(jnp.bfloat16)
    partial_out = jnp.dot(hidden_low, down_mat, preferred_element_type=jnp.float32)
    ffn_out = lax.psum_scatter(
        partial_out.astype(jnp.bfloat16), "tensor", scatter_dimension=0, tiled=True
    ).astype(jnp.float32)
    block_out = (hidden_state + ffn_out).astype(jnp.bfloat16)
    qkv_mat, out_mat, gate_up_mat, down_mat, gains_all = (
        lax.all_gather(qkv_low, "shard", axis=0, tiled=True),
        lax.all_gather(out_low, "shard", axis=0, tiled=True),
        lax.all_gather(gate_up_low, "shard", axis=0, tiled=True),
        lax.all_gather(down_low, "shard", axis=1, tiled=True),
        lax.all_gather(gains_low, "shard", axis=1, tiled=True),
    )
    gains_full = gains_all.astype(jnp.float32)
    grad_rows = lax.all_gather(cotangent, "tensor", axis=0, tiled=True)
    down_grad = jnp.einsum("tf,td->fd", hidden_low, grad_rows, preferred_element_type=jnp.float32)
    hidden_grad = jnp.einsum("td,fd->tf", grad_rows, down_mat, preferred_element_type=jnp.float32)
    gate_grad = hidden_grad * upward * gate_sigmoid * (1.0 + gate_vals * (1.0 - gate_sigmoid))
    upward_grad = hidden_grad * activated
    gate_up_grad_low = jnp.stack([gate_grad, upward_grad], axis=1).astype(jnp.bfloat16)
    gate_up_grad = jnp.einsum(
        "td,tcf->dcf", ffn_rows, gate_up_grad_low, preferred_element_type=jnp.float32
    )
    normed_part = jnp.einsum(
        "tcf,dcf->td", gate_up_grad_low, gate_up_mat, preferred_element_type=jnp.float32
    )
    normed_two_grad = lax.psum_scatter(
        normed_part.astype(jnp.bfloat16), "tensor", scatter_dimension=0, tiled=True
    ).astype(jnp.float32)
    gain_two_grad, state_norm_grad = norm_back(
        hidden_state, inverse_two, gains_full[1], normed_two_grad
    )
    state_grad = cotangent.astype(jnp.float32) + state_norm_grad
    branch_low = state_grad.astype(jnp.bfloat16)
    out_grad = jnp.einsum("tk,td->kd", attended_low, branch_low, preferred_element_type=jnp.float32)
    attended_gradient = jnp.einsum(
        "td,kd->tk", branch_low, out_mat, preferred_element_type=jnp.float32
    )
    attended_gradient_narrow = attended_gradient.astype(jnp.bfloat16).reshape(
        shard_rows, KEY_VALUE_HEADS, pack_groups, HEAD_SIZE
    )
    delta_rows = jnp.sum(attended_gradient_narrow.astype(jnp.float32) * attended_heads, axis=-1)

    def sweep_backward(query_grad, scan_item):
        block_id, kv_block = scan_item
        scores, visible = block_scores(query_low, kv_block[:, 0], row_index, row_start, block_id)
        softmax_rows = jnp.where(visible, jnp.exp(scores - log_total[..., None]), 0.0)
        softmax_low = softmax_rows.astype(jnp.bfloat16)
        probs_grad = jnp.einsum(
            "qhgd,khd->qhgk",
            attended_gradient_narrow,
            kv_block[:, 1],
            preferred_element_type=jnp.float32,
        )
        scores_low = (softmax_rows * (probs_grad - delta_rows[..., None])).astype(jnp.bfloat16)
        query_grad = query_grad + jnp.einsum(
            "qhgk,khd->qhgd", scores_low, kv_block[:, 0], preferred_element_type=jnp.float32
        ) * (1.0 / math.sqrt(HEAD_SIZE))
        key_grad = jnp.einsum(
            "qhgk,qhgd->khd", scores_low, query_low, preferred_element_type=jnp.float32
        ) * (1.0 / math.sqrt(HEAD_SIZE))
        value_grad = jnp.einsum(
            "qhgk,qhgd->khd",
            softmax_low,
            attended_gradient_narrow,
            preferred_element_type=jnp.float32,
        )
        return (query_grad, jnp.stack([key_grad, value_grad], axis=1))

    query_grad, kv_terms = lax.scan(
        sweep_backward,
        jnp.zeros((shard_rows, KEY_VALUE_HEADS, pack_groups, HEAD_SIZE), jnp.float32),
        (block_numbers, key_value_blocks),
    )
    kv_terms = kv_terms.reshape(total_keys, 2 * KEY_COLUMNS)
    key_value_gradient = lax.psum_scatter(
        kv_terms.astype(jnp.bfloat16), ("context", "tensor"), scatter_dimension=0, tiled=True
    ).astype(jnp.float32)
    key_back = unrotate(
        key_value_gradient[:, :KEY_COLUMNS].reshape(shard_rows, KEY_VALUE_HEADS, HEAD_SIZE),
        cosine_table,
        sine_table,
    ).reshape(shard_rows, KEY_COLUMNS)
    query_back = unrotate(
        query_grad.reshape(shard_rows, QUERY_HEADS, HEAD_SIZE), cosine_table, sine_table
    ).reshape(shard_rows, MODEL_WIDTH)
    projected_low = jnp.concatenate(
        [query_back, key_back, key_value_gradient[:, KEY_COLUMNS:]], axis=1
    ).astype(jnp.bfloat16)
    qkv_grad = jnp.einsum("td,tk->dk", first_low, projected_low, preferred_element_type=jnp.float32)
    normed_one_grad = jnp.einsum(
        "tk,dk->td", projected_low, qkv_mat, preferred_element_type=jnp.float32
    )
    gain_one_grad, input_norm_grad = norm_back(inputs, inverse_one, gains_full[0], normed_one_grad)
    tokens_grad = state_grad + input_norm_grad
    gains_grad = jnp.stack([gain_one_grad, gain_two_grad])
    qkv_part, out_part, gate_up_part, down_part, gains_part = (
        lax.psum_scatter(
            qkv_grad.astype(jnp.bfloat16), "shard", scatter_dimension=0, tiled=True
        ).astype(jnp.float32),
        lax.psum_scatter(
            out_grad.astype(jnp.bfloat16), "shard", scatter_dimension=0, tiled=True
        ).astype(jnp.float32),
        lax.psum_scatter(
            gate_up_grad.astype(jnp.bfloat16), "shard", scatter_dimension=0, tiled=True
        ).astype(jnp.float32),
        lax.psum_scatter(
            down_grad.astype(jnp.bfloat16), "shard", scatter_dimension=1, tiled=True
        ).astype(jnp.float32),
        lax.psum_scatter(
            gains_grad.astype(jnp.bfloat16), "shard", scatter_dimension=1, tiled=True
        ).astype(jnp.float32),
    )
    qkv_red, out_red, gains_red = (
        lax.psum(qkv_part.astype(jnp.bfloat16), ("context", "tensor")).astype(jnp.float32),
        lax.psum(out_part.astype(jnp.bfloat16), ("context", "tensor")).astype(jnp.float32),
        lax.psum(gains_part.astype(jnp.bfloat16), ("context", "tensor")).astype(jnp.float32),
    )
    gate_up_red, down_red = (
        lax.psum(gate_up_part.astype(jnp.bfloat16), "context").astype(jnp.float32),
        lax.psum(down_part.astype(jnp.bfloat16), "context").astype(jnp.float32),
    )
    results = adam_step(qkv_weight, qkv_first, qkv_second, qkv_red, RATES[0], DECAYS[0])
    results = results + adam_step(out_weight, out_first, out_second, out_red, RATES[1], DECAYS[1])
    results = results + adam_step(
        gate_up_weight, gate_up_first, gate_up_second, gate_up_red, RATES[2], DECAYS[2]
    )
    results = results + adam_step(
        down_weight, down_first, down_second, down_red, RATES[3], DECAYS[3]
    )
    results = results + adam_step(
        norm_gains, gains_first, gains_second, gains_red, RATES[4], DECAYS[4]
    )
    return (block_out, tokens_grad) + results


def solution(mesh):
    placed = (
        P(("shard", "context", "tensor"), None),
        P(("shard", "context", "tensor"), None),
        P("shard", None),
        P("shard", None),
        P("shard", None),
        P("shard", None),
        P("shard", None),
        P("shard", None),
        P("shard", None),
        P("shard", None, "tensor"),
        P("shard", None, "tensor"),
        P("shard", None, "tensor"),
        P("tensor", "shard"),
        P("tensor", "shard"),
        P("tensor", "shard"),
        P(None, "shard"),
        P(None, "shard"),
        P(None, "shard"),
    )
    return jax.shard_map(
        shards,
        mesh=mesh,
        in_specs=placed,
        out_specs=(
            P(("shard", "context", "tensor"), None),
            P(("shard", "context", "tensor"), None),
            P("shard", None),
            P("shard", None),
            P("shard", None),
            P("shard", None),
            P("shard", None),
            P("shard", None),
            P("shard", None, "tensor"),
            P("shard", None, "tensor"),
            P("shard", None, "tensor"),
            P("tensor", "shard"),
            P("tensor", "shard"),
            P("tensor", "shard"),
            P(None, "shard"),
            P(None, "shard"),
            P(None, "shard"),
        ),
        check_vma=False,
    )
```

profile of v0, /device:TPU:0, one launch (start us, length us, event | category | flops | bytes accessed | tf_op | source)
XLA Modules:
  0.0 680.1 jit_solution(17888606527032099341)
XLA Ops:
  7.3 2.5 convert_element_type.139
  9.8 9.5 %all-gather = bf16[4,240,2]{1,2,0:T(2,128)(2,1)S(1)} all-gather(bf16[1,240,2]{1,2,0:T(2,128)(2,1)S(1)} %convert_bitcast_fusion), channel_id=1, replica_groups=mesh['shard'=4,'context'=4,'tensor'=2] {'shard'}, dimensions={0}, use_global_device_ids=true | all-gather | bytes 4800 | tf_op jit(solution)/shard_map/all_gather | solution.py:137
  21.2 36.4 %all-gather.7.cloned.1.call-done = bf16[960,1600]{1,0:T(8,128)(2,1)} async-done(((bf16[240,1600]{1,0:T(8,128)(2,1)}), bf16[960,1600]{1,0:T(8,128)(2,1)}) %all-gather.7.cloned.1.call-update) | async-done | bytes 3072016 | tf_op jit(solution)/shard_map/all_gather | solution.py:133
  57.6 3.5 fusion.72
  62.8 2.1 convert_element_type.144
  65.0 1.2 copy.149
  66.2 1.2 copy-done.14
  68.4 2.2 all_gather.36
  70.7 18.1 %all-gather.9.cloned.1.call-done = bf16[1024,640]{0,1:T(8,128)(2,1)} async-done(((bf16[128,640]{0,1:T(8,128)(2,1)}), bf16[1024,640]{0,1:T(8,128)(2,1)}) %all-gather.9.cloned.1.call-update) | async-done | bytes 1310736 | tf_op jit(solution)/shard_map/all_gather | solution.py:172
  88.8 4.4 reshape.351
  93.2 1.6 copy.107
  94.8 15.8 %while.37 = (s32[]{:T(128)}, f32[128,5,3]{0,2,1:T(4,128)S(1)}, f32[128,5,3]{0,2,1:T(4,128)S(1)}, s32[2]{0:T(128)S(1)}, s32[128]{0:T(128)}, /*index=5*/bf16[2,512...) while((s32[]{:T(128)}, f32[128,5,3]{0,2,1:T(4,128)S(1)}, ...), condition=%wide.region_6.7_spmd.clone, body=%wide.region_3.6_spmd.clone.sunk | while | flops 133900288 | bytes 10050724 | solution.py:192
  96.9 2.7 fusion.134
  99.6 3.0 select_reduce_fusion.2
  104.7 2.7 fusion.134
  107.5 3.0 select_reduce_fusion.2
  111.2 9.8 %while.38 = (s32[]{:T(128)}, f32[128,5,3,64]{0,3,2,1:T(8,128)}, bf16[2,512,2,5,64]{1,4,3,2,0:T(8,128)(2,1)S(1)}, s32[2]{0:T(128)S(1)}, s32[128]{0:T(128)}, /*ind...) while((s32[]{:T(128)}, f32[128,5,3,64]{0,3,2,1:T(8,128)}, ...), condition=%wide.region_8.9_spmd.clone, body=%wide.region_7.8_spmd.clone.sunk | while | flops 256033408 | bytes 3339427 | solution.py:209
  113.2 2.7 fusion.137
  117.9 3.0 fusion.137
  122.0 2.0 all-gather.11.cloned.1.call-done
  124.0 2.4 multiply_reduce_fusion.1
  126.7 2.4 all_gather.33
  129.1 55.9 %all-gather.13.cloned.1.call-done = bf16[960,2,1280]{2,0,1:T(8,128)(2,1)} async-done(((bf16[240,2,1280]{2,0,1:T(8,128)(2,1)}), bf16[960,2,1280]{2,0,1:T(8,128)(2,1)}) %all-gather.13.cloned.1.call-update) | async-done | bytes 4915216 | tf_op jit(solution)/shard_map/all_gather | solution.py:135
  185.0 5.4 fusion.66
  190.5 35.1 %all-gather.15.cloned.1.call-done = bf16[1280,960]{0,1:T(8,128)(2,1)} async-done(((bf16[1280,240]{0,1:T(8,128)(2,1)}), bf16[1280,960]{0,1:T(8,128)(2,1)}) %all-gather.15.cloned.1.call-update) | async-done | bytes 2457616 | tf_op jit(solution)/shard_map/all_gather | solution.py:136
  225.6 4.7 fusion.51
  231.2 1.5 fusion.41
  233.8 2.7 convolution_convert_fusion.4
  237.6 4.2 reduce-scatter.25.cloned.1.call-done
  241.8 1.1 copy.132
  243.9 10.0 %reduce-scatter.23.cloned.1.call-done = bf16[128,960]{1,0:T(8,128)(2,1)} async-done(((bf16[256,960]{1,0:T(8,128)(2,1)}), bf16[128,960]{1,0:T(8,128)(2,1)}) %reduce-scatter.23.cloned.1.call-update) | async-done | bytes 245776
  253.9 1.1 copy.130
  258.5 27.8 %while.39 = (s32[]{:T(128)}, f32[128,5,3,64]{0,3,2,1:T(8,128)}, bf16[2,512,2,5,64]{1,4,3,2,0:T(8,128)(2,1)}, bf16[2,512,2,5,64]{1,4,3,2,0:T(8,128)(2,1)S(1)}, s3...) while((s32[]{:T(128)}, f32[128,5,3,64]{0,3,2,1:T(8,128)}, ...), condition=%wide.region_15.16_spmd.clone, body=%wide.region_14.15_spmd.clone.sunk | while | flops 641180288 | bytes 55505848 | solution.py:294
  259.4 1.6 dynamic_slice.40
  262.5 2.1 fusion.146
  264.7 2.3 fusion.147
  266.9 3.0 fusion.148
  273.2 1.6 dynamic_slice.40
  276.3 2.1 fusion.146
  278.5 2.4 fusion.147
  280.9 3.0 fusion.148
  286.3 2.7 copy.110
  289.4 1.4 copy.133
  290.9 2.0 convolution_convert_fusion.3
  293.1 32.5 %reduce-scatter.27.cloned.1.call-done = bf16[128,640]{1,0:T(8,128)(2,1)} async-done(((bf16[1024,640]{1,0:T(8,128)(2,1)}), bf16[128,640]{1,0:T(8,128)(2,1)}) %reduce-scatter.27.cloned.1.call-update) | async-done | bytes 163856
  327.0 2.8 convolution_convert_fusion.1
  331.0 2.2 convolution_convert_fusion.2
  334.8 3.7 convolution_convert_fusion
  338.5 22.8 %reduce-scatter.17.cloned.1.call-done = bf16[240,960]{1,0:T(8,128)(2,1)} async-done(((bf16[960,960]{1,0:T(8,128)(2,1)}), bf16[240,960]{1,0:T(8,128)(2,1)}) %reduce-scatter.17.cloned.1.call-update) | async-done | bytes 460816 | tf_op jit(solution)/shard_map/reduce_scatter | solution.py:325
  361.4 47.6 %reduce-scatter.29.cloned.1.call-done = bf16[240,1600]{1,0:T(8,128)(2,1)} async-done(((bf16[960,1600]{1,0:T(8,128)(2,1)}), bf16[240,1600]{1,0:T(8,128)(2,1)}) %reduce-scatter.29.cloned.1.call-update) | async-done | bytes 768016
  410.3 3.0 fusion.63
  413.4 9.2 %all-reduce.1 = bf16[2,960]{1,0:T(2,128)(2,1)S(1)} all-reduce(bf16[2,960]{1,0:T(2,128)(2,1)S(1)} %pad_maximum_fusion.11), channel_id=9, replica_groups=mesh['shard'=4,'context'=4,'tensor'=2] {'shard'}, use_global_device_ids=true, to_apply=%region_28.29.clone | all-reduce | flops 1920 | bytes 7680
  422.7 22.9 %psum.39 = bf16[2,240]{1,0:T(2,128)(2,1)S(1)} all-reduce(bf16[2,240]{1,0:T(2,128)(2,1)S(1)} %constant_dynamic-slice_fusion), channel_id=1, replica_groups=mesh['shard'=4,'context'=4,'tensor'=2] {'context','tensor'}, use_global_device_ids=true, to_apply=%region_29.30 | all-reduce | flops 480 | bytes 1920 | tf_op jit(solution)/shard_map/psum | solution.py:341
  445.6 5.6 reduce-scatter.21.cloned.1.call-done
  451.1 61.9 %reduce-scatter.19.cloned.1.call-done = bf16[240,2,1280]{2,0,1:T(8,128)(2,1)} async-done(((bf16[960,2,1280]{2,0,1:T(8,128)(2,1)}), bf16[240,2,1280]{2,0,1:T(8,128)(2,1)}) %reduce-scatter.19.cloned.1.call-update) | async-done | bytes 1228816 | tf_op jit(solution)/shard_map/reduce_scatter | solution.py:328
  514.7 60.8 %all-reduce.7.cloned.1.call-done = (bf16[240,1600]{1,0:T(8,128)(2,1)}, bf16[240,960]{1,0:T(8,128)(2,1)}) async-done(((bf16[240,1600]{1,0:T(8,128)(2,1)}, bf16[240,960]{1,0:T(8,128)(2,1)}), (bf16[240,1600]{1,0:T(8,128)(2,1)}, bf16[240,960]{1,0:T(8,128)(2,1)})) %all-reduce.7.cloned.1.call-update) | async-done | bytes 1228816 | tf_op jit(solution)/shard_map/psum | solution.py:339
  575.6 3.6 add_subtract_fusion
  579.2 3.1 multiply_subtract_fusion.1
  582.4 73.8 %all-reduce.9.cloned.1.call-done = (bf16[240,2,1280]{2,0,1:T(8,128)(2,1)}, bf16[1280,240]{0,1:T(8,128)(2,1)}) async-done(((bf16[240,2,1280]{2,0,1:T(8,128)(2,1)}, bf16[1280,240]{0,1:T(8,128)(2,1)}), (bf16[240,2,1280]{2,0,1:T(8,128)(2,1)}, bf16[1280,240]{0,1:T(8,128)(2,1)})) %all-reduce.9.cloned.1.call-update) | async-done | bytes 1843216 | tf_op jit(solution)/shard_map/psum | solution.py:344
  656.1 4.7 multiply_subtract_fusion
  660.8 3.3 copy.115
  664.2 3.3 copy.116
  667.5 3.3 copy.117
  670.9 2.5 multiply_subtract_fusion.2
  (253 shorter events, 34.8 us)
Async XLA Ops:
  7.2 2.6 copy-start.47
  7.2 12.2 %copy-start.53 = (s32[1,2]{1,0:T(1,128)S(1)}, s32[1,2]{1,0:T(1,128)}, u32[]{:S(2)}) copy-start(s32[1,2]{1,0:T(1,128)} %param.26) | copy-start | bytes 28
  7.2 13.0 %copy-start.6 = (bf16[128,960]{0,1:T(8,128)(2,1)S(1)}, bf16[128,960]{0,1:T(8,128)(2,1)}, u32[]{:S(2)}) copy-start(bf16[128,960]{0,1:T(8,128)(2,1)} %param.24) | copy-start | bytes 737284
  7.2 50.4 %all-gather.7.cloned.1.call-start = ((), (), s32[]{:S(2)}) async-start(), calls=%async_computation.7 | async-start | bytes 3993600 | tf_op jit(solution)/shard_map/all_gather | solution.py:133
  9.7 79.1 %all-gather.9.cloned.1.call-start = ((), (), s32[]{:S(2)}) async-start(), calls=%async_computation.8 | async-start | bytes 1474560 | tf_op jit(solution)/shard_map/all_gather | solution.py:172
  20.4 40.7 %copy-start.49 = (f32[128]{0:T(128)}, f32[128]{0:T(128)S(1)}, u32[]{:S(2)}) copy-start(f32[128]{0:T(128)S(1)} %add_rsqrt_fusion.1) | copy-start | bytes 1540
  21.0 36.6 %copy-start.43 = (f32[1,960]{1,0:T(1,128)}, f32[1,960]{1,0:T(1,128)S(1)}, u32[]{:S(2)}) copy-start(f32[1,960]{1,0:T(1,128)S(1)} %get-tuple-element.579) | copy-start | bytes 11524
  61.1 3.8 copy-start.4
  62.8 61.3 %all-gather.11.cloned.1.call-start = ((), (), s32[]{:S(2)}) async-start(), calls=%async_computation.9 | async-start | bytes 2457600 | tf_op jit(solution)/shard_map/all_gather | solution.py:134
  64.9 120.1 %all-gather.13.cloned.1.call-start = ((), (), s32[]{:S(2)}) async-start(), calls=%async_computation.10 | async-start | bytes 6144000 | tf_op jit(solution)/shard_map/all_gather | solution.py:135
  66.1 2.3 copy-start.32
  66.2 4.4 slice-start
  66.2 159.5 %all-gather.15.cloned.1.call-start = ((), (), s32[]{:S(2)}) async-start(), calls=%async_computation.11 | async-start | bytes 3072000 | tf_op jit(solution)/shard_map/all_gather | solution.py:136
  68.3 173.5 %reduce-scatter.25.cloned.1.call-start = ((), (), s32[]{:S(2)}) async-start(), calls=%async_computation.16 | async-start | bytes 786432
  70.6 155.1 %copy-start.16 = (bf16[256,960]{0,1:T(8,128)(2,1)}, bf16[256,960]{0,1:T(8,128)(2,1)S(1)}, u32[]{:S(2)}) copy-start(bf16[256,960]{0,1:T(8,128)(2,1)S(1)} %all_gather.36) | copy-start | bytes 1474564
  122.0 4.5 copy-start.20
  129.1 61.4 %copy-start.12 = (bf16[256,960]{0,1:T(8,128)(2,1)}, bf16[256,960]{0,1:T(8,128)(2,1)S(1)}, u32[]{:S(2)}) copy-start(bf16[256,960]{0,1:T(8,128)(2,1)S(1)} %all_gather.33) | copy-start | bytes 1474564
  225.6 5.6 copy-start.3
  230.4 2.3 copy-start.37
  233.7 20.2 %reduce-scatter.23.cloned.1.call-start = ((), (), s32[]{:S(2)}) async-start(), calls=%async_computation.15 | async-start | bytes 786432
  237.5 88.0 %reduce-scatter.27.cloned.1.call-start = ((), (), s32[]{:S(2)}) async-start(), calls=%async_computation.17 | async-start | bytes 1474560
  255.0 1.6 copy-start.8
  255.0 2.3 copy-start.22
  258.6 3.8 copy-start.1
  258.6 3.8 copy-start.34
  258.6 3.8 copy-start.45
  259.4 5.2 copy-start
  262.5 2.2 copy-start.23
  264.6 2.3 copy-start.24
  264.6 2.3 copy-start.35
  272.4 3.8 copy-start.1
  272.4 3.8 copy-start.34
  272.5 3.8 copy-start.45
  273.2 5.2 copy-start
  276.3 2.2 copy-start.23
  278.5 2.5 copy-start.24
  278.5 2.5 copy-start.35
  290.8 2.1 copy-start.2
  290.8 70.5 %reduce-scatter.17.cloned.1.call-start = ((), (), s32[]{:S(2)}) async-start(), calls=%async_computation.12 | async-start | bytes 2457600 | tf_op jit(solution)/shard_map/reduce_scatter | solution.py:325
  292.9 34.1 %copy-start.7 = (bf16[128,960]{0,1:T(8,128)(2,1)S(1)}, bf16[128,960]{0,1:T(8,128)(2,1)}, u32[]{:S(2)}) copy-start(bf16[128,960]{0,1:T(8,128)(2,1)} %param.24) | copy-start | bytes 737284
  292.9 34.1 %copy-start.44 = (f32[1,960]{1,0:T(1,128)S(1)}, f32[1,960]{1,0:T(1,128)}, u32[]{:S(2)}) copy-start(f32[1,960]{1,0:T(1,128)} %copy-done.43) | copy-start | bytes 11524
  292.9 34.1 %copy-start.50 = (f32[128]{0:T(128)S(1)}, f32[128]{0:T(128)}, u32[]{:S(2)}) copy-start(f32[128]{0:T(128)} %copy-done.49) | copy-start | bytes 1540
  292.9 116.1 %reduce-scatter.29.cloned.1.call-start = ((), (), s32[]{:S(2)}) async-start(), calls=%async_computation.18 | async-start | bytes 3993600
  329.8 121.4 %reduce-scatter.21.cloned.1.call-start = ((), (), s32[]{:S(2)}) async-start(), calls=%async_computation.14 | async-start | bytes 3072000 | tf_op jit(solution)/shard_map/reduce_scatter | solution.py:331
  333.2 1.6 copy-start.40
  333.3 179.8 %reduce-scatter.19.cloned.1.call-start = ((), (), s32[]{:S(2)}) async-start(), calls=%async_computation.13 | async-start | bytes 6144000 | tf_op jit(solution)/shard_map/reduce_scatter | solution.py:328
  338.5 70.6 %copy-start.54 = (u32[32]{0:T(128)S(1)}, u32[32]{0:T(128)}, u32[]{:S(2)}) copy-start(u32[32]{0:T(128)} %constant.84) | copy-start | bytes 388
  338.5 71.8 %copy-start.46 = (bf16[960]{0:T(1024)(128)(2,1)S(1)}, bf16[960]{0:T(1024)(128)(2,1)}, u32[]{:S(2)}) copy-start(bf16[960]{0:T(1024)(128)(2,1)} %get-tuple-element.486) | copy-start | bytes 5764
  338.5 237.1 %all-reduce.7.cloned.1.call-start = ((), (), s32[]{:S(2)}) async-start(), calls=%async_computation.19 | async-start | bytes 2580480 | tf_op jit(solution)/shard_map/psum | solution.py:339
  409.0 247.1 %all-reduce.9.cloned.1.call-start = ((), (), s32[]{:S(2)}) async-start(), calls=%async_computation.20 | async-start | bytes 3686400 | tf_op jit(solution)/shard_map/psum | solution.py:344
  410.3 102.8 %copy-start.48 = (f32[2,240]{1,0:T(2,128)S(1)}, f32[2,240]{1,0:T(2,128)}, u32[]{:S(2)}) copy-start(f32[2,240]{1,0:T(2,128)} %param.39) | copy-start | bytes 5764
  410.3 102.8 %copy-start.51 = (f32[2,240]{1,0:T(2,128)S(1)}, f32[2,240]{1,0:T(2,128)}, u32[]{:S(2)}) copy-start(f32[2,240]{1,0:T(2,128)} %param.40) | copy-start | bytes 5764
  410.3 102.8 %copy-start.52 = (f32[2,240]{1,0:T(2,128)S(1)}, f32[2,240]{1,0:T(2,128)}, u32[]{:S(2)}) copy-start(f32[2,240]{1,0:T(2,128)} %param.41) | copy-start | bytes 5764
  413.4 162.2 %copy-start.18 = (f32[240,960]{1,0:T(8,128)S(1)}, f32[240,960]{1,0:T(8,128)}, u32[]{:S(2)}) copy-start(f32[240,960]{1,0:T(8,128)} %param.30) | copy-start | bytes 2764804
  413.4 162.2 %copy-start.31 = (f32[240,960]{1,0:T(8,128)S(1)}, f32[240,960]{1,0:T(8,128)}, u32[]{:S(2)}) copy-start(f32[240,960]{1,0:T(8,128)} %param.31) | copy-start | bytes 2764804
  575.6 3.6 copy-start.11
  575.6 3.6 copy-start.25
  575.6 3.6 copy-start.26
  575.6 3.6 copy-start.36
  579.2 76.9 %copy-start.5 = (f32[240,2,1280]{2,1,0:T(2,128)S(1)}, f32[240,2,1280]{2,1,0:T(2,128)}, u32[]{:S(2)}) copy-start(f32[240,2,1280]{2,1,0:T(2,128)} %param.33) | copy-start | bytes 7372804
  667.5 3.3 copy-start.15
  667.5 3.3 copy-start.29
  667.5 3.3 copy-start.30
  667.5 3.3 copy-start.42
  (15 other events, 18.2 us)
Sparse Core Ops, SparseCore 0:
  10.5 47.0 all-gather.6
  62.9 25.8 all-gather.8
  91.2 32.7 all-gather.10
  126.3 58.6 all-gather.12
  187.3 38.2 all-gather.14
  233.8 7.9 reduce-scatter.24
  244.7 9.1 reduce-scatter.22
  291.0 34.5 reduce-scatter.26
  329.2 32.1 reduce-scatter.16
  364.2 44.6 reduce-scatter.28
  412.9 38.1 reduce-scatter.20
  454.3 58.7 reduce-scatter.18
  515.6 59.8 all-reduce.6
  578.0 78.0 all-reduce.8
where the time goes:
time: 688 us; the launch traced here: 680 us
  waiting for transfers between devices  467 us (68%)
  matrix products  63.6 us (9%)
  blocking collectives  46.2 us (7%)
  local copies, waits for them, and re-layouts  44.1 us (6%)
  other arithmetic  38.8 us (6%)
  between operations  15.5 us (2%)
    unnamed x18, waiting for transfers between devices  94.4 us
    psum x1, waiting for transfers between devices, shards(): lax.psum(gate_up_part.astype(jnp.bfloat16), 'context').astype(jnp.float32)  73.8 us
    reduce_scatter x1, waiting for transfers between devices, shards(): lax.psum_scatter(gate_up_grad.astype(jnp.bfloat16), 'shard', scatter_dime...  61.9 us
    psum x1, waiting for transfers between devices, shards(): lax.psum(qkv_part.astype(jnp.bfloat16), ('context', 'tensor'))  60.8 us
    all_gather x1, waiting for transfers between devices, shards(): lax.all_gather(gate_up_low, 'shard', axis=0, tiled=True)  55.9 us
    all_gather x1, waiting for transfers between devices, shards(): lax.all_gather(qkv_low, 'shard', axis=0, tiled=True)  36.4 us
    all_gather x1, waiting for transfers between devices, shards(): lax.all_gather(down_low, 'shard', axis=1, tiled=True)  35.1 us
    unnamed x107, local copies, waits for them, and re-layouts  26.1 us
  transfers between devices with their start and end apart: 14, of which 14 were waited for; matrix products, arithmetic and copies ran while one was open for 11% of the time, Pallas kernels for 0%

commit v1 on v0

--- a/solution.py
+++ b/solution.py
@@ -1,8 +1,11 @@
+import functools
 import math
 
 import jax
 import jax.numpy as jnp
 from jax import lax
+from jax.experimental import pallas as pl
+from jax.experimental.pallas import tpu as pltpu
 from jax.sharding import PartitionSpec as P
 
 MODEL_WIDTH = 960
@@ -21,6 +24,316 @@
 ADAM_EPS = 1e-08
 RATES = (0.06, 1.0, 0.06, 0.04, 0.4)
 DECAYS = (0.1, 0.1, 0.1, 0.1, 0.0)
+
+
+MESH = pl.DeviceIdType.MESH
+BF16 = jnp.bfloat16
+GAIN_ROWS = 16
+ROW_CHUNKS = 3
+
+
+def plane_peers():
+    s = lax.axis_index("shard")
+    c = lax.axis_index("context")
+    t = lax.axis_index("tensor")
+    x, y = lax.rem(s, 2), s // 2
+    across, along, diagonal = 2 * y + 1 - x, 2 * (1 - y) + x, 2 * (1 - y) + 1 - x
+    return s, c, t, across, along, diagonal
+
+
+def greet(devices):
+    barrier = pltpu.get_barrier_semaphore()
+    for device in devices:
+        pl.semaphore_signal(barrier, inc=1, device_id=device, device_id_type=MESH)
+    pl.semaphore_wait(barrier, len(devices))
+
+
+def gather_kernel(w, gains, out, gains_out, send, recv, local):
+    s, c, t, across, along, diagonal = plane_peers()
+    to_x, to_y, to_d, to_core = (across, c, t), (along, c, t), (diagonal, c, t), (s, c, 1 - t)
+    greet((to_x, to_y, to_d, to_core))
+
+    def block(k):
+        return t if k == 0 else k + 1
+
+    def copy(src, dst, lane, k, device):
+        return pltpu.make_async_remote_copy(
+            src_ref=src,
+            dst_ref=dst,
+            send_sem=send.at[lane, k],
+            recv_sem=recv.at[lane, k],
+            device_id=device,
+            device_id_type=MESH,
+        )
+
+    def own(lane, k):
+        return copy(w.at[block(k)], out.at[block(k), s], lane, k, (to_x, to_y)[lane])
+
+    def onward(k):
+        if k < 2:
+            place = out.at[block(k), across]
+            return copy(place, place, 2, k, to_y)
+        place = out.at[block(k), along]
+        return copy(place, place, 2, k, to_x)
+
+    def sideways(i):
+        place = out.at[t, (across, along, diagonal)[i]]
+        return copy(place, place, 3, i, to_core)
+
+    def small(i):
+        return copy(gains, gains_out.at[s], 4, i, (to_x, to_y, to_d)[i])
+
+    keep = pltpu.make_async_copy(w, out.at[:, s], local.at[0])
+    keep_gains = pltpu.make_async_copy(gains, gains_out.at[s], local.at[1])
+    for i in range(3):
+        small(i).start()
+    for k in range(4):
+        own(0, k).start()
+        own(1, (k + 2) % 4).start()
+    keep.start()
+    keep_gains.start()
+    for k in range(2):
+        own(0, k).wait_recv()
+        onward(k).start()
+        if k == 0:
+            sideways(0).start()
+        own(1, k + 2).wait_recv()
+        onward(k + 2).start()
+    own(1, 0).wait_recv()
+    sideways(1).start()
+    own(1, 1).wait_recv()
+    own(0, 2).wait_recv()
+    own(0, 3).wait_recv()
+    onward(0).wait_recv()
+    sideways(2).start()
+    for k in range(1, 4):
+        onward(k).wait_recv()
+    for i in range(3):
+        sideways(i).wait_recv()
+        small(i).wait_recv()
+    for k in range(4):
+        own(0, k).wait_send()
+        own(1, k).wait_send()
+        onward(k).wait_send()
+    for i in range(3):
+        sideways(i).wait_send()
+        small(i).wait_send()
+    keep.wait()
+    keep_gains.wait()
+
+
+def gather_weights(w, gains):
+    blocks, rows, cols = w.shape
+    return pl.pallas_call(
+        gather_kernel,
+        out_shape=(
+            jax.ShapeDtypeStruct((blocks, 4, rows, cols), BF16),
+            jax.ShapeDtypeStruct((4,) + gains.shape, BF16),
+        ),
+        in_specs=[pl.BlockSpec(memory_space=pl.ANY)] * 2,
+        out_specs=[pl.BlockSpec(memory_space=pl.ANY)] * 2,
+        scratch_shapes=[
+            pltpu.SemaphoreType.DMA((5, 4)),
+            pltpu.SemaphoreType.DMA((5, 4)),
+            pltpu.SemaphoreType.DMA((2,)),
+        ],
+        compiler_params=pltpu.CompilerParams(collective_id=0, has_side_effects=True),
+        name="gather_weights",
+    )(w, gains)
+
+
+def reduce_kernel(
+    n, chunks, attn, ffn, attn_out, ffn_out, side, first, partial, direct, summed, line, middle, carry, send, recv
+):
+    s, c, t, across, along, diagonal = plane_peers()
+    half = n // 2
+    low = c < half
+    inner = jnp.where(low, c + 1, c - 1)
+    outer = jnp.where(low, c - 1, c + 1)
+    to_x, to_y, to_core = (across, c, t), (along, c, t), (s, c, 1 - t)
+    at_end = (c == 0) | (c == n - 1)
+    at_middle = (c == half - 1) | (c == half)
+    barrier = pltpu.get_barrier_semaphore()
+    for device in (to_x, to_y, to_core, (s, inner, t)):
+        pl.semaphore_signal(barrier, inc=1, device_id=device, device_id_type=MESH)
+
+    @pl.when(jnp.logical_not(at_end))
+    def _():
+        pl.semaphore_signal(barrier, inc=1, device_id=(s, outer, t), device_id_type=MESH)
+        pl.semaphore_wait(barrier, 5)
+
+    @pl.when(at_end)
+    def _():
+        pl.semaphore_wait(barrier, 4)
+
+    def copy(src, dst, lane, i, device):
+        return pltpu.make_async_remote_copy(
+            src_ref=src,
+            dst_ref=dst,
+            send_sem=send.at[lane, i],
+            recv_sem=recv.at[lane, i],
+            device_id=device,
+            device_id_type=MESH,
+        )
+
+    def rows_of(i, buffer):
+        return buffer.at[i, pl.ds(0, chunks[i][2])]
+
+    def mine(i, owner):
+        k, start, size = chunks[i]
+        if k == 0:
+            return side.at[owner, pl.ds(start, size)]
+        return ffn.at[k - 1, owner, pl.ds(start, size)]
+
+    def result(i):
+        k, start, size = chunks[i]
+        if k == 0:
+            return attn_out.at[t, pl.ds(start, size)]
+        return ffn_out.at[k - 1, pl.ds(start, size)]
+
+    def x_first(i):
+        return chunks[i][0] < 2
+
+    def add(*refs):
+        total = refs[0][...].astype(jnp.float32)
+        for ref in refs[1:]:
+            total = total + ref[...].astype(jnp.float32)
+        return total.astype(BF16)
+
+    def send_first(i):
+        return copy(mine(i, diagonal), rows_of(i, first), 0, i, to_x if x_first(i) else to_y)
+
+    def send_direct(i):
+        owner, device = (across, to_x) if x_first(i) else (along, to_y)
+        return copy(mine(i, owner), rows_of(i, direct), 1, i, device)
+
+    def send_summed(i):
+        return copy(rows_of(i, partial), rows_of(i, summed), 2, i, to_y if x_first(i) else to_x)
+
+    def send_in(i):
+        return copy(rows_of(i, carry), rows_of(i, line), 3, i, (s, inner, t))
+
+    def send_middle(i):
+        return copy(rows_of(i, carry), rows_of(i, middle), 4, i, (s, inner, t))
+
+    def send_out(i):
+        return copy(result(i), result(i), 5, i, (s, outer, t))
+
+    def send_core(i):
+        return copy(result(i), result(i), 6, i, to_core)
+
+    def send_side():
+        return copy(attn.at[1 - t], side, 7, 0, to_core)
+
+    count = len(chunks)
+    send_side().start()
+    for i in range(count):
+        if chunks[i][0] != 0:
+            send_first(i).start()
+            send_direct(i).start()
+
+    send_side().wait()
+    for owner in range(4):
+        side[owner] = add(attn.at[t, owner], side.at[owner])
+    for i in range(count):
+        if chunks[i][0] == 0:
+            send_first(i).start()
+            send_direct(i).start()
+
+    def stage_plane(i):
+        send_first(i).wait_recv()
+        owner = along if x_first(i) else across
+        partial[i, pl.ds(0, chunks[i][2])] = add(mine(i, owner), rows_of(i, first))
+        send_summed(i).start()
+
+    def stage_in(i):
+        send_direct(i).wait_recv()
+        send_summed(i).wait_recv()
+        carry[i, pl.ds(0, chunks[i][2])] = add(mine(i, s), rows_of(i, direct), rows_of(i, summed))
+
+        @pl.when(at_end)
+        def _():
+            send_in(i).start()
+
+    def stage_fold(i):
+        @pl.when(jnp.logical_not(at_end))
+        def _():
+            send_in(i).wait_recv()
+            carry[i, pl.ds(0, chunks[i][2])] = add(rows_of(i, carry), rows_of(i, line))
+
+            @pl.when(at_middle)
+            def _():
+                send_middle(i).start()
+
+            @pl.when(jnp.logical_not(at_middle))
+            def _():
+                send_in(i).start()
+
+    def stage_total(i):
+        @pl.when(at_middle)
+        def _():
+            send_middle(i).wait()
+            result(i)[...] = add(rows_of(i, carry), rows_of(i, middle))
+
+        @pl.when(jnp.logical_not(at_middle))
+        def _():
+            send_out(i).wait_recv()
+            send_in(i).wait_send()
+
+        @pl.when(jnp.logical_not(at_end))
+        def _():
+            send_out(i).start()
+
+        if chunks[i][0] == 0:
+            send_core(i).start()
+
+    stages = (stage_plane, stage_in, stage_fold, stage_total)
+    for step in range(count + len(stages) - 1):
+        for depth, stage in enumerate(stages):
+            if 0 <= step - depth < count:
+                stage(step - depth)
+    for i in range(count):
+        send_first(i).wait_send()
+        send_direct(i).wait_send()
+        send_summed(i).wait_send()
+
+        @pl.when(jnp.logical_not(at_end))
+        def _():
+            send_out(i).wait_send()
+
+        if chunks[i][0] == 0:
+            send_core(i).wait()
+
+
+def reduce_grads(n, attn, ffn):
+    attn_rows, ffn_rows, cols = attn.shape[2], ffn.shape[2], attn.shape[3]
+    chunks = []
+    step = ffn_rows // ROW_CHUNKS
+    tail = attn_rows - step * (ROW_CHUNKS - 1)
+    for k in (1, 2, 3, 0):
+        for j in range(ROW_CHUNKS):
+            chunks.append((k, j * step, tail if k == 0 and j == ROW_CHUNKS - 1 else step))
+    order = [i for pair in zip(range(ROW_CHUNKS), range(ROW_CHUNKS, 2 * ROW_CHUNKS)) for i in pair]
+    order = order + list(range(2 * ROW_CHUNKS, 4 * ROW_CHUNKS))
+    chunks = [chunks[i] for i in order]
+    count, most = len(chunks), max(step, tail)
+    held = pltpu.VMEM((count, most, cols), BF16)
+    return pl.pallas_call(
+        functools.partial(reduce_kernel, n, tuple(chunks)),
+        out_shape=(
+            jax.ShapeDtypeStruct((2, attn_rows, cols), BF16),
+            jax.ShapeDtypeStruct((3, ffn_rows, cols), BF16),
+        ),
+        in_specs=[pl.BlockSpec(memory_space=pltpu.VMEM)] * 2,
+        out_specs=[pl.BlockSpec(memory_space=pltpu.VMEM)] * 2,
+        scratch_shapes=[pltpu.VMEM((4, attn_rows, cols), BF16)]
+        + [held] * 7
+        + [pltpu.SemaphoreType.DMA((8, count)), pltpu.SemaphoreType.DMA((8, count))],
+        compiler_params=pltpu.CompilerParams(
+            collective_id=1, has_side_effects=True, vmem_limit_bytes=56 * 1024 * 1024
+        ),
+        name="reduce_grads",
+    )(attn, ffn)
 
 
 def rope_angles(position):
@@ -129,13 +442,33 @@
     gate_up_low = gate_up_weight.astype(jnp.bfloat16)
     down_low = down_weight.astype(jnp.bfloat16)
     gains_low = norm_gains.astype(jnp.bfloat16)
-    qkv_mat, out_mat, gate_up_mat, down_mat, gains_all = (
-        lax.all_gather(qkv_low, "shard", axis=0, tiled=True),
-        lax.all_gather(out_low, "shard", axis=0, tiled=True),
-        lax.all_gather(gate_up_low, "shard", axis=0, tiled=True),
-        lax.all_gather(down_low, "shard", axis=1, tiled=True),
-        lax.all_gather(gains_low, "shard", axis=1, tiled=True),
-    )
+    plane = lax.axis_size("shard") == 4 and lax.axis_size("context") % 2 == 0
+    width, hidden_units = MODEL_WIDTH + KEY_COLUMNS, down_weight.shape[0]
+    plane = plane and hidden_units == width
+    if plane:
+        weights = jnp.stack(
+            [
+                qkv_low[:, :width],
+                jnp.concatenate([qkv_low[:, width:], out_low], axis=1),
+                gate_up_low[:, 0],
+                gate_up_low[:, 1],
+                down_low.T,
+            ]
+        )
+        own_gains = jnp.pad(gains_low, ((0, GAIN_ROWS - 2), (0, 0)))
+        gathered, gains_parts = gather_weights(weights, own_gains)
+        gathered = gathered.reshape(5, MODEL_WIDTH, width)
+        qkv_mat = jnp.concatenate([gathered[0], gathered[1, :, :KEY_COLUMNS]], axis=1)
+        out_mat = gathered[1, :, KEY_COLUMNS:]
+        gate_mat, up_mat, down_mat_t = gathered[2], gathered[3], gathered[4]
+        gains_all = gains_parts[:, :2].transpose(1, 0, 2).reshape(2, MODEL_WIDTH)
+    else:
+        qkv_mat = lax.all_gather(qkv_low, "shard", axis=0, tiled=True)
+        out_mat = lax.all_gather(out_low, "shard", axis=0, tiled=True)
+        gate_up_mat = lax.all_gather(gate_up_low, "shard", axis=0, tiled=True)
+        gate_mat, up_mat = gate_up_mat[:, 0], gate_up_mat[:, 1]
+        down_mat_t = lax.all_gather(down_low, "shard", axis=1, tiled=True).T
+        gains_all = lax.all_gather(gains_low, "shard", axis=1, tiled=True)
     gains_full = gains_all.astype(jnp.float32)
     tensor_size = lax.axis_size("tensor")
     offset = (lax.axis_index("context") * tensor_size + lax.axis_index("tensor")) * shard_rows
@@ -217,37 +550,30 @@
     normed_two, inverse_two = rms_norm(hidden_state, gains_full[1])
     second_low = normed_two.astype(jnp.bfloat16)
     ffn_rows = lax.all_gather(second_low, "tensor", axis=0, tiled=True)
-    gate_up = jnp.einsum("td,dcf->tcf", ffn_rows, gate_up_mat, preferred_element_type=jnp.float32)
-    gate_vals = gate_up[:, 0]
-    upward = gate_up[:, 1]
+    gate_vals = jnp.dot(ffn_rows, gate_mat, preferred_element_type=jnp.float32)
+    upward = jnp.dot(ffn_rows, up_mat, preferred_element_type=jnp.float32)
     gate_sigmoid = jax.nn.sigmoid(gate_vals)
     activated = gate_vals * gate_sigmoid
     hidden_low = (activated * upward).astype(jnp.bfloat16)
-    partial_out = jnp.dot(hidden_low, down_mat, preferred_element_type=jnp.float32)
+    partial_out = jnp.einsum("tf,df->td", hidden_low, down_mat_t, preferred_element_type=jnp.float32)
     ffn_out = lax.psum_scatter(
         partial_out.astype(jnp.bfloat16), "tensor", scatter_dimension=0, tiled=True
     ).astype(jnp.float32)
     block_out = (hidden_state + ffn_out).astype(jnp.bfloat16)
-    qkv_mat, out_mat, gate_up_mat, down_mat, gains_all = (
-        lax.all_gather(qkv_low, "shard", axis=0, tiled=True),
-        lax.all_gather(out_low, "shard", axis=0, tiled=True),
-        lax.all_gather(gate_up_low, "shard", axis=0, tiled=True),
-        lax.all_gather(down_low, "shard", axis=1, tiled=True),
-        lax.all_gather(gains_low, "shard", axis=1, tiled=True),
-    )
-    gains_full = gains_all.astype(jnp.float32)
     grad_rows = lax.all_gather(cotangent, "tensor", axis=0, tiled=True)
-    down_grad = jnp.einsum("tf,td->fd", hidden_low, grad_rows, preferred_element_type=jnp.float32)
-    hidden_grad = jnp.einsum("td,fd->tf", grad_rows, down_mat, preferred_element_type=jnp.float32)
+    down_grad_t = jnp.einsum("td,tf->df", grad_rows, hidden_low, preferred_element_type=jnp.float32)
+    hidden_grad = jnp.dot(grad_rows, down_mat_t, preferred_element_type=jnp.float32)
     gate_grad = hidden_grad * upward * gate_sigmoid * (1.0 + gate_vals * (1.0 - gate_sigmoid))
     upward_grad = hidden_grad * activated
-    gate_up_grad_low = jnp.stack([gate_grad, upward_grad], axis=1).astype(jnp.bfloat16)
-    gate_up_grad = jnp.einsum(
-        "td,tcf->dcf", ffn_rows, gate_up_grad_low, preferred_element_type=jnp.float32
+    gate_grad_low = gate_grad.astype(jnp.bfloat16)
+    upward_grad_low = upward_grad.astype(jnp.bfloat16)
+    gate_grad = jnp.einsum("td,tf->df", ffn_rows, gate_grad_low, preferred_element_type=jnp.float32)
+    upward_grad = jnp.einsum(
+        "td,tf->df", ffn_rows, upward_grad_low, preferred_element_type=jnp.float32
     )
     normed_part = jnp.einsum(
-        "tcf,dcf->td", gate_up_grad_low, gate_up_mat, preferred_element_type=jnp.float32
-    )
+        "tf,df->td", gate_grad_low, gate_mat, preferred_element_type=jnp.float32
+    ) + jnp.einsum("tf,df->td", upward_grad_low, up_mat, preferred_element_type=jnp.float32)
     normed_two_grad = lax.psum_scatter(
         normed_part.astype(jnp.bfloat16), "tensor", scatter_dimension=0, tiled=True
     ).astype(jnp.float32)
@@ -318,32 +644,60 @@
     gain_one_grad, input_norm_grad = norm_back(inputs, inverse_one, gains_full[0], normed_one_grad)
     tokens_grad = state_grad + input_norm_grad
     gains_grad = jnp.stack([gain_one_grad, gain_two_grad])
-    qkv_part, out_part, gate_up_part, down_part, gains_part = (
-        lax.psum_scatter(
-            qkv_grad.astype(jnp.bfloat16), "shard", scatter_dimension=0, tiled=True
-        ).astype(jnp.float32),
-        lax.psum_scatter(
-            out_grad.astype(jnp.bfloat16), "shard", scatter_dimension=0, tiled=True
-        ).astype(jnp.float32),
-        lax.psum_scatter(
-            gate_up_grad.astype(jnp.bfloat16), "shard", scatter_dimension=0, tiled=True
-        ).astype(jnp.float32),
-        lax.psum_scatter(
-            down_grad.astype(jnp.bfloat16), "shard", scatter_dimension=1, tiled=True
-        ).astype(jnp.float32),
-        lax.psum_scatter(
-            gains_grad.astype(jnp.bfloat16), "shard", scatter_dimension=1, tiled=True
-        ).astype(jnp.float32),
-    )
-    qkv_red, out_red, gains_red = (
-        lax.psum(qkv_part.astype(jnp.bfloat16), ("context", "tensor")).astype(jnp.float32),
-        lax.psum(out_part.astype(jnp.bfloat16), ("context", "tensor")).astype(jnp.float32),
-        lax.psum(gains_part.astype(jnp.bfloat16), ("context", "tensor")).astype(jnp.float32),
-    )
-    gate_up_red, down_red = (
-        lax.psum(gate_up_part.astype(jnp.bfloat16), "context").astype(jnp.float32),
-        lax.psum(down_part.astype(jnp.bfloat16), "context").astype(jnp.float32),
-    )
+    if plane:
+        rows = MODEL_WIDTH // 4
+        attn_grad = jnp.stack(
+            [
+                qkv_grad[:, :width].astype(jnp.bfloat16),
+                jnp.concatenate([qkv_grad[:, width:], out_grad], axis=1).astype(jnp.bfloat16),
+            ]
+        ).reshape(2, 4, rows, width)
+        gain_rows = jnp.pad(
+            gains_grad.astype(jnp.bfloat16).reshape(2, 4, rows).transpose(1, 0, 2),
+            ((0, 0), (0, GAIN_ROWS - 2), (0, width - rows)),
+        )
+        gain_rows = jnp.stack([gain_rows, jnp.zeros_like(gain_rows)])
+        attn_grad = jnp.concatenate([attn_grad, gain_rows], axis=2)
+        ffn_grad = jnp.stack(
+            [part.astype(jnp.bfloat16) for part in (gate_grad, upward_grad, down_grad_t)]
+        ).reshape(3, 4, rows, width)
+        attn_red, ffn_red = reduce_grads(lax.axis_size("context"), attn_grad, ffn_grad)
+        gains_red = attn_red[0, rows : rows + 2, :rows].astype(jnp.float32)
+        qkv_red = jnp.concatenate(
+            [attn_red[0, :rows], attn_red[1, :rows, :KEY_COLUMNS]], axis=1
+        ).astype(jnp.float32)
+        out_red = attn_red[1, :rows, KEY_COLUMNS:].astype(jnp.float32)
+        gate_up_red = jnp.stack([ffn_red[0], ffn_red[1]], axis=1).astype(jnp.float32)
+        down_red = ffn_red[2].T.astype(jnp.float32)
+    else:
+        gate_up_grad = jnp.stack([gate_grad, upward_grad], axis=1)
+        down_grad = down_grad_t.T
+        qkv_part, out_part, gate_up_part, down_part, gains_part = (
+            lax.psum_scatter(
+                qkv_grad.astype(jnp.bfloat16), "shard", scatter_dimension=0, tiled=True
+            ).astype(jnp.float32),
+            lax.psum_scatter(
+                out_grad.astype(jnp.bfloat16), "shard", scatter_dimension=0, tiled=True
+            ).astype(jnp.float32),
+            lax.psum_scatter(
+                gate_up_grad.astype(jnp.bfloat16), "shard", scatter_dimension=0, tiled=True
+            ).astype(jnp.float32),
+            lax.psum_scatter(
+                down_grad.astype(jnp.bfloat16), "shard", scatter_dimension=1, tiled=True
+            ).astype(jnp.float32),
+            lax.psum_scatter(
+                gains_grad.astype(jnp.bfloat16), "shard", scatter_dimension=1, tiled=True
+            ).astype(jnp.float32),
+        )
+        qkv_red, out_red, gains_red = (
+            lax.psum(qkv_part.astype(jnp.bfloat16), ("context", "tensor")).astype(jnp.float32),
+            lax.psum(out_part.astype(jnp.bfloat16), ("context", "tensor")).astype(jnp.float32),
+            lax.psum(gains_part.astype(jnp.bfloat16), ("context", "tensor")).astype(jnp.float32),
+        )
+        gate_up_red, down_red = (
+            lax.psum(gate_up_part.astype(jnp.bfloat16), "context").astype(jnp.float32),
+            lax.psum(down_part.astype(jnp.bfloat16), "context").astype(jnp.float32),
+        )
     results = adam_step(qkv_weight, qkv_first, qkv_second, qkv_red, RATES[0], DECAYS[0])
     results = results + adam_step(out_weight, out_first, out_second, out_red, RATES[1], DECAYS[1])
     results = results + adam_step(

time: 688 us -> 510 us (0.74)
  waiting for transfers between devices: 467 us -> 57 us
  Pallas kernels: 0 us -> 254 us
  blocking collectives: 46.2 us -> 4.66 us
  local copies, waits for them, and re-layouts: 44.1 us -> 62 us
  other arithmetic: 38.8 us -> 46.8 us
  matrix products: 63.6 us -> 56.7 us
    pallas_call x0 -> x2, Pallas kernels: none -> 254 us  [the longest x1 156 us: reduce_grads(): pl.pallas_call(functools.partial(reduce_kernel, n, tuple(chunks)), out_sh...]
    psum x2 -> x0, waiting for transfers between devices: 135 us -> none  [the longest x1 73.8 us: shards(): lax.psum(gate_up_part.astype(jnp.bfloat16), 'context').astype(jnp.float32)]
    all_gather x4 -> x0, waiting for transfers between devices: 129 us -> none  [the longest x1 55.9 us: shards(): lax.all_gather(gate_up_low, 'shard', axis=0, tiled=True)]
    reduce_scatter x3 -> x0, waiting for transfers between devices: 90.3 us -> none  [the longest x1 61.9 us: shards(): lax.psum_scatter(gate_up_grad.astype(jnp.bfloat16), 'shard', scatter_dime...]
    unnamed x18 -> x7, waiting for transfers between devices: 94.4 us -> 35.1 us
    psum x1 -> x0, blocking collectives: 22.9 us -> none  [shards(): lax.psum(gains_part.astype(jnp.bfloat16), ('context', 'tensor'))]
    all_gather x1 -> x0, blocking collectives: 9.52 us -> none  [shards(): lax.all_gather(gains_low, 'shard', axis=1, tiled=True)]
    unnamed x1 -> x0, blocking collectives: 9.17 us -> none
  transfers between devices with their start and end apart: 14 -> 4, of which waited for: 14 -> 4; matrix products, arithmetic and copies ran while one was open for 11% -> 4% of each run, Pallas kernels for 0% -> 0%
where the time goes in v1:
time: 510 us; the launch traced here: 501 us
  Pallas kernels  254 us (50%)
  local copies, waits for them, and re-layouts  62 us (12%)
  waiting for transfers between devices  57 us (11%)
  matrix products  56.7 us (11%)
  other arithmetic  46.8 us (9%)
  between operations  14.9 us (3%)
    pallas_call x1, Pallas kernels, reduce_grads(): pl.pallas_call(functools.partial(reduce_kernel, n, tuple(chunks)), out_sh...  156 us
    pallas_call x1, Pallas kernels, gather_weights(): pl.pallas_call(gather_kernel, out_shape=(jax.ShapeDtypeStruct((blocks, 4,...  98.7 us
    unnamed x7, waiting for transfers between devices  35.1 us
    unnamed x128, local copies, waits for them, and re-layouts  28.2 us
    all_gather x1, waiting for transfers between devices, shards(): lax.all_gather(kv_local, ('context', 'tensor'), axis=0, tiled=True)  21.9 us
    sub x5, other arithmetic, adam_step(): weight - learning * (first_hat / (jnp.sqrt(second_hat) + ADAM_EPS) + deca...  13.7 us
  transfers between devices with their start and end apart: 4, of which 4 were waited for; matrix products, arithmetic and copies ran while one was open for 4% of the time, Pallas kernels for 0%

profile of v1, /device:TPU:0, one launch (start us, length us, event | category | flops | bytes accessed | tf_op | source)
XLA Modules:
  0.0 501.4 jit_solution(1138493813947585483)
XLA Ops:
  7.3 1.7 convert_element_type.162
  11.2 1.6 copy-done.12
  13.4 98.7 %gather_weights.1 = (bf16[5,4,240,1280]{3,2,1,0:T(8,128)(2,1)}, bf16[4,16,240]{2,1,0:T(8,128)(2,1)}) custom-call(bf16[5,240,1280]{2,1,0:T(8,128)(2,1)} %copy-done.12, bf16[16,240]{1,0:T(8,128)(2,1)} %pad.9.gains), custom_call_target="tpu_custom_call" | custom-call | tf_op jit(solution)/shard_map/gather_weights/pallas_call | solution.py:127
  112.1 6.8 %fusion.98 = (bf16[1,4,240,1280]{3,2,1,0:T(8,128)(2,1)}, bf16[1,4,240,1280]{3,2,1,0:T(8,128)(2,1)}, bf16[1,4,240,1280]{3,2,1,0:T(8,128)(2,1)}, bf16[1,4,240,1280]{3,2,1,0:T(8,128)(2,1)S(1)}) fusion(bf16[5,4,240,1280]{3,2,1,0:T(8,128)(2,1)} %get-tuple-element.165), kind=kLoop, calls=%fused_computation.195 | loop fusion | bytes 19660800 | tf_op jit(solution)/shard_map/slice | solution.py:463
  118.9 1.7 slice_bitcast_fusion.19
  121.6 1.6 fusion.42
  126.7 1.1 slice.189
  128.0 2.2 all_gather.11
  130.2 21.9 %all-gather.2.cloned.1.call-done = bf16[1024,640]{0,1:T(8,128)(2,1)} async-done(((bf16[128,640]{0,1:T(8,128)(2,1)}), bf16[1024,640]{0,1:T(8,128)(2,1)}) %all-gather.2.cloned.1.call-update) | async-done | bytes 1310736 | tf_op jit(solution)/shard_map/all_gather | solution.py:505
  152.1 3.6 reshape.435
  155.9 15.7 %while.37 = (s32[]{:T(128)}, f32[128,5,3]{0,2,1:T(4,128)S(1)}, f32[128,5,3]{0,2,1:T(4,128)S(1)}, s32[2]{0:T(128)S(1)}, s32[128]{0:T(128)}, /*index=5*/bf16[2,512...) while((s32[]{:T(128)}, f32[128,5,3]{0,2,1:T(4,128)S(1)}, ...), condition=%wide.region_6.7_spmd.clone, body=%wide.region_3.6_spmd.clone.sunk | while | flops 133900288 | bytes 10050724 | solution.py:525
  158.1 2.6 fusion.150
  160.7 3.0 select_reduce_fusion.2
  165.9 2.6 fusion.150
  168.5 3.0 select_reduce_fusion.2
  172.2 9.9 %while.38 = (s32[]{:T(128)}, f32[128,5,3,64]{0,3,2,1:T(8,128)}, bf16[2,512,2,5,64]{1,4,3,2,0:T(8,128)(2,1)S(1)}, s32[2]{0:T(128)S(1)}, s32[128]{0:T(128)}, /*ind...) while((s32[]{:T(128)}, f32[128,5,3,64]{0,3,2,1:T(8,128)}, ...), condition=%wide.region_8.9_spmd.clone, body=%wide.region_7.8_spmd.clone.sunk | while | flops 256033408 | bytes 3339427 | solution.py:542
  174.4 2.7 fusion.153
  179.2 3.0 fusion.153
  182.2 1.1 convert_element_type.172
  183.3 3.7 multiply_reduce_fusion.1
  187.2 2.5 all_gather.10
  192.2 2.3 multiply_convert_fusion
  195.4 1.6 fusion.48
  197.0 2.0 copy.122
  199.1 3.3 convolution_convert_fusion.4
  202.5 2.1 copy.120
  204.6 1.1 reduce-scatter.12.cloned.1.call-done
  205.7 1.1 copy.123
  207.8 9.9 %reduce-scatter.10.cloned.1.call-done = bf16[128,960]{1,0:T(8,128)(2,1)} async-done(((bf16[256,960]{1,0:T(8,128)(2,1)}), bf16[128,960]{1,0:T(8,128)(2,1)}) %reduce-scatter.10.cloned.1.call-update) | async-done | bytes 245776
  217.7 1.1 copy.121
  220.6 3.1 fusion.53
  223.7 1.6 multiply_reduce_fusion
  225.8 29.1 %while.39 = (s32[]{:T(128)}, f32[128,5,3,64]{0,3,2,1:T(8,128)}, bf16[2,512,2,5,64]{1,4,3,2,0:T(8,128)(2,1)}, bf16[2,512,2,5,64]{1,4,3,2,0:T(8,128)(2,1)S(1)}, s3...) while((s32[]{:T(128)}, f32[128,5,3,64]{0,3,2,1:T(8,128)}, ...), condition=%wide.region_15.16_spmd.clone, body=%wide.region_14.15_spmd.clone.sunk | while | flops 641180288 | bytes 53539712 | solution.py:620
  227.0 1.8 dynamic_slice.40
  230.3 2.4 fusion.162
  232.8 2.3 fusion.163
  235.0 3.0 fusion.164
  239.4 1.0 copy-done.33
  241.3 1.8 dynamic_slice.40
  244.6 2.4 fusion.162
  247.0 2.4 fusion.163
  249.5 3.0 fusion.164
  253.9 1.0 copy-done.33
  254.9 2.7 copy.98
  257.9 1.4 copy.124
  262.6 3.5 pad_maximum_fusion.ffn
  266.9 3.0 convert_bitcast_fusion
  269.9 24.0 %reduce-scatter.14.cloned.1.call-done = bf16[128,640]{1,0:T(8,128)(2,1)} async-done(((bf16[1024,640]{1,0:T(8,128)(2,1)}), bf16[128,640]{1,0:T(8,128)(2,1)}) %reduce-scatter.14.cloned.1.call-update) | async-done | bytes 163856
  293.9 1.7 fusion.99
  295.7 1.6 copy.127
  298.4 2.9 fusion.75
  304.1 6.5 %fusion.37.attn = bf16[2,4,256,1280]{3,2,1,0:T(8,128)(2,1)} fusion(bf16[1,4,16,1280]{3,2,1,0:T(8,128)(2,1)S(1)} %pad_bitcast_fusion, bf16[1,4,240,960]{3,2,1,0:T(8,128)(2,1)} %convert_bitcast_fusion, bf16[1,4,240,320]{3,2,1,0:T(8,128)(2,1)} %bitcast.340, bf16[1,4,240,1280]{3,2,1,0:T(8,128)(2,1)S(1)} %bitcast.330), kind=kLoop, calls=%fused_computation.60 | loop fusion | flops 26214400 | bytes 10321920 | tf_op jit(solution)/shard_map/concatenate | solution.py:660
  310.6 155.6 %reduce_grads.1 = (bf16[2,256,1280]{2,1,0:T(8,128)(2,1)}, bf16[3,240,1280]{2,1,0:T(8,128)(2,1)}) custom-call(bf16[2,4,256,1280]{3,2,1,0:T(8,128)(2,1)} %fusion.37.attn, bf16[3,4,240,1280]{3,2,1,0:T(8,128)(2,1)} %pad_maximum_fusion.ffn), custom_call_target="tpu_custom_call" | custom-call | tf_op jit(solution)/shard_map/reduce_grads/pallas_call | solution.py:321
  466.2 1.1 slice_bitcast_fusion.26
  467.3 1.1 slice_bitcast_fusion.25
  468.4 1.3 slice_bitcast_fusion.24
  469.8 2.0 multiply_subtract_fusion
  471.8 3.3 copy.105
  475.1 3.3 copy.106
  478.5 3.3 copy.107
  482.8 3.7 add_subtract_fusion
  486.6 3.7 multiply_subtract_fusion.2
  490.3 1.3 multiply_subtract_fusion.3
  491.6 3.1 multiply_subtract_fusion.1
  (251 shorter events, 36.2 us)
Async XLA Ops:
  7.2 2.5 copy-start.5
  7.2 144.9 %all-gather.2.cloned.1.call-start = ((), (), s32[]{:S(2)}) async-start(), calls=%async_computation.3 | async-start | bytes 1474560 | tf_op jit(solution)/shard_map/all_gather | solution.py:505
  7.2 1.8 copy-start.17
  9.8 1.3 copy-start.10
  11.2 1.6 copy-start.12
  112.1 9.4 %copy-start.19 = (bf16[128,960]{0,1:T(8,128)(2,1)S(1)}, bf16[128,960]{0,1:T(8,128)(2,1)}, u32[]{:S(2)}) copy-start(bf16[128,960]{0,1:T(8,128)(2,1)} %param.24) | copy-start | bytes 737284
  118.9 4.4 copy-start.24
  120.6 2.7 copy-start.41
  121.5 1.8 copy-start.51
  121.6 1.6 copy-start.58
  121.6 2.6 copy-start.62
  124.2 3.8 copy-start.38
  126.7 79.0 %reduce-scatter.12.cloned.1.call-start = ((), (), s32[]{:S(2)}) async-start(), calls=%async_computation.5 | async-start | bytes 786432
  130.2 61.3 %copy-start.15 = (bf16[256,960]{0,1:T(8,128)(2,1)}, bf16[256,960]{0,1:T(8,128)(2,1)S(1)}, u32[]{:S(2)}) copy-start(bf16[256,960]{0,1:T(8,128)(2,1)S(1)} %all_gather.11) | copy-start | bytes 1474564
  172.2 11.0 %copy-start.20 = (bf16[128,960]{0,1:T(8,128)(2,1)S(1)}, bf16[128,960]{0,1:T(8,128)(2,1)}, u32[]{:S(2)}) copy-start(bf16[128,960]{0,1:T(8,128)(2,1)} %param.24) | copy-start | bytes 737284
  183.2 7.3 %copy-start.40 = (bf16[128,5,3,64]{0,3,2,1:T(8,128)(2,1)}, bf16[128,5,3,64]{0,3,2,1:T(8,128)(2,1)S(1)}, u32[]{:S(2)}) copy-start(bf16[128,5,3,64]{0,3,2,1:T(8,128)(2,1)S(1)} %convert_element_type.172) | copy-start | bytes 737284
  183.2 6.4 %copy-start.8 = (bf16[1,4,240,1280]{3,2,1,0:T(8,128)(2,1)S(1)}, bf16[1,4,240,1280]{3,2,1,0:T(8,128)(2,1)}, u32[]{:S(2)}) copy-start(bf16[1,4,240,1280]{3,2,1,0:T(8,128)(2,1)} %get-tuple-element.527) | copy-start | bytes 7372804
  187.1 3.4 copy-start.7
  189.7 1.8 copy-start.2
  190.6 1.7 copy-start.26
  194.5 2.5 copy-start.43
  195.4 3.8 copy-start.47
  199.1 18.7 %reduce-scatter.10.cloned.1.call-start = ((), (), s32[]{:S(2)}) async-start(), calls=%async_computation.4 | async-start | bytes 786432
  202.5 16.4 %copy-start.39 = (bf16[128,960]{0,1:T(8,128)(2,1)S(1)}, bf16[128,960]{0,1:T(8,128)(2,1)}, u32[]{:S(2)}) copy-start(bf16[128,960]{0,1:T(8,128)(2,1)} %param.25) | copy-start | bytes 737284
  204.6 89.4 %reduce-scatter.14.cloned.1.call-start = ((), (), s32[]{:S(2)}) async-start(), calls=%async_computation.6 | async-start | bytes 1474560
  218.9 4.8 copy-start.27
  226.3 6.4 %copy-start.1 = (bf16[512,2,5,64]{0,3,2,1:T(8,128)(2,1)}, bf16[512,2,5,64]{0,3,2,1:T(8,128)(2,1)S(1)}, u32[]{:S(2)}) copy-start(bf16[512,2,5,64]{0,3,2,1:T(8,128)(2,1)S(1)} %dynamic-slice_bitcast_fusion.8) | copy-start | bytes 1966084 | tf_op jit(solution)/shard_map/while
  226.3 4.0 copy-start.54
  227.0 5.7 %copy-start = (f32[5,512,128,3]{2,1,3,0:T(8,128)}, f32[5,512,128,3]{2,1,3,0:T(8,128)S(1)}, u32[]{:S(2)}) copy-start(f32[5,512,128,3]{2,1,3,0:T(8,128)S(1)} %fusion.161) | copy-start | bytes 11796484 | tf_op jit(solution)/shard_map/while
  230.3 2.4 copy-start.28
  232.8 2.3 copy-start.29
  238.0 1.3 copy-start.32
  240.5 6.4 %copy-start.1 = (bf16[512,2,5,64]{0,3,2,1:T(8,128)(2,1)}, bf16[512,2,5,64]{0,3,2,1:T(8,128)(2,1)S(1)}, u32[]{:S(2)}) copy-start(bf16[512,2,5,64]{0,3,2,1:T(8,128)(2,1)S(1)} %dynamic-slice_bitcast_fusion.8) | copy-start | bytes 1966084 | tf_op jit(solution)/shard_map/while
  240.6 4.0 copy-start.54
  241.3 5.7 %copy-start = (f32[5,512,128,3]{2,1,3,0:T(8,128)}, f32[5,512,128,3]{2,1,3,0:T(8,128)S(1)}, u32[]{:S(2)}) copy-start(f32[5,512,128,3]{2,1,3,0:T(8,128)S(1)} %fusion.161) | copy-start | bytes 11796484 | tf_op jit(solution)/shard_map/while
  244.6 2.4 copy-start.28
  247.0 2.4 copy-start.29
  252.5 1.3 copy-start.32
  257.9 1.5 copy-start.16
  257.9 1.5 copy-start.48
  262.6 3.5 copy-start.55
  262.6 4.2 copy-start.4
  262.6 4.3 copy-start.14
  266.8 31.5 %copy-start.21 = (bf16[128,960]{0,1:T(8,128)(2,1)S(1)}, bf16[128,960]{0,1:T(8,128)(2,1)}, u32[]{:S(2)}) copy-start(bf16[128,960]{0,1:T(8,128)(2,1)} %param.24) | copy-start | bytes 737284
  266.8 31.5 %copy-start.25 = (bf16[1,4,240,1280]{3,2,1,0:T(8,128)(2,1)S(1)}, bf16[1,4,240,1280]{3,2,1,0:T(8,128)(2,1)}, u32[]{:S(2)}) copy-start(bf16[1,4,240,1280]{3,2,1,0:T(8,128)(2,1)} %copy-done.24) | copy-start | bytes 7372804
  298.4 3.0 copy-start.50
  298.4 3.0 copy-start.52
  298.4 3.0 copy-start.59
  310.6 159.2 %copy-start.22 = (f32[240,2,1280]{2,1,0:T(2,128)S(1)}, f32[240,2,1280]{2,1,0:T(2,128)}, u32[]{:S(2)}) copy-start(f32[240,2,1280]{2,1,0:T(2,128)} %param.34) | copy-start | bytes 7372804
  310.6 159.2 %copy-start.23 = (f32[240,2,1280]{2,1,0:T(2,128)S(1)}, f32[240,2,1280]{2,1,0:T(2,128)}, u32[]{:S(2)}) copy-start(f32[240,2,1280]{2,1,0:T(2,128)} %param.35) | copy-start | bytes 7372804
  466.2 3.6 copy-start.6
  478.4 3.3 copy-start.49
  478.4 4.3 copy-start.18
  478.4 4.3 copy-start.36
  478.4 4.3 copy-start.37
  482.8 3.7 copy-start.11
  482.8 3.7 copy-start.34
  482.8 3.7 copy-start.35
  486.5 3.8 copy-start.57
  486.5 3.8 copy-start.60
  486.5 3.7 copy-start.61
  486.5 5.0 %copy-start.9 = (f32[240,1600]{1,0:T(8,128)S(1)}, f32[240,1600]{1,0:T(8,128)}, u32[]{:S(2)}) copy-start(f32[240,1600]{1,0:T(8,128)} %param.27) | copy-start | bytes 4608004
  486.5 5.0 %copy-start.30 = (f32[240,1600]{1,0:T(8,128)S(1)}, f32[240,1600]{1,0:T(8,128)}, u32[]{:S(2)}) copy-start(f32[240,1600]{1,0:T(8,128)} %param.28) | copy-start | bytes 4608004
  486.5 5.0 copy-start.31
  (10 other events, 9.4 us)
Sparse Core Ops, SparseCore 0:
  126.8 25.2 all-gather.1
  199.2 6.4 reduce-scatter.11
  208.6 9.0 reduce-scatter.9
  259.5 34.3 reduce-scatter.13

commit v2 on v1

--- a/solution.py
+++ b/solution.py
@@ -29,7 +29,9 @@
 MESH = pl.DeviceIdType.MESH
 BF16 = jnp.bfloat16
 GAIN_ROWS = 16
-ROW_CHUNKS = 3
+ROW_TILE = 16
+ATTN_CHUNKS = 4
+FFN_CHUNKS = 3
 
 
 def plane_peers():
@@ -52,9 +54,9 @@
     s, c, t, across, along, diagonal = plane_peers()
     to_x, to_y, to_d, to_core = (across, c, t), (along, c, t), (diagonal, c, t), (s, c, 1 - t)
     greet((to_x, to_y, to_d, to_core))
-
-    def block(k):
-        return t if k == 0 else k + 1
+    rows = w.shape[1]
+    upper = (rows // 2 + ROW_TILE - 1) // ROW_TILE * ROW_TILE
+    parts = (pl.ds(0, upper), pl.ds(upper, rows - upper))
 
     def copy(src, dst, lane, k, device):
         return pltpu.make_async_remote_copy(
@@ -67,57 +69,49 @@
         )
 
     def own(lane, k):
-        return copy(w.at[block(k)], out.at[block(k), s], lane, k, (to_x, to_y)[lane])
+        return copy(w.at[t, parts[k]], out.at[t, s, parts[k]], lane, k, (to_x, to_y)[lane])
 
     def onward(k):
-        if k < 2:
-            place = out.at[block(k), across]
-            return copy(place, place, 2, k, to_y)
-        place = out.at[block(k), along]
-        return copy(place, place, 2, k, to_x)
-
-    def sideways(i):
-        place = out.at[t, (across, along, diagonal)[i]]
-        return copy(place, place, 3, i, to_core)
+        place = out.at[t, (across, along)[k], parts[k]]
+        return copy(place, place, 2, k, (to_y, to_x)[k])
+
+    def sideways(i, k):
+        place = out.at[t, (across, along, diagonal)[i], parts[k]]
+        return copy(place, place, 3 + i, k, to_core)
 
     def small(i):
-        return copy(gains, gains_out.at[s], 4, i, (to_x, to_y, to_d)[i])
+        return copy(gains, gains_out.at[s], 6, i, (to_x, to_y, to_d)[i])
 
     keep = pltpu.make_async_copy(w, out.at[:, s], local.at[0])
     keep_gains = pltpu.make_async_copy(gains, gains_out.at[s], local.at[1])
+    for k in range(2):
+        own(0, k).start()
+        own(1, 1 - k).start()
     for i in range(3):
         small(i).start()
-    for k in range(4):
-        own(0, k).start()
-        own(1, (k + 2) % 4).start()
     keep.start()
     keep_gains.start()
+    own(0, 0).wait_recv()
+    onward(0).start()
+    own(1, 1).wait_recv()
+    onward(1).start()
+    sideways(0, 0).start()
+    sideways(1, 1).start()
+    own(0, 1).wait_recv()
+    sideways(0, 1).start()
+    own(1, 0).wait_recv()
+    sideways(1, 0).start()
     for k in range(2):
-        own(0, k).wait_recv()
-        onward(k).start()
-        if k == 0:
-            sideways(0).start()
-        own(1, k + 2).wait_recv()
-        onward(k + 2).start()
-    own(1, 0).wait_recv()
-    sideways(1).start()
-    own(1, 1).wait_recv()
-    own(0, 2).wait_recv()
-    own(0, 3).wait_recv()
-    onward(0).wait_recv()
-    sideways(2).start()
-    for k in range(1, 4):
         onward(k).wait_recv()
+        sideways(2, k).start()
     for i in range(3):
-        sideways(i).wait_recv()
-        small(i).wait_recv()
-    for k in range(4):
+        for k in range(2):
+            sideways(i, k).wait()
+        small(i).wait()
+    for k in range(2):
         own(0, k).wait_send()
         own(1, k).wait_send()
         onward(k).wait_send()
-    for i in range(3):
-        sideways(i).wait_send()
-        small(i).wait_send()
     keep.wait()
     keep_gains.wait()
 
@@ -133,8 +127,8 @@
         in_specs=[pl.BlockSpec(memory_space=pl.ANY)] * 2,
         out_specs=[pl.BlockSpec(memory_space=pl.ANY)] * 2,
         scratch_shapes=[
-            pltpu.SemaphoreType.DMA((5, 4)),
-            pltpu.SemaphoreType.DMA((5, 4)),
+            pltpu.SemaphoreType.DMA((7, 3)),
+            pltpu.SemaphoreType.DMA((7, 3)),
             pltpu.SemaphoreType.DMA((2,)),
         ],
         compiler_params=pltpu.CompilerParams(collective_id=0, has_side_effects=True),
@@ -142,14 +136,45 @@
     )(w, gains)
 
 
+ACROSS = ((0, 1), (1, 0), (2, 3), (3, 2))
+ALONG = ((0, 2), (2, 0), (1, 3), (3, 1))
+
+
+def swap(block, pairs):
+    return lax.ppermute(block, "shard", pairs)
+
+
+def plane_gather(block, x_first):
+    s, c, t, across, along, diagonal = plane_peers()
+    from_x, from_y = swap(block, ACROSS), swap(block, ALONG)
+    from_d = swap(from_x, ALONG) if x_first else swap(from_y, ACROSS)
+    whole = jnp.zeros((4,) + block.shape, block.dtype)
+    for owner, part in ((s, block), (across, from_x), (along, from_y), (diagonal, from_d)):
+        whole = lax.dynamic_update_index_in_dim(whole, part, owner, 0)
+    return whole
+
+
+def plane_scatter(blocks, x_first):
+    s, c, t, across, along, diagonal = plane_peers()
+    near, far, straight, turn = (across, along, ACROSS, ALONG) if x_first else (along, across, ALONG, ACROSS)
+
+    def part(owner):
+        return lax.dynamic_index_in_dim(blocks, owner, 0, keepdims=False)
+
+    first = swap(part(diagonal), straight)
+    direct = swap(part(near), straight)
+    summed = swap((part(far).astype(jnp.float32) + first.astype(jnp.float32)).astype(BF16), turn)
+    total = part(s).astype(jnp.float32) + direct.astype(jnp.float32) + summed.astype(jnp.float32)
+    return total.astype(BF16)
+
+
 def reduce_kernel(
     n, chunks, attn, ffn, attn_out, ffn_out, side, first, partial, direct, summed, line, middle, carry, send, recv
 ):
     s, c, t, across, along, diagonal = plane_peers()
     half = n // 2
-    low = c < half
-    inner = jnp.where(low, c + 1, c - 1)
-    outer = jnp.where(low, c - 1, c + 1)
+    inner = jnp.where(c < half, c + 1, c - 1)
+    outer = jnp.where(c < half, c - 1, c + 1)
     to_x, to_y, to_core = (across, c, t), (along, c, t), (s, c, 1 - t)
     at_end = (c == 0) | (c == n - 1)
     at_middle = (c == half - 1) | (c == half)
@@ -176,14 +201,19 @@
             device_id_type=MESH,
         )
 
+    count = len(chunks)
+    attn_chunks = [i for i in range(count) if chunks[i][0] == 0]
+    base = attn_chunks[0]
+
     def rows_of(i, buffer):
         return buffer.at[i, pl.ds(0, chunks[i][2])]
 
+    def plane_rows(i, buffer):
+        return buffer.at[i - base, pl.ds(0, chunks[i][2])]
+
     def mine(i, owner):
         k, start, size = chunks[i]
-        if k == 0:
-            return side.at[owner, pl.ds(start, size)]
-        return ffn.at[k - 1, owner, pl.ds(start, size)]
+        return side.at[owner, pl.ds(start, size)]
 
     def result(i):
         k, start, size = chunks[i]
@@ -191,8 +221,12 @@
             return attn_out.at[t, pl.ds(start, size)]
         return ffn_out.at[k - 1, pl.ds(start, size)]
 
+    def addend(i):
+        k, start, size = chunks[i]
+        return rows_of(i, carry) if k == 0 else ffn.at[k - 1, pl.ds(start, size)]
+
     def x_first(i):
-        return chunks[i][0] < 2
+        return (i - base) % 2 == 0
 
     def add(*refs):
         total = refs[0][...].astype(jnp.float32)
@@ -201,16 +235,19 @@
         return total.astype(BF16)
 
     def send_first(i):
-        return copy(mine(i, diagonal), rows_of(i, first), 0, i, to_x if x_first(i) else to_y)
+        return copy(mine(i, diagonal), plane_rows(i, first), 0, i, to_x if x_first(i) else to_y)
 
     def send_direct(i):
         owner, device = (across, to_x) if x_first(i) else (along, to_y)
-        return copy(mine(i, owner), rows_of(i, direct), 1, i, device)
+        return copy(mine(i, owner), plane_rows(i, direct), 1, i, device)
 
     def send_summed(i):
-        return copy(rows_of(i, partial), rows_of(i, summed), 2, i, to_y if x_first(i) else to_x)
+        return copy(plane_rows(i, partial), plane_rows(i, summed), 2, i, to_y if x_first(i) else to_x)
 
     def send_in(i):
+        return copy(addend(i), rows_of(i, line), 3, i, (s, inner, t))
+
+    def send_through(i):
         return copy(rows_of(i, carry), rows_of(i, line), 3, i, (s, inner, t))
 
     def send_middle(i):
@@ -225,41 +262,37 @@
     def send_side():
         return copy(attn.at[1 - t], side, 7, 0, to_core)
 
-    count = len(chunks)
-    send_side().start()
-    for i in range(count):
-        if chunks[i][0] != 0:
+    def start_in(i):
+        @pl.when(at_end)
+        def _():
+            send_in(i).start()
+
+    def stage_cores():
+        send_side().wait()
+        for owner in range(4):
+            side[owner] = add(attn.at[t, owner], side.at[owner])
+        for i in attn_chunks:
             send_first(i).start()
-            send_direct(i).start()
-
-    send_side().wait()
-    for owner in range(4):
-        side[owner] = add(attn.at[t, owner], side.at[owner])
-    for i in range(count):
-        if chunks[i][0] == 0:
-            send_first(i).start()
+        for i in attn_chunks:
             send_direct(i).start()
 
     def stage_plane(i):
         send_first(i).wait_recv()
         owner = along if x_first(i) else across
-        partial[i, pl.ds(0, chunks[i][2])] = add(mine(i, owner), rows_of(i, first))
+        partial[i - base, pl.ds(0, chunks[i][2])] = add(mine(i, owner), plane_rows(i, first))
         send_summed(i).start()
 
-    def stage_in(i):
+    def stage_chips(i):
         send_direct(i).wait_recv()
         send_summed(i).wait_recv()
-        carry[i, pl.ds(0, chunks[i][2])] = add(mine(i, s), rows_of(i, direct), rows_of(i, summed))
-
-        @pl.when(at_end)
-        def _():
-            send_in(i).start()
+        carry[i, pl.ds(0, chunks[i][2])] = add(mine(i, s), plane_rows(i, direct), plane_rows(i, summed))
+        start_in(i)
 
     def stage_fold(i):
         @pl.when(jnp.logical_not(at_end))
         def _():
             send_in(i).wait_recv()
-            carry[i, pl.ds(0, chunks[i][2])] = add(rows_of(i, carry), rows_of(i, line))
+            carry[i, pl.ds(0, chunks[i][2])] = add(addend(i), rows_of(i, line))
 
             @pl.when(at_middle)
             def _():
@@ -267,7 +300,7 @@
 
             @pl.when(jnp.logical_not(at_middle))
             def _():
-                send_in(i).start()
+                send_through(i).start()
 
     def stage_total(i):
         @pl.when(at_middle)
@@ -287,37 +320,43 @@
         if chunks[i][0] == 0:
             send_core(i).start()
 
-    stages = (stage_plane, stage_in, stage_fold, stage_total)
-    for step in range(count + len(stages) - 1):
-        for depth, stage in enumerate(stages):
-            if 0 <= step - depth < count:
-                stage(step - depth)
+    send_side().start()
+    for i in range(base):
+        start_in(i)
+    for step in range(count + 1):
+        if step == 2:
+            stage_cores()
+        if step == 4:
+            for i in attn_chunks:
+                stage_plane(i)
+        if 6 <= step < 6 + len(attn_chunks):
+            stage_chips(attn_chunks[step - 6])
+        if step < count:
+            stage_fold(step)
+        if step >= 1:
+            stage_total(step - 1)
     for i in range(count):
-        send_first(i).wait_send()
-        send_direct(i).wait_send()
-        send_summed(i).wait_send()
+        if chunks[i][0] == 0:
+            send_first(i).wait_send()
+            send_direct(i).wait_send()
+            send_summed(i).wait_send()
+            send_core(i).wait()
 
         @pl.when(jnp.logical_not(at_end))
         def _():
             send_out(i).wait_send()
 
-        if chunks[i][0] == 0:
-            send_core(i).wait()
-
 
 def reduce_grads(n, attn, ffn):
-    attn_rows, ffn_rows, cols = attn.shape[2], ffn.shape[2], attn.shape[3]
+    attn_rows, ffn_rows, cols = attn.shape[2], ffn.shape[1], attn.shape[3]
     chunks = []
-    step = ffn_rows // ROW_CHUNKS
-    tail = attn_rows - step * (ROW_CHUNKS - 1)
     for k in (1, 2, 3, 0):
-        for j in range(ROW_CHUNKS):
-            chunks.append((k, j * step, tail if k == 0 and j == ROW_CHUNKS - 1 else step))
-    order = [i for pair in zip(range(ROW_CHUNKS), range(ROW_CHUNKS, 2 * ROW_CHUNKS)) for i in pair]
-    order = order + list(range(2 * ROW_CHUNKS, 4 * ROW_CHUNKS))
-    chunks = [chunks[i] for i in order]
-    count, most = len(chunks), max(step, tail)
+        rows, pieces = (attn_rows, ATTN_CHUNKS) if k == 0 else (ffn_rows, FFN_CHUNKS)
+        for j in range(pieces):
+            chunks.append((k, j * (rows // pieces), rows // pieces))
+    count, most = len(chunks), max(size for k, start, size in chunks)
     held = pltpu.VMEM((count, most, cols), BF16)
+    plane_held = pltpu.VMEM((ATTN_CHUNKS, most, cols), BF16)
     return pl.pallas_call(
         functools.partial(reduce_kernel, n, tuple(chunks)),
         out_shape=(
@@ -327,10 +366,11 @@
         in_specs=[pl.BlockSpec(memory_space=pltpu.VMEM)] * 2,
         out_specs=[pl.BlockSpec(memory_space=pltpu.VMEM)] * 2,
         scratch_shapes=[pltpu.VMEM((4, attn_rows, cols), BF16)]
-        + [held] * 7
+        + [plane_held] * 4
+        + [held] * 3
         + [pltpu.SemaphoreType.DMA((8, count)), pltpu.SemaphoreType.DMA((8, count))],
         compiler_params=pltpu.CompilerParams(
-            collective_id=1, has_side_effects=True, vmem_limit_bytes=56 * 1024 * 1024
+            collective_id=1, has_side_effects=True, vmem_limit_bytes=48 * 1024 * 1024
         ),
         name="reduce_grads",
     )(attn, ffn)
@@ -447,20 +487,26 @@
     plane = plane and hidden_units == width
     if plane:
         weights = jnp.stack(
-            [
-                qkv_low[:, :width],
-                jnp.concatenate([qkv_low[:, width:], out_low], axis=1),
-                gate_up_low[:, 0],
-                gate_up_low[:, 1],
-                down_low.T,
-            ]
+            [qkv_low[:, :width], jnp.concatenate([qkv_low[:, width:], out_low], axis=1)]
         )
         own_gains = jnp.pad(gains_low, ((0, GAIN_ROWS - 2), (0, 0)))
         gathered, gains_parts = gather_weights(weights, own_gains)
-        gathered = gathered.reshape(5, MODEL_WIDTH, width)
+        gathered, gains_parts, gate_low, up_low, down_low_t = lax.optimization_barrier(
+            (gathered, gains_parts, gate_up_low[:, 0], gate_up_low[:, 1], down_low.T)
+        )
+        gathered = gathered.reshape(2, MODEL_WIDTH, width)
         qkv_mat = jnp.concatenate([gathered[0], gathered[1, :, :KEY_COLUMNS]], axis=1)
         out_mat = gathered[1, :, KEY_COLUMNS:]
-        gate_mat, up_mat, down_mat_t = gathered[2], gathered[3], gathered[4]
+        gate_mat = plane_gather(gate_low, True).reshape(MODEL_WIDTH, hidden_units)
+        up_mat = plane_gather(up_low, False).reshape(MODEL_WIDTH, hidden_units)
+        middle_column = hidden_units // 2
+        down_mat_t = jnp.concatenate(
+            [
+                plane_gather(down_low_t[:, :middle_column], True),
+                plane_gather(down_low_t[:, middle_column:], False),
+            ],
+            axis=2,
+        ).reshape(MODEL_WIDTH, hidden_units)
         gains_all = gains_parts[:, :2].transpose(1, 0, 2).reshape(2, MODEL_WIDTH)
     else:
         qkv_mat = lax.all_gather(qkv_low, "shard", axis=0, tiled=True)
@@ -658,9 +704,20 @@
         )
         gain_rows = jnp.stack([gain_rows, jnp.zeros_like(gain_rows)])
         attn_grad = jnp.concatenate([attn_grad, gain_rows], axis=2)
+        gate_blocks, up_blocks, down_blocks = (
+            part.astype(jnp.bfloat16).reshape(4, rows, width)
+            for part in (gate_grad, upward_grad, down_grad_t)
+        )
+        down_part = jnp.concatenate(
+            [
+                plane_scatter(down_blocks[:, :, :middle_column], True),
+                plane_scatter(down_blocks[:, :, middle_column:], False),
+            ],
+            axis=1,
+        )
         ffn_grad = jnp.stack(
-            [part.astype(jnp.bfloat16) for part in (gate_grad, upward_grad, down_grad_t)]
-        ).reshape(3, 4, rows, width)
+            [plane_scatter(gate_blocks, True), plane_scatter(up_blocks, False), down_part]
+        )
         attn_red, ffn_red = reduce_grads(lax.axis_size("context"), attn_grad, ffn_grad)
         gains_red = attn_red[0, rows : rows + 2, :rows].astype(jnp.float32)
         qkv_red = jnp.concatenate(

time: 510 us -> 430 us (0.84)
  Pallas kernels: 254 us -> 119 us
  starting transfers between devices: 0.16 us -> 25.1 us
  local copies, waits for them, and re-layouts: 62 us -> 78.4 us
  other arithmetic: 46.8 us -> 56.1 us
    pallas_call x1, Pallas kernels: 156 us -> 76 us  [reduce_grads(): pl.pallas_call(functools.partial(reduce_kernel, n, tuple(chunks)), out_sh...]
    ppermute x0 -> x24, waiting for transfers between devices: none -> 59.4 us  [swap(): return lax.ppermute(block, 'shard', pairs)]
    pallas_call x1, Pallas kernels: 98.7 us -> 42.9 us  [gather_weights(): pl.pallas_call(gather_kernel, out_shape=(jax.ShapeDtypeStruct((blocks, 4,...]
    unnamed x7, waiting for transfers between devices: 35.1 us -> 0.09 us
    ppermute x0 -> x24, starting transfers between devices: none -> 24.9 us  [swap(): return lax.ppermute(block, 'shard', pairs)]
    all_gather x1, waiting for transfers between devices: 21.9 us -> 0.01 us  [shards(): lax.all_gather(kv_local, ('context', 'tensor'), axis=0, tiled=True)]
    dynamic_update_slice x0 -> x16, local copies, waits for them, and re-layouts: none -> 12.8 us  [plane_gather(): whole = lax.dynamic_update_index_in_dim(whole, part, owner, 0)]
    convert_element_type x0 -> x6, other arithmetic: none -> 10.3 us  [the longest x4 7.88 us: plane_scatter(): (part(far).astype(jnp.float32) + first.astype(jnp.float32)).astype(BF16)]
  transfers between devices with their start and end apart: 4 -> 28, of which waited for: 4 -> 9; matrix products, arithmetic and copies ran while one was open for 4% -> 23% of each run, Pallas kernels for 0% -> 0%
where the time goes in v2:
time: 430 us; the launch traced here: 424 us
  Pallas kernels  119 us (28%)
  local copies, waits for them, and re-layouts  78.4 us (18%)
  matrix products  61.4 us (14%)
  waiting for transfers between devices  59.5 us (14%)
  other arithmetic  56.1 us (13%)
  starting transfers between devices  25.1 us (6%)
  between operations  15.3 us (4%)
  blocking collectives  4.94 us (1%)
  loops' own time  4.68 us (1%)
    pallas_call x1, Pallas kernels, reduce_grads(): pl.pallas_call(functools.partial(reduce_kernel, n, tuple(chunks)), out_sh...  76 us
    ppermute x24, waiting for transfers between devices, swap(): return lax.ppermute(block, 'shard', pairs)  59.4 us
    pallas_call x1, Pallas kernels, gather_weights(): pl.pallas_call(gather_kernel, out_shape=(jax.ShapeDtypeStruct((blocks, 4,...  42.9 us
    unnamed x145, local copies, waits for them, and re-layouts  28 us
    ppermute x24, starting transfers between devices, swap(): return lax.ppermute(block, 'shard', pairs)  24.9 us
    dynamic_update_slice x16, local copies, waits for them, and re-layouts, plane_gather(): whole = lax.dynamic_update_index_in_dim(whole, part, owner, 0)  12.8 us
    sub x5, other arithmetic, adam_step(): weight - learning * (first_hat / (jnp.sqrt(second_hat) + ADAM_EPS) + deca...  10.6 us
  transfers between devices with their start and end apart: 28, of which 9 were waited for; matrix products, arithmetic and copies ran while one was open for 23% of the time, Pallas kernels for 0%

profile of v2, /device:TPU:0, one launch (start us, length us, event | category | flops | bytes accessed | tf_op | source)
XLA Modules:
  0.0 424.4 jit_solution(18225425678075625840)
XLA Ops:
  7.3 1.7 convert_element_type.270
  14.8 42.9 %gather_weights.1 = (bf16[2,4,240,1280]{3,2,1,0:T(8,128)(2,1)}, bf16[4,16,240]{2,1,0:T(8,128)(2,1)}) custom-call(bf16[2,240,1280]{2,1,0:T(8,128)(2,1)} %pad_maximum_fusion.6.w, bf16[16,240]{1,0:T(8,128)(2,1)} %pad.9.gains), custom_call_target="tpu_custom_call" | custom-call | tf_op jit(solution)/shard_map/gather_weights/pallas_call | solution.py:121
  62.6 1.9 slice.140
  64.5 2.6 slice_bitcast_fusion.19
  68.7 2.8 fusion.42
  78.5 2.6 all_gather.11
  82.5 1.6 broadcast.256.clone.1
  85.7 1.7 bitcast_dynamic-update-slice_fusion.10
  91.5 1.7 bitcast_dynamic-update-slice_fusion.9
  95.4 6.5 %collective-permute-done.4 = bf16[240,1280]{1,0:T(8,128)(2,1)S(1)} collective-permute-done((bf16[240,1280]{1,0:T(8,128)(2,1)S(1)}, bf16[240,1280]{1,0:T(8,128)(2,1)S(1)}, u32[]{:S(2)}, u32[]{:S(2)}) %collective-permute-start.4) | collective-permute-done | bytes 614432 | tf_op jit(solution)/shard_map/ppermute | solution.py:144
  106.5 4.2 collective-permute-done.11
  111.5 10.1 %collective-permute-done.8 = bf16[240,640]{1,0:T(8,128)(2,1)S(1)} collective-permute-done((bf16[240,640]{1,0:T(8,128)(2,1)}, bf16[240,640]{1,0:T(8,128)(2,1)S(1)}, u32[]{:S(2)}, u32[]{:S(2)}) %collective-permute-start.8) | collective-permute-done | bytes 307232 | tf_op jit(solution)/shard_map/ppermute | solution.py:144
  124.0 2.0 convolution_bitcast_fusion.1
  126.0 7.9 %collective-permute-done.2 = bf16[240,1280]{1,0:T(8,128)(2,1)S(1)} collective-permute-done((bf16[240,1280]{1,0:T(8,128)(2,1)S(1)}, bf16[240,1280]{1,0:T(8,128)(2,1)S(1)}, u32[]{:S(2)}, u32[]{:S(2)}) %collective-permute-start.2) | collective-permute-done | bytes 614432 | tf_op jit(solution)/shard_map/ppermute | solution.py:144
  134.9 4.4 %reshape.456 = bf16[2,512,2,5,64]{1,0,4,3,2:T(2,128)(2,1)} reshape(bf16[1024,640]{0,1:T(8,128)(2,1)} %all-gather.2.cloned.1.call-done) | data formatting | bytes 2621440 | tf_op jit(solution)/shard_map/reshape | solution.py:555
  139.2 1.6 copy.94
  140.8 15.8 %while.37 = (s32[]{:T(128)}, f32[128,5,3]{0,2,1:T(4,128)S(1)}, f32[128,5,3]{0,2,1:T(4,128)S(1)}, s32[2]{0:T(128)S(1)}, s32[128]{0:T(128)}, /*index=5*/bf16[2,512...) while((s32[]{:T(128)}, f32[128,5,3]{0,2,1:T(4,128)S(1)}, ...), condition=%wide.region_6.7_spmd.clone, body=%wide.region_3.6_spmd.clone.sunk | while | flops 133900288 | bytes 10050724 | solution.py:571
  142.9 2.7 fusion.160
  145.6 3.0 select_reduce_fusion.2
  150.8 2.7 fusion.160
  153.5 3.0 select_reduce_fusion.2
  157.2 8.1 %while.38 = (s32[]{:T(128)}, f32[128,5,3,64]{0,3,2,1:T(8,128)S(1)}, bf16[2,512,2,5,64]{1,4,3,2,0:T(8,128)(2,1)S(1)}, s32[2]{0:T(128)S(1)}, s32[128]{0:T(128)}, /...) while((s32[]{:T(128)}, f32[128,5,3,64]{0,3,2,1:T(8,128)S(1)}, ...), condition=%wide.region_8.9_spmd.clone, body=%wide.region_7.8_spmd.clone.sunk | while | flops 256033408 | bytes 3339427 | solution.py:588
  159.3 1.9 fusion.163
  163.4 1.9 fusion.163
  165.4 3.8 multiply_reduce_fusion.1
  169.4 2.3 all_gather.10
  173.1 3.2 multiply_convert_fusion.1
  176.3 1.6 convolution_convert_fusion.4
  177.9 2.2 convolution_convert_fusion.1
  181.0 2.3 convolution_convert_fusion.2
  183.3 2.5 fusion.48
  186.9 1.9 fusion.108
  201.3 1.8 fusion.68
  204.6 1.8 fusion.71
  206.4 13.5 %collective-permute-done.16 = bf16[240,1280]{1,0:T(8,128)(2,1)} collective-permute-done((bf16[240,1280]{1,0:T(8,128)(2,1)}, bf16[240,1280]{1,0:T(8,128)(2,1)}, u32[]{:S(2)}, u32[]{:S(2)}) %collective-permute-start.16) | collective-permute-done | bytes 614432 | tf_op jit(solution)/shard_map/ppermute | solution.py:144
  221.3 2.2 fusion.50
  227.7 3.3 fusion.59
  231.0 1.6 multiply_reduce_fusion
  233.1 28.8 %while.39 = (s32[]{:T(128)}, f32[128,5,3,64]{0,3,2,1:T(8,128)}, bf16[2,512,2,5,64]{1,4,3,2,0:T(8,128)(2,1)}, bf16[2,512,2,5,64]{1,4,3,2,0:T(8,128)(2,1)S(1)}, s3...) while((s32[]{:T(128)}, f32[128,5,3,64]{0,3,2,1:T(8,128)}, ...), condition=%wide.region_15.16_spmd.clone, body=%wide.region_14.15_spmd.clone.sunk | while | flops 641180288 | bytes 53603772 | solution.py:666
  234.2 1.8 dynamic_slice.122
  237.4 2.3 fusion.172
  239.8 2.3 fusion.173
  242.1 3.0 fusion.174
  248.4 1.8 dynamic_slice.122
  251.7 2.3 fusion.172
  254.1 2.5 fusion.173
  256.5 3.0 fusion.174
  262.0 2.7 copy.97
  266.0 2.6 copy.123
  269.3 2.0 fusion.53
  280.0 2.9 convert_bitcast_fusion
  283.0 15.6 %collective-permute-done.17 = bf16[240,1280]{1,0:T(8,128)(2,1)} collective-permute-done((bf16[240,1280]{1,0:T(8,128)(2,1)}, bf16[240,1280]{1,0:T(8,128)(2,1)}, u32[]{:S(2)}, u32[]{:S(2)}) %collective-permute-start.17) | collective-permute-done | bytes 614432 | tf_op jit(solution)/shard_map/ppermute | solution.py:144
  298.6 1.7 fusion.67
  303.5 3.7 fusion.85
  308.4 1.6 slice.201
  310.1 6.8 %fusion.37.attn = bf16[2,4,256,1280]{3,2,1,0:T(8,128)(2,1)} fusion(bf16[1,4,16,1280]{3,2,1,0:T(8,128)(2,1)S(1)} %pad_bitcast_fusion, bf16[1,4,240,960]{3,2,1,0:T(8,128)(2,1)} %convert_bitcast_fusion, bf16[1,4,240,320]{3,2,1,0:T(8,128)(2,1)S(1)} %bitcast.407, bf16[1,4,240,1280]{3,2,1,0:T(8,128)(2,1)} %bitcast.402), kind=kLoop, calls=%fused_computation.59 | loop fusion | flops 26214400 | bytes 10321920 | tf_op jit(solution)/shard_map/concatenate | solution.py:706
  316.9 76.0 %reduce_grads.1 = (bf16[2,256,1280]{2,1,0:T(8,128)(2,1)S(1)}, bf16[3,240,1280]{2,1,0:T(8,128)(2,1)S(1)}) custom-call(bf16[2,4,256,1280]{3,2,1,0:T(8,128)(2,1)} %fusion.37.attn, bf16[3,240,1280]{2,1,0:T(8,128)(2,1)S(1)} %pad_maximum_fusion.5.ffn), custom_call_target="tpu_custom_call" | custom-call | tf_op jit(solution)/shard_map/reduce_grads/pallas_call | solution.py:360
  394.7 2.0 multiply_subtract_fusion
  396.6 3.3 copy.104
  400.0 3.3 copy.105
  403.3 3.3 copy.106
  408.0 2.5 add_subtract_fusion
  410.6 2.5 multiply_subtract_fusion.2
  414.3 3.1 multiply_subtract_fusion.1
  (364 shorter events, 94.3 us)
Async XLA Ops:
  7.2 127.6 %all-gather.2.cloned.1.call-start = ((), (), s32[]{:S(2)}) async-start(), calls=%async_computation.3 | async-start | bytes 1474560 | tf_op jit(solution)/shard_map/all_gather | solution.py:551
  58.5 26.6 %collective-permute-start.9 = (bf16[240,640]{1,0:T(8,128)(2,1)}, bf16[240,640]{1,0:T(8,128)(2,1)}, u32[]{:S(2)}, u32[]{:S(2)}) collective-permute-start(bf16[240,640]{1,0:T(8,128)(2,1)} %get-tuple-element.553), channel_id=1, source_target_pairs={{0,8},{8,0},{16,24},{24,16},{1,9},{9,1},{17,25},{25,17},{2,10},{10... | collective-permute-start | bytes 921608 | tf_op jit(solution)/shard_map/ppermute | solution.py:144
  59.1 30.9 %collective-permute-start.10 = (bf16[240,640]{1,0:T(8,128)(2,1)}, bf16[240,640]{1,0:T(8,128)(2,1)}, u32[]{:S(2)}, u32[]{:S(2)}) collective-permute-start(bf16[240,640]{1,0:T(8,128)(2,1)} %get-tuple-element.553), channel_id=1, source_target_pairs={{0,16},{16,0},{8,24},{24,8},{1,17},{17,1},{9,25},{25,9},{2,18},{18... | collective-permute-start | bytes 921608 | tf_op jit(solution)/shard_map/ppermute | solution.py:144
  59.6 27.8 %collective-permute-start.6 = (bf16[240,640]{1,0:T(8,128)(2,1)}, bf16[240,640]{1,0:T(8,128)(2,1)}, u32[]{:S(2)}, u32[]{:S(2)}) collective-permute-start(bf16[240,640]{1,0:T(8,128)(2,1)} %get-tuple-element.552), channel_id=1, source_target_pairs={{0,8},{8,0},{16,24},{24,16},{1,9},{9,1},{17,25},{25,17},{2,10},{10... | collective-permute-start | bytes 921608 | tf_op jit(solution)/shard_map/ppermute | solution.py:144
  61.1 32.1 %collective-permute-start.7 = (bf16[240,640]{1,0:T(8,128)(2,1)}, bf16[240,640]{1,0:T(8,128)(2,1)}, u32[]{:S(2)}, u32[]{:S(2)}) collective-permute-start(bf16[240,640]{1,0:T(8,128)(2,1)} %get-tuple-element.552), channel_id=1, source_target_pairs={{0,16},{16,0},{8,24},{24,8},{1,17},{17,1},{9,25},{25,9},{2,18},{18... | collective-permute-start | bytes 921608 | tf_op jit(solution)/shard_map/ppermute | solution.py:144
  62.6 5.9 %copy-start.23 = (bf16[128,960]{0,1:T(8,128)(2,1)S(1)}, bf16[128,960]{0,1:T(8,128)(2,1)}, u32[]{:S(2)}) copy-start(bf16[128,960]{0,1:T(8,128)(2,1)} %param.24) | copy-start | bytes 737284
  64.5 7.0 %copy-start.30 = (bf16[1,4,240,1280]{3,2,1,0:T(8,128)(2,1)}, bf16[1,4,240,1280]{3,2,1,0:T(8,128)(2,1)S(1)}, u32[]{:S(2)}) copy-start(bf16[1,4,240,1280]{3,2,1,0:T(8,128)(2,1)S(1)} %slice.140) | copy-start | bytes 7372804
  68.7 3.7 copy-start.73
  74.7 148.8 %reduce-scatter.12.cloned.1.call-start = ((), (), s32[]{:S(2)}) async-start(), calls=%async_computation.5 | async-start | bytes 786432
  74.8 20.0 %collective-permute-start.3 = (bf16[240,1280]{1,0:T(8,128)(2,1)}, bf16[240,1280]{1,0:T(8,128)(2,1)}, u32[]{:S(2)}, u32[]{:S(2)}) collective-permute-start(bf16[240,1280]{1,0:T(8,128)(2,1)} %get-tuple-element.177), channel_id=1, source_target_pairs={{0,8},{8,0},{16,24},{24,16},{1,9},{9,1},{17,25},{25,17},{2,10},{10... | collective-permute-start | bytes 1843208 | tf_op jit(solution)/shard_map/ppermute | solution.py:144
  75.4 5.7 %copy-start.61 = (f32[4,240]{1,0:T(4,128)S(1)}, f32[4,240]{1,0:T(4,128)}, u32[]{:S(2)}) copy-start(f32[4,240]{1,0:T(4,128)} %get-tuple-element.462) | copy-start | bytes 11524
  84.1 4.8 %copy-start.16 = (bf16[4,240,640]{2,1,0:T(8,128)(2,1)S(1)}, bf16[4,240,640]{2,1,0:T(8,128)(2,1)}, u32[]{:S(2)}) copy-start(bf16[4,240,640]{2,1,0:T(8,128)(2,1)} %copy-done.15) | copy-start | bytes 3686404
  85.1 16.8 %collective-permute-start.4 = (bf16[240,1280]{1,0:T(8,128)(2,1)S(1)}, bf16[240,1280]{1,0:T(8,128)(2,1)S(1)}, u32[]{:S(2)}, u32[]{:S(2)}) collective-permute-start(bf16[240,1280]{1,0:T(8,128)(2,1)S(1)} %copy-done.34), channel_id=1, source_target_pairs={{0,16},{16,0},{8,24},{24,8},{1,17},{17,1},{9,25},{25,9},{2,18},{18... | collective-permute-start | bytes 1843208 | tf_op jit(solution)/shard_map/ppermute | solution.py:144
  87.4 17.1 %collective-permute-start = (bf16[240,1280]{1,0:T(8,128)(2,1)S(1)}, bf16[240,1280]{1,0:T(8,128)(2,1)S(1)}, u32[]{:S(2)}, u32[]{:S(2)}) collective-permute-start(bf16[240,1280]{1,0:T(8,128)(2,1)S(1)} %copy-done.33), channel_id=1, source_target_pairs={{0,8},{8,0},{16,24},{24,16},{1,9},{9,1},{17,25},{25,17},{2,10},{10... | collective-permute-start | bytes 1843208 | tf_op jit(solution)/shard_map/ppermute | solution.py:144
  89.9 31.7 %collective-permute-start.1 = (bf16[240,1280]{1,0:T(8,128)(2,1)S(1)}, bf16[240,1280]{1,0:T(8,128)(2,1)S(1)}, u32[]{:S(2)}, u32[]{:S(2)}) collective-permute-start(bf16[240,1280]{1,0:T(8,128)(2,1)S(1)} %copy-done.33), channel_id=1, source_target_pairs={{0,16},{16,0},{8,24},{24,8},{1,17},{17,1},{9,25},{25,9},{2,18},{18... | collective-permute-start | bytes 1843208 | tf_op jit(solution)/shard_map/ppermute | solution.py:144
  93.2 17.6 %collective-permute-start.11 = (bf16[240,640]{1,0:T(8,128)(2,1)}, bf16[240,640]{1,0:T(8,128)(2,1)S(1)}, u32[]{:S(2)}, u32[]{:S(2)}) collective-permute-start(bf16[240,640]{1,0:T(8,128)(2,1)} %collective-permute-done.10), channel_id=1, source_target_pairs={{0,8},{8,0},{16,24},{24,16},{1,9},{9,1},{17,25},{25,17},{2,10},{10... | collective-permute-start | bytes 921608 | tf_op jit(solution)/shard_map/ppermute | solution.py:144
  94.8 26.9 %collective-permute-start.8 = (bf16[240,640]{1,0:T(8,128)(2,1)}, bf16[240,640]{1,0:T(8,128)(2,1)S(1)}, u32[]{:S(2)}, u32[]{:S(2)}) collective-permute-start(bf16[240,640]{1,0:T(8,128)(2,1)} %collective-permute-done.6), channel_id=1, source_target_pairs={{0,16},{16,0},{8,24},{24,8},{1,17},{17,1},{9,25},{25,9},{2,18},{18... | collective-permute-start | bytes 921608 | tf_op jit(solution)/shard_map/ppermute | solution.py:144
  101.9 24.1 %collective-permute-start.5 = (bf16[240,1280]{1,0:T(8,128)(2,1)S(1)}, bf16[240,1280]{1,0:T(8,128)(2,1)S(1)}, u32[]{:S(2)}, u32[]{:S(2)}) collective-permute-start(bf16[240,1280]{1,0:T(8,128)(2,1)S(1)} %collective-permute-done.4), channel_id=1, source_target_pairs={{0,8},{8,0},{16,24},{24,16},{1,9},{9,1},{17,25},{25,17},{2,10},{10... | collective-permute-start | bytes 1843208 | tf_op jit(solution)/shard_map/ppermute | solution.py:144
  104.5 29.5 %collective-permute-start.2 = (bf16[240,1280]{1,0:T(8,128)(2,1)S(1)}, bf16[240,1280]{1,0:T(8,128)(2,1)S(1)}, u32[]{:S(2)}, u32[]{:S(2)}) collective-permute-start(bf16[240,1280]{1,0:T(8,128)(2,1)S(1)} %collective-permute-done), channel_id=1, source_target_pairs={{0,16},{16,0},{8,24},{24,8},{1,17},{17,1},{9,25},{25,9},{2,18},{18... | collective-permute-start | bytes 1843208 | tf_op jit(solution)/shard_map/ppermute | solution.py:144
  126.0 8.8 %copy-start.8 = (bf16[4,240,1280]{2,1,0:T(8,128)(2,1)}, bf16[4,240,1280]{2,1,0:T(8,128)(2,1)S(1)}, u32[]{:S(2)}) copy-start(bf16[4,240,1280]{2,1,0:T(8,128)(2,1)S(1)} %bitcast_dynamic-update-slice_fusion) | copy-start | bytes 7372804
  140.8 16.4 %copy-start.35 = (f32[128,5,3,64]{0,3,2,1:T(8,128)S(1)}, f32[128,5,3,64]{0,3,2,1:T(8,128)}, u32[]{:S(2)}) copy-start(f32[128,5,3,64]{0,3,2,1:T(8,128)} %custom-call.2) | copy-start | bytes 1474564
  165.3 3.9 copy-start.36
  165.4 3.8 copy-start.51
  165.4 6.4 %copy-start.9 = (bf16[4,240,1280]{2,1,0:T(8,128)(2,1)S(1)}, bf16[4,240,1280]{2,1,0:T(8,128)(2,1)}, u32[]{:S(2)}) copy-start(bf16[4,240,1280]{2,1,0:T(8,128)(2,1)} %copy-done.8) | copy-start | bytes 7372804
  169.2 3.4 copy-start.19
  176.3 7.0 %copy-start.52 = (bf16[256,1280]{1,0:T(8,128)(2,1)}, bf16[256,1280]{1,0:T(8,128)(2,1)S(1)}, u32[]{:S(2)}) copy-start(bf16[256,1280]{1,0:T(8,128)(2,1)S(1)} %get-tuple-element.535) | copy-start | bytes 1966084
  186.8 38.8 %reduce-scatter.10.cloned.1.call-start = ((), (), s32[]{:S(2)}) async-start(), calls=%async_computation.4 | async-start | bytes 786432
  188.7 5.3 %copy-start.14 = (bf16[4,240,640]{2,1,0:T(8,128)(2,1)}, bf16[4,240,640]{2,1,0:T(8,128)(2,1)S(1)}, u32[]{:S(2)}) copy-start(bf16[4,240,640]{2,1,0:T(8,128)(2,1)S(1)} %get-tuple-element.543) | copy-start | bytes 3686404
  188.8 15.8 %copy-start.13 = (bf16[4,240,640]{2,1,0:T(8,128)(2,1)}, bf16[4,240,640]{2,1,0:T(8,128)(2,1)S(1)}, u32[]{:S(2)}) copy-start(bf16[4,240,640]{2,1,0:T(8,128)(2,1)S(1)} %get-tuple-element.542) | copy-start | bytes 3686404
  188.8 5.9 %copy-start.53 = (bf16[256,1280]{1,0:T(8,128)(2,1)S(1)}, bf16[256,1280]{1,0:T(8,128)(2,1)}, u32[]{:S(2)}) copy-start(bf16[256,1280]{1,0:T(8,128)(2,1)} %copy-done.52) | copy-start | bytes 1966084
  189.7 10.4 %collective-permute-start.22 = (bf16[240,640]{1,0:T(8,128)(2,1)}, bf16[240,640]{1,0:T(8,128)(2,1)}, u32[]{:S(2)}, u32[]{:S(2)}) collective-permute-start(bf16[240,640]{1,0:T(8,128)(2,1)} %get-tuple-element.549), channel_id=1, source_target_pairs={{0,16},{16,0},{8,24},{24,8},{1,17},{17,1},{9,25},{25,9},{2,18},{18... | collective-permute-start | bytes 921608 | tf_op jit(solution)/shard_map/ppermute | solution.py:144
  190.2 81.1 %collective-permute-start.21 = (bf16[240,640]{1,0:T(8,128)(2,1)}, bf16[240,640]{1,0:T(8,128)(2,1)}, u32[]{:S(2)}, u32[]{:S(2)}) collective-permute-start(bf16[240,640]{1,0:T(8,128)(2,1)} %get-tuple-element.548), channel_id=1, source_target_pairs={{0,16},{16,0},{8,24},{24,8},{1,17},{17,1},{9,25},{25,9},{2,18},{18... | collective-permute-start | bytes 921608 | tf_op jit(solution)/shard_map/ppermute | solution.py:144
  192.7 10.5 %collective-permute-start.19 = (bf16[240,640]{1,0:T(8,128)(2,1)}, bf16[240,640]{1,0:T(8,128)(2,1)}, u32[]{:S(2)}, u32[]{:S(2)}) collective-permute-start(bf16[240,640]{1,0:T(8,128)(2,1)} %get-tuple-element.547), channel_id=1, source_target_pairs={{0,8},{8,0},{16,24},{24,16},{1,9},{9,1},{17,25},{25,17},{2,10},{10... | collective-permute-start | bytes 921608 | tf_op jit(solution)/shard_map/ppermute | solution.py:144
  194.1 80.6 %collective-permute-start.18 = (bf16[240,640]{1,0:T(8,128)(2,1)}, bf16[240,640]{1,0:T(8,128)(2,1)}, u32[]{:S(2)}, u32[]{:S(2)}) collective-permute-start(bf16[240,640]{1,0:T(8,128)(2,1)} %get-tuple-element.546), channel_id=1, source_target_pairs={{0,8},{8,0},{16,24},{24,16},{1,9},{9,1},{17,25},{25,17},{2,10},{10... | collective-permute-start | bytes 921608 | tf_op jit(solution)/shard_map/ppermute | solution.py:144
  197.0 22.9 %collective-permute-start.16 = (bf16[240,1280]{1,0:T(8,128)(2,1)}, bf16[240,1280]{1,0:T(8,128)(2,1)}, u32[]{:S(2)}, u32[]{:S(2)}) collective-permute-start(bf16[240,1280]{1,0:T(8,128)(2,1)} %get-tuple-element.541), channel_id=1, source_target_pairs={{0,16},{16,0},{8,24},{24,8},{1,17},{17,1},{9,25},{25,9},{2,18},{18... | collective-permute-start | bytes 1843208 | tf_op jit(solution)/shard_map/ppermute | solution.py:144
  199.6 102.4 %reduce-scatter.14.cloned.1.call-start = ((), (), s32[]{:S(2)}) async-start(), calls=%async_computation.6 | async-start | bytes 1474560
  200.1 24.5 %copy-start.20 = (f32[128,960]{0,1:T(8,128)S(1)}, f32[128,960]{0,1:T(8,128)}, u32[]{:S(2)}) copy-start(f32[128,960]{0,1:T(8,128)} %copy-done.19) | copy-start | bytes 1474564
  200.2 82.8 %collective-permute-start.15 = (bf16[240,1280]{1,0:T(8,128)(2,1)}, bf16[240,1280]{1,0:T(8,128)(2,1)}, u32[]{:S(2)}, u32[]{:S(2)}) collective-permute-start(bf16[240,1280]{1,0:T(8,128)(2,1)} %get-tuple-element.540), channel_id=1, source_target_pairs={{0,16},{16,0},{8,24},{24,8},{1,17},{17,1},{9,25},{25,9},{2,18},{18... | collective-permute-start | bytes 1843208 | tf_op jit(solution)/shard_map/ppermute | solution.py:144
  203.2 65.5 %collective-permute-start.13 = (bf16[240,1280]{1,0:T(8,128)(2,1)}, bf16[240,1280]{1,0:T(8,128)(2,1)}, u32[]{:S(2)}, u32[]{:S(2)}) collective-permute-start(bf16[240,1280]{1,0:T(8,128)(2,1)} %get-tuple-element.539), channel_id=1, source_target_pairs={{0,8},{8,0},{16,24},{24,16},{1,9},{9,1},{17,25},{25,17},{2,10},{10... | collective-permute-start | bytes 1843208 | tf_op jit(solution)/shard_map/ppermute | solution.py:144
  206.4 20.4 %copy-start.50 = (bf16[128,960]{0,1:T(8,128)(2,1)S(1)}, bf16[128,960]{0,1:T(8,128)(2,1)}, u32[]{:S(2)}) copy-start(bf16[128,960]{0,1:T(8,128)(2,1)} %param.25) | copy-start | bytes 737284
  219.9 52.1 %collective-permute-start.23 = (bf16[240,640]{1,0:T(8,128)(2,1)}, bf16[240,640]{1,0:T(8,128)(2,1)}, u32[]{:S(2)}, u32[]{:S(2)}) collective-permute-start(bf16[240,640]{1,0:T(8,128)(2,1)} %fusion.68), channel_id=1, source_target_pairs={{0,8},{8,0},{16,24},{24,16},{1,9},{9,1},{17,25},{25,17},{2,10},{10... | collective-permute-start | bytes 921608 | tf_op jit(solution)/shard_map/ppermute | solution.py:144
  227.7 4.9 %copy-start.17 = (f32[128,960]{0,1:T(8,128)}, f32[128,960]{0,1:T(8,128)S(1)}, u32[]{:S(2)}) copy-start(f32[128,960]{0,1:T(8,128)S(1)} %get-tuple-element.558) | copy-start | bytes 1474564
  233.4 4.0 copy-start.1
  233.4 4.0 copy-start.62
  233.4 4.0 copy-start.64
  234.2 5.6 %copy-start = (f32[5,512,128,3]{2,1,3,0:T(8,128)}, f32[5,512,128,3]{2,1,3,0:T(8,128)S(1)}, u32[]{:S(2)}) copy-start(f32[5,512,128,3]{2,1,3,0:T(8,128)S(1)} %fusion.171) | copy-start | bytes 11796484 | tf_op jit(solution)/shard_map/while
  247.6 4.0 copy-start.1
  247.7 4.0 copy-start.62
  247.7 4.0 copy-start.64
  248.4 5.6 %copy-start = (f32[5,512,128,3]{2,1,3,0:T(8,128)}, f32[5,512,128,3]{2,1,3,0:T(8,128)S(1)}, u32[]{:S(2)}) copy-start(f32[5,512,128,3]{2,1,3,0:T(8,128)S(1)} %fusion.171) | copy-start | bytes 11796484 | tf_op jit(solution)/shard_map/while
  268.6 8.6 %collective-permute-start.20 = (bf16[240,640]{1,0:T(8,128)(2,1)S(1)}, bf16[240,640]{1,0:T(8,128)(2,1)S(1)}, u32[]{:S(2)}, u32[]{:S(2)}) collective-permute-start(bf16[240,640]{1,0:T(8,128)(2,1)S(1)} %copy-done.56), channel_id=1, source_target_pairs={{0,16},{16,0},{8,24},{24,8},{1,17},{17,1},{9,25},{25,9},{2,18},{18... | collective-permute-start | bytes 921608 | tf_op jit(solution)/shard_map/ppermute | solution.py:144
  271.3 8.0 %copy-start.65 = (bf16[960]{0:T(1024)(128)(2,1)S(1)}, bf16[960]{0:T(1024)(128)(2,1)}, u32[]{:S(2)}) copy-start(bf16[960]{0:T(1024)(128)(2,1)} %get-tuple-element.460) | copy-start | bytes 5764
  271.3 8.6 %copy-start.18 = (f32[128,960]{0,1:T(8,128)S(1)}, f32[128,960]{0,1:T(8,128)}, u32[]{:S(2)}) copy-start(f32[128,960]{0,1:T(8,128)} %copy-done.17) | copy-start | bytes 1474564
  271.3 28.9 %collective-permute-start.12 = (bf16[240,1280]{1,0:T(8,128)(2,1)}, bf16[240,1280]{1,0:T(8,128)(2,1)}, u32[]{:S(2)}, u32[]{:S(2)}) collective-permute-start(bf16[240,1280]{1,0:T(8,128)(2,1)} %get-tuple-element.538), channel_id=1, source_target_pairs={{0,8},{8,0},{16,24},{24,16},{1,9},{9,1},{17,25},{25,17},{2,10},{10... | collective-permute-start | bytes 1843208 | tf_op jit(solution)/shard_map/ppermute | solution.py:144
  272.0 26.6 %collective-permute-start.17 = (bf16[240,1280]{1,0:T(8,128)(2,1)}, bf16[240,1280]{1,0:T(8,128)(2,1)}, u32[]{:S(2)}, u32[]{:S(2)}) collective-permute-start(bf16[240,1280]{1,0:T(8,128)(2,1)} %fusion.50), channel_id=1, source_target_pairs={{0,8},{8,0},{16,24},{24,16},{1,9},{9,1},{17,25},{25,17},{2,10},{10... | collective-permute-start | bytes 1843208 | tf_op jit(solution)/shard_map/ppermute | solution.py:144
  274.7 25.5 %collective-permute-start.14 = (bf16[240,1280]{1,0:T(8,128)(2,1)}, bf16[240,1280]{1,0:T(8,128)(2,1)}, u32[]{:S(2)}, u32[]{:S(2)}) collective-permute-start(bf16[240,1280]{1,0:T(8,128)(2,1)} %fusion.53), channel_id=1, source_target_pairs={{0,16},{16,0},{8,24},{24,8},{1,17},{17,1},{9,25},{25,9},{2,18},{18... | collective-permute-start | bytes 1843208 | tf_op jit(solution)/shard_map/ppermute | solution.py:144
  278.4 4.5 %copy-start.5 = (f32[128,5,3,64]{0,3,2,1:T(8,128)S(1)}, f32[128,5,3,64]{0,3,2,1:T(8,128)}, u32[]{:S(2)}) copy-start(f32[128,5,3,64]{0,3,2,1:T(8,128)} %get-tuple-element.179) | copy-start | bytes 1474564
  283.0 18.8 %copy-start.27 = (bf16[1,240,1280]{2,1,0:T(8,128)(2,1)S(1)}, bf16[1,240,1280]{2,1,0:T(8,128)(2,1)}, u32[]{:S(2)}) copy-start(bf16[1,240,1280]{2,1,0:T(8,128)(2,1)} %maximum_bitcast_fusion.2) | copy-start | bytes 1843204
  316.9 76.2 %copy-start.28 = (f32[240,2,1280]{2,1,0:T(2,128)S(1)}, f32[240,2,1280]{2,1,0:T(2,128)}, u32[]{:S(2)}) copy-start(f32[240,2,1280]{2,1,0:T(2,128)} %param.34) | copy-start | bytes 7372804
  316.9 76.2 %copy-start.29 = (f32[240,2,1280]{2,1,0:T(2,128)S(1)}, f32[240,2,1280]{2,1,0:T(2,128)}, u32[]{:S(2)}) copy-start(f32[240,2,1280]{2,1,0:T(2,128)} %param.35) | copy-start | bytes 7372804
  403.3 3.4 copy-start.70
  403.3 4.4 %copy-start.47 = (f32[240,960]{1,0:T(8,128)S(1)}, f32[240,960]{1,0:T(8,128)}, u32[]{:S(2)}) copy-start(f32[240,960]{1,0:T(8,128)} %param.31) | copy-start | bytes 2764804
  403.3 4.4 %copy-start.48 = (f32[240,960]{1,0:T(8,128)S(1)}, f32[240,960]{1,0:T(8,128)}, u32[]{:S(2)}) copy-start(f32[240,960]{1,0:T(8,128)} %param.32) | copy-start | bytes 2764804
  410.6 3.7 copy-start.42
  (50 other events, 107.7 us)
Sparse Core Ops, SparseCore 0:
  74.8 25.2 all-gather.1
  186.9 8.2 reduce-scatter.11
  199.7 8.7 reduce-scatter.9
  268.7 32.7 reduce-scatter.13

commit v3 on v2

--- a/solution.py
+++ b/solution.py
@@ -16,7 +16,6 @@
 KEY_COLUMNS = 320
 
 
-NEGATIVE_HUGE = -1e30
 NORM_EPS = 1e-05
 ROPE_BASE = 100000.0
 BETA_ONE = 0.9
@@ -28,6 +27,7 @@
 
 MESH = pl.DeviceIdType.MESH
 BF16 = jnp.bfloat16
+NEGATIVE_HUGE = -1e30
 GAIN_ROWS = 16
 ROW_TILE = 16
 ATTN_CHUNKS = 4
@@ -136,6 +136,92 @@
     )(w, gains)
 
 
+GROUP = QUERY_HEADS // KEY_VALUE_HEADS
+SCORE_SCALE = 1.0 / math.sqrt(HEAD_SIZE)
+
+
+def heads_of(ref, group):
+    first = group * GROUP
+    return jnp.concatenate(
+        [ref[:, (first + i) * HEAD_SIZE : (first + i + 1) * HEAD_SIZE] for i in range(GROUP)], axis=0
+    )
+
+
+def side_by_side(stacked):
+    rows = stacked.shape[0] // GROUP
+    return [stacked[i * rows : (i + 1) * rows] for i in range(GROUP)]
+
+
+def visible_keys(index_ref, keys):
+    rows = index_ref.shape[0]
+    column = lax.broadcasted_iota(jnp.int32, (rows, keys), 1)
+    seen = (column >= index_ref[:, 1:2]) & (column <= index_ref[:, 0:1])
+    bias = jnp.where(seen, 0.0, NEGATIVE_HUGE)
+    return jnp.concatenate([bias] * GROUP, axis=0)
+
+
+def contract(left, right, dims):
+    return lax.dot_general(left, right, (dims, ((), ())), preferred_element_type=jnp.float32)
+
+
+def softmax_of(query, key, bias):
+    scores = contract(query, key, ((1,), (1,))) * SCORE_SCALE + bias
+    exponent = jnp.exp(scores - jnp.max(scores, axis=-1, keepdims=True))
+    return exponent * (1.0 / jnp.sum(exponent, axis=-1, keepdims=True))
+
+
+def columns_of(group):
+    return slice(group * HEAD_SIZE, (group + 1) * HEAD_SIZE)
+
+
+def attend_kernel(index_ref, query_ref, kv_ref, out_ref):
+    bias = visible_keys(index_ref, kv_ref.shape[0])
+    parts = []
+    for group in range(KEY_VALUE_HEADS):
+        key = kv_ref[:, columns_of(group)]
+        value = kv_ref[:, columns_of(KEY_VALUE_HEADS + group)]
+        probs = softmax_of(heads_of(query_ref, group), key, bias).astype(BF16)
+        parts += side_by_side(contract(probs, value, ((1,), (0,))))
+    out_ref[...] = jnp.concatenate(parts, axis=1)
+
+
+def attend_back_kernel(index_ref, query_ref, kv_ref, grad_ref, out_ref, query_grad_ref, kv_grad_ref):
+    bias = visible_keys(index_ref, kv_ref.shape[0])
+    query_parts, key_parts, value_parts = [], [], []
+    for group in range(KEY_VALUE_HEADS):
+        key = kv_ref[:, columns_of(group)]
+        value = kv_ref[:, columns_of(KEY_VALUE_HEADS + group)]
+        query = heads_of(query_ref, group)
+        grad = heads_of(grad_ref, group)
+        delta = jnp.sum(grad.astype(jnp.float32) * heads_of(out_ref, group), axis=-1, keepdims=True)
+        probs = softmax_of(query, key, bias)
+        probs_grad = contract(grad, value, ((1,), (1,)))
+        scores_grad = (probs * (probs_grad - delta)).astype(BF16)
+        query_parts += side_by_side(contract(scores_grad, key, ((1,), (0,))) * SCORE_SCALE)
+        key_parts.append(contract(scores_grad, query, ((0,), (0,))) * SCORE_SCALE)
+        value_parts.append(contract(probs.astype(BF16), grad, ((0,), (0,))))
+    query_grad_ref[...] = jnp.concatenate(query_parts, axis=1)
+    kv_grad_ref[...] = jnp.concatenate(key_parts + value_parts, axis=1).astype(BF16)
+
+
+def attention_call(kernel, name, passes, out_shape, *operands):
+    rows, keys = operands[1].shape[0], operands[2].shape[0]
+    whole = pl.BlockSpec(memory_space=pltpu.VMEM)
+    return pl.pallas_call(
+        kernel,
+        out_shape=out_shape,
+        in_specs=[whole] * len(operands),
+        out_specs=[whole] * len(out_shape),
+        compiler_params=pltpu.CompilerParams(vmem_limit_bytes=40 * 1024 * 1024),
+        cost_estimate=pl.CostEstimate(
+            flops=passes * 4 * 2 * QUERY_HEADS * rows * keys * HEAD_SIZE,
+            bytes_accessed=8 * 1024 * 1024,
+            transcendentals=QUERY_HEADS * rows * keys,
+        ),
+        name=name,
+    )(*operands)
+
+
 ACROSS = ((0, 1), (1, 0), (2, 3), (3, 2))
 ALONG = ((0, 2), (2, 0), (1, 3), (3, 1))
 
@@ -144,27 +230,37 @@
     return lax.ppermute(block, "shard", pairs)
 
 
-def plane_gather(block, x_first):
+def plane_neighbours(block):
+    return block, swap(block, ACROSS), swap(block, ALONG)
+
+
+def plane_diagonal(near, x_first):
+    return swap(near[1], ALONG) if x_first else swap(near[2], ACROSS)
+
+
+def plane_join(near, from_d):
     s, c, t, across, along, diagonal = plane_peers()
-    from_x, from_y = swap(block, ACROSS), swap(block, ALONG)
-    from_d = swap(from_x, ALONG) if x_first else swap(from_y, ACROSS)
+    block, from_x, from_y = near
     whole = jnp.zeros((4,) + block.shape, block.dtype)
     for owner, part in ((s, block), (across, from_x), (along, from_y), (diagonal, from_d)):
         whole = lax.dynamic_update_index_in_dim(whole, part, owner, 0)
     return whole
 
 
-def plane_scatter(blocks, x_first):
+def plane_first(blocks, x_first):
     s, c, t, across, along, diagonal = plane_peers()
-    near, far, straight, turn = (across, along, ACROSS, ALONG) if x_first else (along, across, ALONG, ACROSS)
+    near, far, straight = (across, along, ACROSS) if x_first else (along, across, ALONG)
 
     def part(owner):
         return lax.dynamic_index_in_dim(blocks, owner, 0, keepdims=False)
 
     first = swap(part(diagonal), straight)
-    direct = swap(part(near), straight)
-    summed = swap((part(far).astype(jnp.float32) + first.astype(jnp.float32)).astype(BF16), turn)
-    total = part(s).astype(jnp.float32) + direct.astype(jnp.float32) + summed.astype(jnp.float32)
+    summed = (part(far).astype(jnp.float32) + first.astype(jnp.float32)).astype(BF16)
+    return summed, part(near), part(s)
+
+
+def plane_scatter(summed, direct, kept):
+    total = kept.astype(jnp.float32) + direct.astype(jnp.float32) + summed.astype(jnp.float32)
     return total.astype(BF16)
 
 
@@ -441,18 +537,6 @@
         first_hat / (jnp.sqrt(second_hat) + ADAM_EPS) + decay_rate * weight
     )
     return (weight_new, first_new, second_new)
-
-
-def block_scores(query_low, key_block, row_index, row_start, block_id):
-    rows_per_block = key_block.shape[0]
-    scores = jnp.einsum(
-        "qhgd,khd->qhgk", query_low, key_block, preferred_element_type=jnp.float32
-    ) * (1.0 / math.sqrt(HEAD_SIZE))
-    column_index = block_id * rows_per_block + jnp.arange(rows_per_block, dtype=jnp.int32)
-    visible = (column_index[None, :] >= row_start[:, None]) & (
-        column_index[None, :] <= row_index[:, None]
-    )
-    return (scores, visible[:, None, None, :])
 
 
 def shards(
@@ -497,16 +581,20 @@
         gathered = gathered.reshape(2, MODEL_WIDTH, width)
         qkv_mat = jnp.concatenate([gathered[0], gathered[1, :, :KEY_COLUMNS]], axis=1)
         out_mat = gathered[1, :, KEY_COLUMNS:]
-        gate_mat = plane_gather(gate_low, True).reshape(MODEL_WIDTH, hidden_units)
-        up_mat = plane_gather(up_low, False).reshape(MODEL_WIDTH, hidden_units)
         middle_column = hidden_units // 2
-        down_mat_t = jnp.concatenate(
-            [
-                plane_gather(down_low_t[:, :middle_column], True),
-                plane_gather(down_low_t[:, middle_column:], False),
-            ],
-            axis=2,
-        ).reshape(MODEL_WIDTH, hidden_units)
+        neighbours = [
+            plane_neighbours(block)
+            for block in (
+                gate_low,
+                up_low,
+                down_low_t[:, :middle_column],
+                down_low_t[:, middle_column:],
+            )
+        ]
+        diagonals = [
+            plane_diagonal(near, x_first)
+            for near, x_first in zip(neighbours, (True, False, True, False))
+        ]
         gains_all = gains_parts[:, :2].transpose(1, 0, 2).reshape(2, MODEL_WIDTH)
     else:
         qkv_mat = lax.all_gather(qkv_low, "shard", axis=0, tiled=True)
@@ -550,47 +638,28 @@
     )
     key_value_whole = lax.all_gather(kv_local, ("context", "tensor"), axis=0, tiled=True)
     total_keys = key_value_whole.shape[0]
-    rows_per_block = min(512, total_keys)
-    count_of_blocks = total_keys // rows_per_block
-    key_value_blocks = key_value_whole.reshape(
-        count_of_blocks, rows_per_block, 2, KEY_VALUE_HEADS, HEAD_SIZE
-    )
-    block_numbers = jnp.arange(count_of_blocks, dtype=jnp.int32)
-
-    def scan_total(scan_carry, scan_item):
-        running, running_sum = scan_carry
-        block_id, kv_block = scan_item
-        scores, visible = block_scores(query_low, kv_block[:, 0], row_index, row_start, block_id)
-        masked = jnp.where(visible, scores, NEGATIVE_HUGE)
-        highest = jnp.maximum(running, jnp.max(masked, axis=-1))
-        exponent = jnp.where(visible, jnp.exp(masked - highest[..., None]), 0.0)
-        running_sum = running_sum * jnp.exp(running - highest) + jnp.sum(exponent, axis=-1)
-        return ((highest, running_sum), None)
-
-    latest_start = jnp.full((shard_rows, KEY_VALUE_HEADS, pack_groups), NEGATIVE_HUGE, jnp.float32)
-    (running, running_sum), unused = lax.scan(
-        scan_total, (latest_start, jnp.zeros_like(latest_start)), (block_numbers, key_value_blocks)
-    )
-    log_total = running + jnp.log(running_sum)
-
-    def sweep_output(accumulated, scan_item):
-        block_id, kv_block = scan_item
-        scores, visible = block_scores(query_low, kv_block[:, 0], row_index, row_start, block_id)
-        softmax_rows = jnp.where(visible, jnp.exp(scores - log_total[..., None]), 0.0)
-        accumulated = accumulated + jnp.einsum(
-            "qhgk,khd->qhgd",
-            softmax_rows.astype(jnp.bfloat16),
-            kv_block[:, 1],
-            preferred_element_type=jnp.float32,
-        )
-        return (accumulated, None)
-
-    attended_heads, unused = lax.scan(
-        sweep_output,
-        jnp.zeros((shard_rows, KEY_VALUE_HEADS, pack_groups, HEAD_SIZE), jnp.float32),
-        (block_numbers, key_value_blocks),
-    )
-    attended_low = attended_heads.reshape(shard_rows, MODEL_WIDTH).astype(jnp.bfloat16)
+    row_span = jnp.stack([row_index, row_start], axis=1)
+    query_flat = query_low.reshape(shard_rows, MODEL_WIDTH)
+    (attended_heads,) = attention_call(
+        attend_kernel,
+        "attend",
+        2,
+        (jax.ShapeDtypeStruct((shard_rows, MODEL_WIDTH), jnp.float32),),
+        row_span,
+        query_flat,
+        key_value_whole,
+    )
+    if plane:
+        attended_heads, diagonals = lax.optimization_barrier((attended_heads, diagonals))
+        gate_mat, up_mat, down_left, down_right = (
+            plane_join(near, far) for near, far in zip(neighbours, diagonals)
+        )
+        gate_mat = gate_mat.reshape(MODEL_WIDTH, hidden_units)
+        up_mat = up_mat.reshape(MODEL_WIDTH, hidden_units)
+        down_mat_t = jnp.concatenate([down_left, down_right], axis=2).reshape(
+            MODEL_WIDTH, hidden_units
+        )
+    attended_low = attended_heads.astype(jnp.bfloat16)
     branch = jnp.dot(attended_low, out_mat, preferred_element_type=jnp.float32)
     hidden_state = inputs + branch
     normed_two, inverse_two = rms_norm(hidden_state, gains_full[1])
@@ -617,6 +686,22 @@
     upward_grad = jnp.einsum(
         "td,tf->df", ffn_rows, upward_grad_low, preferred_element_type=jnp.float32
     )
+    if plane:
+        rows = MODEL_WIDTH // 4
+        gate_blocks, up_blocks, down_blocks = (
+            part.astype(jnp.bfloat16).reshape(4, rows, hidden_units)
+            for part in (gate_grad, upward_grad, down_grad_t)
+        )
+        down_left, down_right = down_blocks[:, :, :middle_column], down_blocks[:, :, middle_column:]
+        scatter_parts = [
+            plane_first(blocks, x_first)
+            for blocks, x_first in (
+                (gate_blocks, True),
+                (up_blocks, False),
+                (down_left, True),
+                (down_right, False),
+            )
+        ]
     normed_part = jnp.einsum(
         "tf,df->td", gate_grad_low, gate_mat, preferred_element_type=jnp.float32
     ) + jnp.einsum("tf,df->td", upward_grad_low, up_mat, preferred_element_type=jnp.float32)
@@ -632,45 +717,35 @@
     attended_gradient = jnp.einsum(
         "td,kd->tk", branch_low, out_mat, preferred_element_type=jnp.float32
     )
-    attended_gradient_narrow = attended_gradient.astype(jnp.bfloat16).reshape(
-        shard_rows, KEY_VALUE_HEADS, pack_groups, HEAD_SIZE
-    )
-    delta_rows = jnp.sum(attended_gradient_narrow.astype(jnp.float32) * attended_heads, axis=-1)
-
-    def sweep_backward(query_grad, scan_item):
-        block_id, kv_block = scan_item
-        scores, visible = block_scores(query_low, kv_block[:, 0], row_index, row_start, block_id)
-        softmax_rows = jnp.where(visible, jnp.exp(scores - log_total[..., None]), 0.0)
-        softmax_low = softmax_rows.astype(jnp.bfloat16)
-        probs_grad = jnp.einsum(
-            "qhgd,khd->qhgk",
-            attended_gradient_narrow,
-            kv_block[:, 1],
-            preferred_element_type=jnp.float32,
-        )
-        scores_low = (softmax_rows * (probs_grad - delta_rows[..., None])).astype(jnp.bfloat16)
-        query_grad = query_grad + jnp.einsum(
-            "qhgk,khd->qhgd", scores_low, kv_block[:, 0], preferred_element_type=jnp.float32
-        ) * (1.0 / math.sqrt(HEAD_SIZE))
-        key_grad = jnp.einsum(
-            "qhgk,qhgd->khd", scores_low, query_low, preferred_element_type=jnp.float32
-        ) * (1.0 / math.sqrt(HEAD_SIZE))
-        value_grad = jnp.einsum(
-            "qhgk,qhgd->khd",
-            softmax_low,
-            attended_gradient_narrow,
-            preferred_element_type=jnp.float32,
-        )
-        return (query_grad, jnp.stack([key_grad, value_grad], axis=1))
-
-    query_grad, kv_terms = lax.scan(
-        sweep_backward,
-        jnp.zeros((shard_rows, KEY_VALUE_HEADS, pack_groups, HEAD_SIZE), jnp.float32),
-        (block_numbers, key_value_blocks),
-    )
-    kv_terms = kv_terms.reshape(total_keys, 2 * KEY_COLUMNS)
+    attended_gradient_narrow = attended_gradient.astype(jnp.bfloat16)
+    if plane:
+        attended_gradient_narrow, scatter_parts = lax.optimization_barrier(
+            (attended_gradient_narrow, scatter_parts)
+        )
+        turns = ((ACROSS, ALONG), (ALONG, ACROSS), (ACROSS, ALONG), (ALONG, ACROSS))
+        directs = [swap(parts[1], straight) for parts, (straight, turn) in zip(scatter_parts, turns)]
+    query_grad, kv_terms = attention_call(
+        attend_back_kernel,
+        "attend_back",
+        5,
+        (
+            jax.ShapeDtypeStruct((shard_rows, MODEL_WIDTH), jnp.float32),
+            jax.ShapeDtypeStruct((total_keys, 2 * KEY_COLUMNS), jnp.bfloat16),
+        ),
+        row_span,
+        query_flat,
+        key_value_whole,
+        attended_gradient_narrow,
+        attended_heads,
+    )
+    if plane:
+        kv_terms, query_grad, directs = lax.optimization_barrier((kv_terms, query_grad, directs))
+        scattered = [
+            plane_scatter(swap(parts[0], turn), direct, parts[2])
+            for parts, direct, (straight, turn) in zip(scatter_parts, directs, turns)
+        ]
     key_value_gradient = lax.psum_scatter(
-        kv_terms.astype(jnp.bfloat16), ("context", "tensor"), scatter_dimension=0, tiled=True
+        kv_terms, ("context", "tensor"), scatter_dimension=0, tiled=True
     ).astype(jnp.float32)
     key_back = unrotate(
         key_value_gradient[:, :KEY_COLUMNS].reshape(shard_rows, KEY_VALUE_HEADS, HEAD_SIZE),
@@ -704,19 +779,8 @@
         )
         gain_rows = jnp.stack([gain_rows, jnp.zeros_like(gain_rows)])
         attn_grad = jnp.concatenate([attn_grad, gain_rows], axis=2)
-        gate_blocks, up_blocks, down_blocks = (
-            part.astype(jnp.bfloat16).reshape(4, rows, width)
-            for part in (gate_grad, upward_grad, down_grad_t)
-        )
-        down_part = jnp.concatenate(
-            [
-                plane_scatter(down_blocks[:, :, :middle_column], True),
-                plane_scatter(down_blocks[:, :, middle_column:], False),
-            ],
-            axis=1,
-        )
         ffn_grad = jnp.stack(
-            [plane_scatter(gate_blocks, True), plane_scatter(up_blocks, False), down_part]
+            [scattered[0], scattered[1], jnp.concatenate([scattered[2], scattered[3]], axis=1)]
         )
         attn_red, ffn_red = reduce_grads(lax.axis_size("context"), attn_grad, ffn_grad)
         gains_red = attn_red[0, rows : rows + 2, :rows].astype(jnp.float32)

time: 430 us -> 382 us (0.89)
  matrix products: 61.4 us -> 28.5 us
  local copies, waits for them, and re-layouts: 78.4 us -> 62.3 us
  other arithmetic: 56.1 us -> 41.7 us
  Pallas kernels: 119 us -> 130 us
  waiting for transfers between devices: 59.5 us -> 69.1 us
  loops' own time: 4.68 us -> 0 us
    dot_general x14 -> x0, matrix products: 27.6 us -> none  [the longest x4 6.86 us: block_scores(): jnp.einsum('qhgd,khd->qhgk', query_low, key_block, preferred_element_type...]
    pallas_call x0 -> x2, Pallas kernels: none -> 13.3 us  [attention_call(): pl.pallas_call(kernel, out_shape=out_shape, in_specs=[whole] * len(operan...]
    reduce_scatter x0 -> x1, waiting for transfers between devices: none -> 9.58 us  [shards(): lax.psum_scatter(kv_terms, ('context', 'tensor'), scatter_dimension=0, ti...]
    reduce_sum x3 -> x0, other arithmetic: 7.69 us -> none  [the longest x2 6.09 us: scan_total(): jnp.sum(exponent, axis=-1)]
    dynamic_update_slice x16, local copies, waits for them, and re-layouts: 12.8 us -> 19.4 us  [plane_join(): whole = lax.dynamic_update_index_in_dim(whole, part, owner, 0)]
    dynamic_slice x6 -> x0, local copies, waits for them, and re-layouts: 5.92 us -> none  [shards(): lax.scan(scan_total, (latest_start, jnp.zeros_like(latest_start)), (block...]
    another operation x3 -> x0, loops' own time: 4.68 us -> none  [the longest x1 1.86 us: shards(): lax.scan(sweep_backward, jnp.zeros((shard_rows, KEY_VALUE_HEADS, pack_gro...]
    and x6 -> x0, other arithmetic: 4.47 us -> none  [block_scores(): (column_index[None, :] >= row_start[:, None]) & (column_index[None, :] <=...]
  transfers between devices with their start and end apart: 28 -> 28, of which waited for: 9 -> 10; matrix products, arithmetic and copies ran while one was open for 23% -> 14% of each run, Pallas kernels for 0% -> 4%
where the time goes in v3:
time: 382 us; the launch traced here: 376 us
  Pallas kernels  130 us (34%)
  waiting for transfers between devices  69.1 us (18%)
  local copies, waits for them, and re-layouts  62.3 us (16%)
  other arithmetic  41.7 us (11%)
  matrix products  28.5 us (7%)
  starting transfers between devices  23.3 us (6%)
  between operations  15.5 us (4%)
  blocking collectives  5.4 us (1%)
    pallas_call x1, Pallas kernels, reduce_grads(): pl.pallas_call(functools.partial(reduce_kernel, n, tuple(chunks)), out_sh...  73.9 us
    ppermute x24, waiting for transfers between devices, swap(): return lax.ppermute(block, 'shard', pairs)  59.4 us
    pallas_call x1, Pallas kernels, gather_weights(): pl.pallas_call(gather_kernel, out_shape=(jax.ShapeDtypeStruct((blocks, 4,...  42.9 us
    unnamed x165, local copies, waits for them, and re-layouts  26.1 us
    ppermute x24, starting transfers between devices, swap(): return lax.ppermute(block, 'shard', pairs)  23 us
    dynamic_update_slice x16, local copies, waits for them, and re-layouts, plane_join(): whole = lax.dynamic_update_index_in_dim(whole, part, owner, 0)  19.4 us
    pallas_call x2, Pallas kernels, attention_call(): pl.pallas_call(kernel, out_shape=out_shape, in_specs=[whole] * len(operan...  13.3 us
    sub x5, other arithmetic, adam_step(): weight - learning * (first_hat / (jnp.sqrt(second_hat) + ADAM_EPS) + deca...  10.6 us
  transfers between devices with their start and end apart: 28, of which 10 were waited for; matrix products, arithmetic and copies ran while one was open for 14% of the time, Pallas kernels for 4%

profile of v3, /device:TPU:0, one launch (start us, length us, event | category | flops | bytes accessed | tf_op | source)
XLA Modules:
  0.0 375.9 jit_solution(15358909367856558909)
XLA Ops:
  9.6 1.7 copy-done.5
  14.5 42.9 %gather_weights.1 = (bf16[2,4,240,1280]{3,2,1,0:T(8,128)(2,1)}, bf16[4,16,240]{2,1,0:T(8,128)(2,1)}) custom-call(bf16[2,240,1280]{2,1,0:T(8,128)(2,1)} %pad_maximum_fusion.6.w, bf16[16,240]{1,0:T(8,128)(2,1)} %pad.9.gains), custom_call_target="tpu_custom_call" | custom-call | tf_op jit(solution)/shard_map/gather_weights/pallas_call | solution.py:121
  59.4 1.5 collective-permute-start.10
  60.9 1.5 collective-permute-start.4
  63.9 1.9 slice.124
  65.8 1.8 slice_bitcast_fusion.7
  67.6 1.6 fusion.6
  71.1 1.6 broadcast.125.clone.1
  72.7 1.9 bitcast_dynamic-update-slice_fusion.7
  77.5 2.7 all_gather.11
  80.7 1.7 bitcast_dynamic-update-slice_fusion.10
  82.4 1.6 collective-permute-start.9
  85.0 1.6 collective-permute-start.2
  86.6 1.7 bitcast_dynamic-update-slice_fusion.9
  89.7 7.6 %collective-permute-done = bf16[240,1280]{1,0:T(8,128)(2,1)} collective-permute-done((bf16[240,1280]{1,0:T(8,128)(2,1)}, bf16[240,1280]{1,0:T(8,128)(2,1)}, u32[]{:S(2)}, u32[]{:S(2)}) %collective-permute-start) | collective-permute-done | bytes 614432 | tf_op jit(solution)/shard_map/ppermute | solution.py:230
  97.3 1.5 collective-permute-start.5
  98.8 1.9 bitcast_dynamic-update-slice_fusion.6
  100.7 9.6 %collective-permute-done.9 = bf16[240,1280]{1,0:T(8,128)(2,1)S(1)} collective-permute-done((bf16[240,1280]{1,0:T(8,128)(2,1)S(1)}, bf16[240,1280]{1,0:T(8,128)(2,1)S(1)}, u32[]{:S(2)}, u32[]{:S(2)}) %collective-permute-start.9) | collective-permute-done | bytes 614432 | tf_op jit(solution)/shard_map/ppermute | solution.py:230
  110.3 1.5 collective-permute-start.1
  113.5 1.9 bitcast_dynamic-update-slice_fusion.5
  115.4 1.3 copy-done
  116.7 4.6 %attend.1.out_ref = f32[128,960]{1,0:T(8,128)S(1)} custom-call(s32[128,2]{1,0:T(8,128)S(1)} %copy.115.index_ref, bf16[128,960]{1,0:T(8,128)(2,1)S(1)} %copy.116.query_ref, bf16[1024,640]{1,0:T(8,128)(2,1)S(1)} %copy-done), custom_call_target="tpu_custom_call" | custom-call | flops 2013265920 | bytes 8388608 | tf_op jit(solution)/shard_map/attend/pallas_call | solution.py:210
  121.3 3.6 collective-permute-done.1
  124.9 4.5 %collective-permute-done.3 = bf16[240,1280]{1,0:T(8,128)(2,1)} collective-permute-done((bf16[240,1280]{1,0:T(8,128)(2,1)}, bf16[240,1280]{1,0:T(8,128)(2,1)}, u32[]{:S(2)}, u32[]{:S(2)}) %collective-permute-start.3) | collective-permute-done | bytes 614432 | tf_op jit(solution)/shard_map/ppermute | solution.py:230
  129.4 3.5 multiply_reduce_fusion
  133.9 2.7 all_gather.10
  139.0 2.4 bitcast_dynamic-update-slice_fusion.4
  144.5 3.9 %multiply_convert_fusion.1 = (bf16[256,1280]{1,0:T(8,128)(2,1)S(1)}, bf16[256,1280]{1,0:T(8,128)(2,1)S(1)}, bf16[256,1280]{1,0:T(8,128)(2,1)}) fusion(f32[256,1280]{1,0:T(8,128)S(1)} %convolution_bitcast_fusion, f32[256,1280]{1,0:T(8,128)S(1)} %fusion.67, bf16[256,960]{0,1:T(8,128)(2,1)S(1)} %all_gather.10, bf16[960,1280]{1,0:T(8,128)(2,1)} %bitcast.22), kind=kOutput, calls=%fused_computation.38 | convolution fusion | flops 634060800 | bytes 7536640 | tf_op jit(solution)/shard_map/dot_general | solution.py:668
  150.1 3.3 fusion.12
  153.4 2.0 copy.137
  156.8 1.5 collective-permute-start.13
  162.1 1.6 convolution_convert_fusion.5
  167.5 2.0 copy.135
  169.5 1.4 collective-permute-start.12
  171.2 8.4 %collective-permute-done.15 = bf16[240,640]{1,0:T(8,128)(2,1)} collective-permute-done((bf16[240,640]{1,0:T(8,128)(2,1)}, bf16[240,640]{1,0:T(8,128)(2,1)}, u32[]{:S(2)}, u32[]{:S(2)}) %collective-permute-start.15) | collective-permute-done | bytes 307232 | tf_op jit(solution)/shard_map/ppermute | solution.py:230
  179.6 1.9 fusion.28
  181.4 1.9 fusion.29
  183.3 2.1 fusion.14
  185.4 2.7 collective-permute-done.12
  188.1 2.2 fusion.15
  191.5 1.4 fusion.35
  195.1 2.8 fusion.19.grad_ref
  199.2 1.6 collective-permute-start.18
  202.4 8.7 %attend_back.1 = (f32[128,960]{1,0:T(8,128)S(1)}, bf16[1024,640]{1,0:T(8,128)(2,1)}) custom-call(s32[128,2]{1,0:T(8,128)S(1)} %copy.115.index_ref, bf16[128,960]{1,0:T(8,128)(2,1)S(1)} %copy.116.query_ref, bf16[1024,640]{1,0:T(8,128)(2,1)S(1)} %copy-done.1, bf16[128,960]{1,0:T(8,128)(2,1)S(1)} %fusion.19.grad_ref, f32[128,960]{1,0:T(8,128)S(1)} %attend.1.out_ref), custom_call_target="tpu_custom_call" | custom-call | flops 5033164800 | bytes 8388608 | tf_op jit(solution)/shard_map/attend_back/pallas_call | solution.py:210
  211.2 10.1 %collective-permute-done.18 = bf16[240,640]{1,0:T(8,128)(2,1)S(1)} collective-permute-done((bf16[240,640]{1,0:T(8,128)(2,1)S(1)}, bf16[240,640]{1,0:T(8,128)(2,1)S(1)}, u32[]{:S(2)}, u32[]{:S(2)}) %collective-permute-start.18) | collective-permute-done | bytes 307232 | tf_op jit(solution)/shard_map/ppermute | solution.py:230
  222.6 2.0 convolution_convert_fusion.4
  227.7 1.3 add_convert_fusion.2
  229.0 6.0 %collective-permute-done.22 = bf16[240,640]{1,0:T(8,128)(2,1)} collective-permute-done((bf16[240,640]{1,0:T(8,128)(2,1)S(1)}, bf16[240,640]{1,0:T(8,128)(2,1)}, u32[]{:S(2)}, u32[]{:S(2)}) %collective-permute-start.22) | collective-permute-done | bytes 307232 | tf_op jit(solution)/shard_map/ppermute | solution.py:230
  236.2 6.9 %collective-permute-done.20 = bf16[240,1280]{1,0:T(8,128)(2,1)} collective-permute-done((bf16[240,1280]{1,0:T(8,128)(2,1)}, bf16[240,1280]{1,0:T(8,128)(2,1)}, u32[]{:S(2)}, u32[]{:S(2)}) %collective-permute-start.20) | collective-permute-done | bytes 614432 | tf_op jit(solution)/shard_map/ppermute | solution.py:230
  243.1 1.3 fusion.26
  244.5 1.3 fusion.27
  246.0 9.6 %reduce-scatter.8.cloned.1.call-done = bf16[128,640]{1,0:T(8,128)(2,1)} async-done(((bf16[1024,640]{1,0:T(8,128)(2,1)}), bf16[128,640]{1,0:T(8,128)(2,1)}) %reduce-scatter.8.cloned.1.call-update) | async-done | bytes 163856 | tf_op jit(solution)/shard_map/reduce_scatter | solution.py:747
  257.0 3.7 fusion.41
  261.8 1.6 slice.177
  263.6 6.9 %fusion.1.attn = bf16[2,4,256,1280]{3,2,1,0:T(8,128)(2,1)} fusion(bf16[1,4,16,1280]{3,2,1,0:T(8,128)(2,1)S(1)} %pad_bitcast_fusion, bf16[1,4,240,960]{3,2,1,0:T(8,128)(2,1)} %bitcast.193, bf16[1,4,240,320]{3,2,1,0:T(8,128)(2,1)S(1)} %bitcast.197, bf16[1,4,240,1280]{3,2,1,0:T(8,128)(2,1)} %bitcast.190), kind=kLoop, calls=%fused_computation.2 | loop fusion | flops 26214400 | bytes 10321920 | tf_op jit(solution)/shard_map/concatenate | solution.py:781
  270.4 73.9 %reduce_grads.1 = (bf16[2,256,1280]{2,1,0:T(8,128)(2,1)S(1)}, bf16[3,240,1280]{2,1,0:T(8,128)(2,1)S(1)}) custom-call(bf16[2,4,256,1280]{3,2,1,0:T(8,128)(2,1)} %fusion.1.attn, bf16[3,240,1280]{2,1,0:T(8,128)(2,1)S(1)} %pad_maximum_fusion.5.ffn), custom_call_target="tpu_custom_call" | custom-call | tf_op jit(solution)/shard_map/reduce_grads/pallas_call | solution.py:456
  344.5 1.5 copy-done.6
  346.0 2.0 multiply_subtract_fusion
  348.0 3.3 copy.130
  351.3 3.3 copy.131
  354.7 3.3 copy.132
  359.7 2.5 add_subtract_fusion
  362.2 2.5 multiply_subtract_fusion.2
  365.9 3.1 multiply_subtract_fusion.1
  (286 shorter events, 52.6 us)
Async XLA Ops:
  7.2 108.2 %all-gather.2.cloned.1.call-start = ((), (), s32[]{:S(2)}) async-start(), calls=%async_computation.3 | async-start | bytes 1474560 | tf_op jit(solution)/shard_map/all_gather | solution.py:639
  9.5 65.2 %copy-start.12 = (bf16[240,1280]{1,0:T(8,128)(2,1)}, bf16[240,1280]{1,0:T(8,128)(2,1)S(1)}, u32[]{:S(2)}) copy-start(bf16[240,1280]{1,0:T(8,128)(2,1)S(1)} %convert_bitcast_fusion.1) | copy-start | bytes 1843204
  14.5 48.4 %copy-start.11 = (bf16[128,960]{0,1:T(8,128)(2,1)S(1)}, bf16[128,960]{0,1:T(8,128)(2,1)}, u32[]{:S(2)}) copy-start(bf16[128,960]{0,1:T(8,128)(2,1)} %param.18) | copy-start | bytes 737284
  58.3 22.0 %collective-permute-start.11 = (bf16[240,640]{1,0:T(8,128)(2,1)}, bf16[240,640]{1,0:T(8,128)(2,1)}, u32[]{:S(2)}, u32[]{:S(2)}) collective-permute-start(bf16[240,640]{1,0:T(8,128)(2,1)} %get-tuple-element.214), channel_id=1, source_target_pairs={{0,8},{8,0},{16,24},{24,16},{1,9},{9,1},{17,25},{25,17},{2,10},{10... | collective-permute-start | bytes 921608 | tf_op jit(solution)/shard_map/ppermute | solution.py:230
  58.8 26.2 %collective-permute-start.6 = (bf16[240,640]{1,0:T(8,128)(2,1)}, bf16[240,640]{1,0:T(8,128)(2,1)}, u32[]{:S(2)}, u32[]{:S(2)}) collective-permute-start(bf16[240,640]{1,0:T(8,128)(2,1)} %get-tuple-element.214), channel_id=1, source_target_pairs={{0,16},{16,0},{8,24},{24,8},{1,17},{17,1},{9,25},{25,9},{2,18},{18... | collective-permute-start | bytes 921608 | tf_op jit(solution)/shard_map/ppermute | solution.py:230
  59.4 28.9 %collective-permute-start.10 = (bf16[240,640]{1,0:T(8,128)(2,1)}, bf16[240,640]{1,0:T(8,128)(2,1)}, u32[]{:S(2)}, u32[]{:S(2)}) collective-permute-start(bf16[240,640]{1,0:T(8,128)(2,1)} %get-tuple-element.215), channel_id=1, source_target_pairs={{0,16},{16,0},{8,24},{24,8},{1,17},{17,1},{9,25},{25,9},{2,18},{18... | collective-permute-start | bytes 921608 | tf_op jit(solution)/shard_map/ppermute | solution.py:230
  60.9 21.5 %collective-permute-start.4 = (bf16[240,640]{1,0:T(8,128)(2,1)}, bf16[240,640]{1,0:T(8,128)(2,1)}, u32[]{:S(2)}, u32[]{:S(2)}) collective-permute-start(bf16[240,640]{1,0:T(8,128)(2,1)} %get-tuple-element.215), channel_id=1, source_target_pairs={{0,8},{8,0},{16,24},{24,16},{1,9},{9,1},{17,25},{25,17},{2,10},{10... | collective-permute-start | bytes 921608 | tf_op jit(solution)/shard_map/ppermute | solution.py:230
  62.3 51.1 %collective-permute-start.8 = (bf16[240,1280]{1,0:T(8,128)(2,1)}, bf16[240,1280]{1,0:T(8,128)(2,1)}, u32[]{:S(2)}, u32[]{:S(2)}) collective-permute-start(bf16[240,1280]{1,0:T(8,128)(2,1)} %get-tuple-element.56), channel_id=1, source_target_pairs={{0,16},{16,0},{8,24},{24,8},{1,17},{17,1},{9,25},{25,9},{2,18},{18... | collective-permute-start | bytes 1843208 | tf_op jit(solution)/shard_map/ppermute | solution.py:230
  63.0 4.5 %copy-start.71 = (f32[128]{0:T(128)}, f32[128]{0:T(128)S(1)}, u32[]{:S(2)}) copy-start(f32[128]{0:T(128)S(1)} %add_rsqrt_fusion.1) | copy-start | bytes 1540
  69.8 5.7 %copy-start.55 = (f32[128,32]{0,1:T(8,128)}, f32[128,32]{0,1:T(8,128)S(1)}, u32[]{:S(2)}) copy-start(f32[128,32]{0,1:T(8,128)S(1)} %get-tuple-element.228) | copy-start | bytes 49156
  69.9 5.7 %copy-start.57 = (f32[128,32]{0,1:T(8,128)}, f32[128,32]{0,1:T(8,128)S(1)}, u32[]{:S(2)}) copy-start(f32[128,32]{0,1:T(8,128)S(1)} %get-tuple-element.229) | copy-start | bytes 49156
  70.8 119.5 %reduce-scatter.12.cloned.1.call-start = ((), (), s32[]{:S(2)}) async-start(), calls=%async_computation.6 | async-start | bytes 786432
  77.4 5.0 %copy-start.30 = (bf16[240,1280]{1,0:T(8,128)(2,1)S(1)}, bf16[240,1280]{1,0:T(8,128)(2,1)}, u32[]{:S(2)}) copy-start(bf16[240,1280]{1,0:T(8,128)(2,1)} %get-tuple-element.57) | copy-start | bytes 1843204
  80.3 17.0 %collective-permute-start = (bf16[240,1280]{1,0:T(8,128)(2,1)}, bf16[240,1280]{1,0:T(8,128)(2,1)}, u32[]{:S(2)}, u32[]{:S(2)}) collective-permute-start(bf16[240,1280]{1,0:T(8,128)(2,1)} %get-tuple-element.56), channel_id=1, source_target_pairs={{0,8},{8,0},{16,24},{24,16},{1,9},{9,1},{17,25},{25,17},{2,10},{10... | collective-permute-start | bytes 1843208 | tf_op jit(solution)/shard_map/ppermute | solution.py:230
  82.4 28.0 %collective-permute-start.9 = (bf16[240,1280]{1,0:T(8,128)(2,1)S(1)}, bf16[240,1280]{1,0:T(8,128)(2,1)S(1)}, u32[]{:S(2)}, u32[]{:S(2)}) collective-permute-start(bf16[240,1280]{1,0:T(8,128)(2,1)S(1)} %copy-done.30), channel_id=1, source_target_pairs={{0,8},{8,0},{16,24},{24,16},{1,9},{9,1},{17,25},{25,17},{2,10},{10... | collective-permute-start | bytes 1843208 | tf_op jit(solution)/shard_map/ppermute | solution.py:230
  85.0 26.8 %collective-permute-start.2 = (bf16[240,1280]{1,0:T(8,128)(2,1)S(1)}, bf16[240,1280]{1,0:T(8,128)(2,1)}, u32[]{:S(2)}, u32[]{:S(2)}) collective-permute-start(bf16[240,1280]{1,0:T(8,128)(2,1)S(1)} %copy-done.30), channel_id=1, source_target_pairs={{0,16},{16,0},{8,24},{24,8},{1,17},{17,1},{9,25},{25,9},{2,18},{18... | collective-permute-start | bytes 1843208 | tf_op jit(solution)/shard_map/ppermute | solution.py:230
  88.3 33.0 %collective-permute-start.7 = (bf16[240,640]{1,0:T(8,128)(2,1)}, bf16[240,640]{1,0:T(8,128)(2,1)}, u32[]{:S(2)}, u32[]{:S(2)}) collective-permute-start(bf16[240,640]{1,0:T(8,128)(2,1)} %collective-permute-done.6), channel_id=1, source_target_pairs={{0,8},{8,0},{16,24},{24,16},{1,9},{9,1},{17,25},{25,17},{2,10},{10... | collective-permute-start | bytes 921608 | tf_op jit(solution)/shard_map/ppermute | solution.py:230
  89.7 23.7 %copy-start.18 = (bf16[4,240,640]{2,1,0:T(8,128)(2,1)}, bf16[4,240,640]{2,1,0:T(8,128)(2,1)S(1)}, u32[]{:S(2)}) copy-start(bf16[4,240,640]{2,1,0:T(8,128)(2,1)S(1)} %bitcast_dynamic-update-slice_fusion.13) | copy-start | bytes 3686404
  97.3 24.0 %collective-permute-start.5 = (bf16[240,640]{1,0:T(8,128)(2,1)}, bf16[240,640]{1,0:T(8,128)(2,1)}, u32[]{:S(2)}, u32[]{:S(2)}) collective-permute-start(bf16[240,640]{1,0:T(8,128)(2,1)} %collective-permute-done.4), channel_id=1, source_target_pairs={{0,16},{16,0},{8,24},{24,8},{1,17},{17,1},{9,25},{25,9},{2,18},{18... | collective-permute-start | bytes 921608 | tf_op jit(solution)/shard_map/ppermute | solution.py:230
  110.3 14.6 %collective-permute-start.1 = (bf16[240,1280]{1,0:T(8,128)(2,1)}, bf16[240,1280]{1,0:T(8,128)(2,1)}, u32[]{:S(2)}, u32[]{:S(2)}) collective-permute-start(bf16[240,1280]{1,0:T(8,128)(2,1)} %collective-permute-done), channel_id=1, source_target_pairs={{0,16},{16,0},{8,24},{24,8},{1,17},{17,1},{9,25},{25,9},{2,18},{18... | collective-permute-start | bytes 1843208 | tf_op jit(solution)/shard_map/ppermute | solution.py:230
  111.9 17.5 %collective-permute-start.3 = (bf16[240,1280]{1,0:T(8,128)(2,1)}, bf16[240,1280]{1,0:T(8,128)(2,1)}, u32[]{:S(2)}, u32[]{:S(2)}) collective-permute-start(bf16[240,1280]{1,0:T(8,128)(2,1)} %collective-permute-done.2), channel_id=1, source_target_pairs={{0,8},{8,0},{16,24},{24,16},{1,9},{9,1},{17,25},{25,17},{2,10},{10... | collective-permute-start | bytes 1843208 | tf_op jit(solution)/shard_map/ppermute | solution.py:230
  121.3 12.4 %copy-start.68 = (f32[960]{0:T(1024)S(1)}, f32[960]{0:T(1024)}, u32[]{:S(2)}) copy-start(f32[960]{0:T(1024)} %mul.484) | copy-start | bytes 11524
  121.3 15.3 %copy-start.21 = (bf16[4,240,640]{2,1,0:T(8,128)(2,1)S(1)}, bf16[4,240,640]{2,1,0:T(8,128)(2,1)}, u32[]{:S(2)}) copy-start(bf16[4,240,640]{2,1,0:T(8,128)(2,1)} %bitcast_dynamic-update-slice_fusion.9) | copy-start | bytes 3686404
  132.9 4.9 %copy-start.19 = (bf16[4,240,640]{2,1,0:T(8,128)(2,1)S(1)}, bf16[4,240,640]{2,1,0:T(8,128)(2,1)}, u32[]{:S(2)}) copy-start(bf16[4,240,640]{2,1,0:T(8,128)(2,1)} %copy-done.18) | copy-start | bytes 3686404
  132.9 4.9 %copy-start.73 = (f32[128]{0:T(128)}, f32[128]{0:T(128)S(1)}, u32[]{:S(2)}) copy-start(f32[128]{0:T(128)S(1)} %add_rsqrt_fusion) | copy-start | bytes 1540
  136.6 12.6 %copy-start.3 = (bf16[256,960]{0,1:T(8,128)(2,1)}, bf16[256,960]{0,1:T(8,128)(2,1)S(1)}, u32[]{:S(2)}) copy-start(bf16[256,960]{0,1:T(8,128)(2,1)S(1)} %all_gather.10) | copy-start | bytes 1474564
  155.4 37.5 %reduce-scatter.10.cloned.1.call-start = ((), (), s32[]{:S(2)}) async-start(), calls=%async_computation.5 | async-start | bytes 786432
  156.8 26.5 %collective-permute-start.13 = (bf16[240,1280]{1,0:T(8,128)(2,1)}, bf16[240,1280]{1,0:T(8,128)(2,1)}, u32[]{:S(2)}, u32[]{:S(2)}) collective-permute-start(bf16[240,1280]{1,0:T(8,128)(2,1)} %get-tuple-element.200), channel_id=1, source_target_pairs={{0,16},{16,0},{8,24},{24,8},{1,17},{17,1},{9,25},{25,9},{2,18},{18... | collective-permute-start | bytes 1843208 | tf_op jit(solution)/shard_map/ppermute | solution.py:230
  159.4 5.1 %copy-start.16 = (bf16[4,240,640]{2,1,0:T(8,128)(2,1)}, bf16[4,240,640]{2,1,0:T(8,128)(2,1)S(1)}, u32[]{:S(2)}) copy-start(bf16[4,240,640]{2,1,0:T(8,128)(2,1)S(1)} %get-tuple-element.197) | copy-start | bytes 3686404
  160.3 19.3 %collective-permute-start.15 = (bf16[240,640]{1,0:T(8,128)(2,1)}, bf16[240,640]{1,0:T(8,128)(2,1)}, u32[]{:S(2)}, u32[]{:S(2)}) collective-permute-start(bf16[240,640]{1,0:T(8,128)(2,1)} %get-tuple-element.208), channel_id=1, source_target_pairs={{0,16},{16,0},{8,24},{24,8},{1,17},{17,1},{9,25},{25,9},{2,18},{18... | collective-permute-start | bytes 921608 | tf_op jit(solution)/shard_map/ppermute | solution.py:230
  165.6 15.8 %collective-permute-start.14 = (bf16[240,640]{1,0:T(8,128)(2,1)}, bf16[240,640]{1,0:T(8,128)(2,1)}, u32[]{:S(2)}, u32[]{:S(2)}) collective-permute-start(bf16[240,640]{1,0:T(8,128)(2,1)} %get-tuple-element.211), channel_id=1, source_target_pairs={{0,8},{8,0},{16,24},{24,16},{1,9},{9,1},{17,25},{25,17},{2,10},{10... | collective-permute-start | bytes 921608 | tf_op jit(solution)/shard_map/ppermute | solution.py:230
  169.5 18.6 %collective-permute-start.12 = (bf16[240,1280]{1,0:T(8,128)(2,1)}, bf16[240,1280]{1,0:T(8,128)(2,1)}, u32[]{:S(2)}, u32[]{:S(2)}) collective-permute-start(bf16[240,1280]{1,0:T(8,128)(2,1)} %get-tuple-element.203), channel_id=1, source_target_pairs={{0,8},{8,0},{16,24},{24,16},{1,9},{9,1},{17,25},{25,17},{2,10},{10... | collective-permute-start | bytes 1843208 | tf_op jit(solution)/shard_map/ppermute | solution.py:230
  170.9 84.7 %reduce-scatter.8.cloned.1.call-start = ((), (), s32[]{:S(2)}) async-start(), calls=%async_computation.4 | async-start | bytes 1474560 | tf_op jit(solution)/shard_map/reduce_scatter | solution.py:747
  185.4 8.7 %copy-start.8 = (f32[128,960]{0,1:T(8,128)S(1)}, f32[128,960]{0,1:T(8,128)}, u32[]{:S(2)}) copy-start(f32[128,960]{0,1:T(8,128)} %copy-done.7) | copy-start | bytes 1474564
  185.4 8.7 %copy-start.43 = (bf16[128,960]{0,1:T(8,128)(2,1)S(1)}, bf16[128,960]{0,1:T(8,128)(2,1)}, u32[]{:S(2)}) copy-start(bf16[128,960]{0,1:T(8,128)(2,1)} %param.19) | copy-start | bytes 737284
  185.4 8.7 %copy-start.69 = (f32[960]{0:T(1024)S(1)}, f32[960]{0:T(1024)}, u32[]{:S(2)}) copy-start(f32[960]{0:T(1024)} %mul.484) | copy-start | bytes 11524
  185.4 8.7 %copy-start.74 = (f32[128]{0:T(128)S(1)}, f32[128]{0:T(128)}, u32[]{:S(2)}) copy-start(f32[128]{0:T(128)} %copy-done.73) | copy-start | bytes 1540
  194.1 5.1 %copy-start.65 = (bf16[240,640]{1,0:T(8,128)(2,1)S(1)}, bf16[240,640]{1,0:T(8,128)(2,1)}, u32[]{:S(2)}) copy-start(bf16[240,640]{1,0:T(8,128)(2,1)} %get-tuple-element.69) | copy-start | bytes 921604
  194.1 6.7 %copy-start.64 = (bf16[240,640]{1,0:T(8,128)(2,1)S(1)}, bf16[240,640]{1,0:T(8,128)(2,1)}, u32[]{:S(2)}) copy-start(bf16[240,640]{1,0:T(8,128)(2,1)} %get-tuple-element.70) | copy-start | bytes 921604
  195.1 6.9 %copy-start.60 = (bf16[240,640]{1,0:T(8,128)(2,1)S(1)}, bf16[240,640]{1,0:T(8,128)(2,1)}, u32[]{:S(2)}) copy-start(bf16[240,640]{1,0:T(8,128)(2,1)} %fusion.28) | copy-start | bytes 921604
  195.1 7.4 %copy-start.1 = (bf16[1024,640]{1,0:T(8,128)(2,1)S(1)}, bf16[1024,640]{1,0:T(8,128)(2,1)}, u32[]{:S(2)}) copy-start(bf16[1024,640]{1,0:T(8,128)(2,1)} %all-gather.2.cloned.1.call-done.kv_ref) | copy-start | bytes 3932164
  197.9 23.5 %collective-permute-start.16 = (bf16[240,1280]{1,0:T(8,128)(2,1)S(1)}, bf16[240,1280]{1,0:T(8,128)(2,1)S(1)}, u32[]{:S(2)}, u32[]{:S(2)}) collective-permute-start(bf16[240,1280]{1,0:T(8,128)(2,1)S(1)} %copy-done.49), channel_id=1, source_target_pairs={{0,8},{8,0},{16,24},{24,16},{1,9},{9,1},{17,25},{25,17},{2,10},{10... | collective-permute-start | bytes 1843208 | tf_op jit(solution)/shard_map/ppermute | solution.py:230
  198.4 23.0 %collective-permute-start.17 = (bf16[240,1280]{1,0:T(8,128)(2,1)S(1)}, bf16[240,1280]{1,0:T(8,128)(2,1)S(1)}, u32[]{:S(2)}, u32[]{:S(2)}) collective-permute-start(bf16[240,1280]{1,0:T(8,128)(2,1)S(1)} %copy-done.48), channel_id=1, source_target_pairs={{0,16},{16,0},{8,24},{24,8},{1,17},{17,1},{9,25},{25,9},{2,18},{18... | collective-permute-start | bytes 1843208 | tf_op jit(solution)/shard_map/ppermute | solution.py:230
  199.2 22.1 %collective-permute-start.18 = (bf16[240,640]{1,0:T(8,128)(2,1)S(1)}, bf16[240,640]{1,0:T(8,128)(2,1)S(1)}, u32[]{:S(2)}, u32[]{:S(2)}) collective-permute-start(bf16[240,640]{1,0:T(8,128)(2,1)S(1)} %copy-done.65), channel_id=1, source_target_pairs={{0,8},{8,0},{16,24},{24,16},{1,9},{9,1},{17,25},{25,17},{2,10},{10... | collective-permute-start | bytes 921608 | tf_op jit(solution)/shard_map/ppermute | solution.py:230
  200.8 20.5 %collective-permute-start.19 = (bf16[240,640]{1,0:T(8,128)(2,1)S(1)}, bf16[240,640]{1,0:T(8,128)(2,1)S(1)}, u32[]{:S(2)}, u32[]{:S(2)}) collective-permute-start(bf16[240,640]{1,0:T(8,128)(2,1)S(1)} %copy-done.64), channel_id=1, source_target_pairs={{0,16},{16,0},{8,24},{24,8},{1,17},{17,1},{9,25},{25,9},{2,18},{18... | collective-permute-start | bytes 921608 | tf_op jit(solution)/shard_map/ppermute | solution.py:230
  202.0 25.7 %collective-permute-start.23 = (bf16[240,640]{1,0:T(8,128)(2,1)S(1)}, bf16[240,640]{1,0:T(8,128)(2,1)}, u32[]{:S(2)}, u32[]{:S(2)}) collective-permute-start(bf16[240,640]{1,0:T(8,128)(2,1)S(1)} %copy-done.60), channel_id=1, source_target_pairs={{0,8},{8,0},{16,24},{24,16},{1,9},{9,1},{17,25},{25,17},{2,10},{10... | collective-permute-start | bytes 921608 | tf_op jit(solution)/shard_map/ppermute | solution.py:230
  222.5 4.8 %copy-start.56 = (f32[128,32]{0,1:T(8,128)S(1)}, f32[128,32]{0,1:T(8,128)}, u32[]{:S(2)}) copy-start(f32[128,32]{0,1:T(8,128)} %copy-done.55) | copy-start | bytes 49156
  222.6 4.8 %copy-start.58 = (f32[128,32]{0,1:T(8,128)S(1)}, f32[128,32]{0,1:T(8,128)}, u32[]{:S(2)}) copy-start(f32[128,32]{0,1:T(8,128)} %copy-done.57) | copy-start | bytes 49156
  222.6 5.2 %copy-start.38 = (bf16[240,640]{1,0:T(8,128)(2,1)S(1)}, bf16[240,640]{1,0:T(8,128)(2,1)}, u32[]{:S(2)}) copy-start(bf16[240,640]{1,0:T(8,128)(2,1)} %get-tuple-element.82) | copy-start | bytes 921604
  224.6 10.5 %copy-start.39 = (bf16[240,640]{1,0:T(8,128)(2,1)S(1)}, bf16[240,640]{1,0:T(8,128)(2,1)}, u32[]{:S(2)}) copy-start(bf16[240,640]{1,0:T(8,128)(2,1)} %get-tuple-element.79) | copy-start | bytes 921604
  224.6 10.5 %copy-start.62 = (bf16[240,640]{1,0:T(8,128)(2,1)S(1)}, bf16[240,640]{1,0:T(8,128)(2,1)}, u32[]{:S(2)}) copy-start(bf16[240,640]{1,0:T(8,128)(2,1)} %copy-done.61) | copy-start | bytes 921604
  224.7 10.4 %collective-permute-start.22 = (bf16[240,640]{1,0:T(8,128)(2,1)S(1)}, bf16[240,640]{1,0:T(8,128)(2,1)}, u32[]{:S(2)}, u32[]{:S(2)}) collective-permute-start(bf16[240,640]{1,0:T(8,128)(2,1)S(1)} %copy-done.59), channel_id=1, source_target_pairs={{0,16},{16,0},{8,24},{24,8},{1,17},{17,1},{9,25},{25,9},{2,18},{18... | collective-permute-start | bytes 921608 | tf_op jit(solution)/shard_map/ppermute | solution.py:230
  225.6 17.6 %collective-permute-start.20 = (bf16[240,1280]{1,0:T(8,128)(2,1)}, bf16[240,1280]{1,0:T(8,128)(2,1)}, u32[]{:S(2)}, u32[]{:S(2)}) collective-permute-start(bf16[240,1280]{1,0:T(8,128)(2,1)} %fusion.15), channel_id=1, source_target_pairs={{0,16},{16,0},{8,24},{24,8},{1,17},{17,1},{9,25},{25,9},{2,18},{18... | collective-permute-start | bytes 1843208 | tf_op jit(solution)/shard_map/ppermute | solution.py:230
  226.8 17.7 %collective-permute-start.21 = (bf16[240,1280]{1,0:T(8,128)(2,1)}, bf16[240,1280]{1,0:T(8,128)(2,1)}, u32[]{:S(2)}, u32[]{:S(2)}) collective-permute-start(bf16[240,1280]{1,0:T(8,128)(2,1)} %fusion.14), channel_id=1, source_target_pairs={{0,8},{8,0},{16,24},{24,16},{1,9},{9,1},{17,25},{25,17},{2,10},{10... | collective-permute-start | bytes 1843208 | tf_op jit(solution)/shard_map/ppermute | solution.py:230
  227.7 15.4 %copy-start.32 = (bf16[240,1280]{1,0:T(8,128)(2,1)S(1)}, bf16[240,1280]{1,0:T(8,128)(2,1)}, u32[]{:S(2)}) copy-start(bf16[240,1280]{1,0:T(8,128)(2,1)} %get-tuple-element.73) | copy-start | bytes 1843204
  227.7 15.4 %copy-start.53 = (bf16[240,1280]{1,0:T(8,128)(2,1)S(1)}, bf16[240,1280]{1,0:T(8,128)(2,1)}, u32[]{:S(2)}) copy-start(bf16[240,1280]{1,0:T(8,128)(2,1)} %copy-done.52) | copy-start | bytes 1843204
  236.1 8.3 %copy-start.31 = (bf16[240,1280]{1,0:T(8,128)(2,1)S(1)}, bf16[240,1280]{1,0:T(8,128)(2,1)}, u32[]{:S(2)}) copy-start(bf16[240,1280]{1,0:T(8,128)(2,1)} %get-tuple-element.76) | copy-start | bytes 1843204
  236.2 8.3 %copy-start.51 = (bf16[240,1280]{1,0:T(8,128)(2,1)S(1)}, bf16[240,1280]{1,0:T(8,128)(2,1)}, u32[]{:S(2)}) copy-start(bf16[240,1280]{1,0:T(8,128)(2,1)} %copy-done.50) | copy-start | bytes 1843204
  245.8 11.2 %copy-start.67 = (f32[960]{0:T(1024)S(1)}, f32[960]{0:T(1024)}, u32[]{:S(2)}) copy-start(f32[960]{0:T(1024)} %copy-done.66) | copy-start | bytes 11524
  245.8 11.2 %copy-start.72 = (f32[128]{0:T(128)S(1)}, f32[128]{0:T(128)}, u32[]{:S(2)}) copy-start(f32[128]{0:T(128)} %copy-done.71) | copy-start | bytes 1540
  270.4 74.1 %copy-start.25 = (f32[240,2,1280]{2,1,0:T(2,128)S(1)}, f32[240,2,1280]{2,1,0:T(2,128)}, u32[]{:S(2)}) copy-start(f32[240,2,1280]{2,1,0:T(2,128)} %param.28) | copy-start | bytes 7372804
  270.4 74.1 %copy-start.26 = (f32[240,2,1280]{2,1,0:T(2,128)S(1)}, f32[240,2,1280]{2,1,0:T(2,128)}, u32[]{:S(2)}) copy-start(f32[240,2,1280]{2,1,0:T(2,128)} %param.29) | copy-start | bytes 7372804
  354.7 5.0 %copy-start.40 = (f32[240,960]{1,0:T(8,128)S(1)}, f32[240,960]{1,0:T(8,128)}, u32[]{:S(2)}) copy-start(f32[240,960]{1,0:T(8,128)} %param.25) | copy-start | bytes 2764804
  354.7 5.0 %copy-start.41 = (f32[240,960]{1,0:T(8,128)S(1)}, f32[240,960]{1,0:T(8,128)}, u32[]{:S(2)}) copy-start(f32[240,960]{1,0:T(8,128)} %param.26) | copy-start | bytes 2764804
  (43 other events, 104.6 us)
Sparse Core Ops, SparseCore 0:
  71.0 23.6 all-gather.1
  155.6 8.1 reduce-scatter.11
  171.1 7.2 reduce-scatter.9
  222.7 32.9 reduce-scatter.7
